TPU v7x, 32 devices: a whole 2x2x4 slice. The times are simulated.
32 devices in a mesh: case: 8 (over z, x), bx: 2 (over y), by: 2 (over core).
Axes of the slice: x: 2, y: 2, z: 4, core: 2. Of those that a mesh axis runs over, the one named last changes fastest.
Arguments:
- displacements: bfloat16 [16, 3, 16, 16, 256], P('case', None, 'bx', 'by'), may hold values from -6 to 6
- material_ids: int32 [16, 16, 256], P('bx', 'by'), may hold values from 0 to 7
- lame: float32 [2, 8], replicated, may hold values from 0.5 to 2
- slab_bounds: int32 [2, 16], P(None, 'bx'), may hold values from 0 to 256, as said below
- load_history: bfloat16 [1024, 16], replicated, may hold values from -1.5 to 1.5
Outputs:
- vm_peak: float32 [16, 16, 256], P('bx', 'by', 'case')
- hyd_range: float32 [16, 16, 256], P('bx', 'by', 'case')
Inputs may be any that keep to these rules, and one draw needn't show every extreme that they name: `slab_bounds`: row 0 lies below 64 and row 1 above 192 for every x.
All inputs are finite; a program needn't handle non-finite values.
Results may differ from a plain program's by a relative error of at most 0.00097.
Values may be sent and summed in bfloat16 or wider, within the bound.
No kernel may reach another device: no remote copies, remote signals or barrier semaphores. Data moves between devices by JAX's collectives and lax.ppermute only.
A program may use at most 64 MiB of HBM per device.

v0:
```python
import jax
import jax.numpy as jnp
from jax import lax
from jax.sharding import PartitionSpec as P


def extended_2(cells, sides, width):
    for axis, dim in sides:
        count = lax.axis_size(axis)
        ends = count - 1
        head = lax.slice_in_dim(cells, 0, width, axis=dim)
        tail = lax.slice_in_dim(cells, cells.shape[dim] - width, cells.shape[dim], axis=dim)
        cells = jnp.concatenate(
            [
                lax.ppermute(tail, axis, [(i, (i + 1) % count) for i in range(ends)]),
                cells,
                lax.ppermute(head, axis, [((i + 1) % count, i) for i in range(ends)]),
            ],
            axis=dim,
        )
    return cells


def derivative(extended, comp, along):
    field = extended[..., comp, :, :, :]
    if along == 0:
        return 0.5 * (field[..., 2:, 1:-1, 1:-1] - field[..., :-2, 1:-1, 1:-1])
    if along == 1:
        return 0.5 * (field[..., 1:-1, 2:, 1:-1] - field[..., 1:-1, :-2, 1:-1])
    return 0.5 * (field[..., 1:-1, 1:-1, 2:] - field[..., 1:-1, 1:-1, :-2])


def combine_stress(grads, shear_mod, lame_first, weight):
    trace = grads[0][0] + grads[1][1] + grads[2][2]
    normal_x = (lame_first * trace + 2.0 * shear_mod * grads[0][0]) * weight
    normal_y = (lame_first * trace + 2.0 * shear_mod * grads[1][1]) * weight
    normal_z = (lame_first * trace + 2.0 * shear_mod * grads[2][2]) * weight
    shear_xy = shear_mod * (grads[0][1] + grads[1][0]) * weight
    shear_yz = shear_mod * (grads[1][2] + grads[2][1]) * weight
    shear_zx = shear_mod * (grads[2][0] + grads[0][2]) * weight
    return jnp.stack([normal_x, normal_y, normal_z, shear_xy, shear_yz, shear_zx], axis=-4)


def stress_field(extended, shear_mod, lame_first, weight):
    extended = extended.astype(jnp.float32)
    grads = [[derivative(extended, comp, along) for along in range(3)] for comp in range(3)]
    return combine_stress(grads, shear_mod, lame_first, weight)


def material_moduli(material_ids, lame):
    shear_mod = jnp.zeros(material_ids.shape, jnp.float32)
    lame_first = jnp.zeros(material_ids.shape, jnp.float32)
    for material in range(lame.shape[1]):
        picked = material_ids == material
        shear_mod = jnp.where(picked, lame[0, material], shear_mod)
        lame_first = jnp.where(picked, lame[1, material], lame_first)
    return (shear_mod, lame_first)


def histories(load_history, blocks):
    cases, comps, rows, cols, single, slab = blocks.shape
    flat = blocks.reshape(cases, comps * rows * cols * single * slab)
    total = load_history.shape[0]
    step_len = min(128, total)
    top_mises = None
    for begin in range(0, total, step_len):
        factors = load_history[begin : begin + step_len]
        history = jnp.dot(factors, flat, preferred_element_type=jnp.float32).reshape(
            step_len, comps, -1
        )
        diff_one = history[:, 0] - history[:, 1]
        diff_two = history[:, 1] - history[:, 2]
        diff_three = history[:, 2] - history[:, 0]
        mises2 = 0.5 * (diff_one * diff_one + diff_two * diff_two + diff_three * diff_three)
        mises2 = mises2 + 3.0 * (
            history[:, 3] * history[:, 3]
            + history[:, 4] * history[:, 4]
            + history[:, 5] * history[:, 5]
        )
        hydro = (history[:, 0] + history[:, 1] + history[:, 2]) / 3.0
        block_mises = jnp.max(mises2, axis=0)
        block_high = jnp.max(hydro, axis=0)
        block_low = jnp.min(hydro, axis=0)
        if top_mises is None:
            top_mises, high, low = (block_mises, block_high, block_low)
        else:
            top_mises = jnp.maximum(top_mises, block_mises)
            high = jnp.maximum(high, block_high)
            low = jnp.minimum(low, block_low)
    peak = jnp.sqrt(top_mises).reshape(rows, cols, slab)
    spread = (high - low).reshape(rows, cols, slab)
    return (peak, spread)


def shards(displacements, material_ids, lame, slab_bounds, load_history):
    cases_here = displacements.shape[0]
    rows = displacements.shape[2]
    cols = displacements.shape[3]
    depth = displacements.shape[4]
    groups = lax.axis_size("case")
    slab = depth // groups
    shear_mod, lame_first = material_moduli(material_ids, lame)
    levels = jnp.arange(depth, dtype=jnp.int32)
    inside = (slab_bounds[0][:, None] <= levels[None, :]) & (
        levels[None, :] < slab_bounds[1][:, None]
    )
    weight = inside.astype(jnp.float32)[:, None, :]
    bordered = extended_2(displacements, (("bx", 2), ("by", 3)), 1)
    extended = jnp.pad(bordered, ((0, 0), (0, 0), (0, 0), (0, 0), (1, 1)))
    stress = stress_field(extended, shear_mod, lame_first, weight).astype(jnp.bfloat16)
    blocks = stress.reshape(cases_here, 6, rows, cols, groups, slab)
    peak, spread = histories(
        load_history, lax.all_to_all(blocks, "case", split_axis=4, concat_axis=0, tiled=True)
    )
    return (peak, spread)


def solution(mesh):
    in_specs = (P("case", None, "bx", "by", None), P("bx", "by", None), P(), P(None, "bx"), P())
    out_specs = (P("bx", "by", "case"), P("bx", "by", "case"))
    return jax.shard_map(shards, mesh=mesh, in_specs=in_specs, out_specs=out_specs, check_vma=False)
```

profile of v0, /device:TPU:0, one launch (start us, length us, event | category | flops | bytes accessed | tf_op | source)
XLA Modules:
  0.0 85.1 jit_solution(9395708904457059000)
XLA Ops:
  0.6 0.8 fusion.102
  1.4 1.3 %collective-permute-start.1 = (bf16[2,3,1,8,256]{4,3,2,1,0:T(8,128)(2,1)S(1)}, bf16[2,3,1,8,256]{4,3,2,1,0:T(8,128)(2,1)S(1)}, u32[]{:S(2)}, u32[]{:S(2)}) collective-permute-start(bf16[2,3,1,8,256]{4,3,2,1,0:T(8,128)(2,1)S(1)} %get-tuple-element.48), channel_id=1, source_target_pairs={{2,0},{3,1},{6,4},{7,5},{10,8},{11,9},{14,12},{15,13},{18,16},{19,... | collective-permute-start | bytes 73736 | tf_op jit(solution)/shard_map/ppermute | solution.py:17
  2.7 4.9 %collective-permute-start = (bf16[2,3,1,8,256]{4,3,2,1,0:T(8,128)(2,1)S(1)}, bf16[2,3,1,8,256]{4,3,2,1,0:T(8,128)(2,1)S(1)}, u32[]{:S(2)}, u32[]{:S(2)}) collective-permute-start(bf16[2,3,1,8,256]{4,3,2,1,0:T(8,128)(2,1)S(1)} %get-tuple-element.49), channel_id=1, source_target_pairs={{0,2},{1,3},{4,6},{5,7},{8,10},{9,11},{12,14},{13,15},{16,18},{17,... | collective-permute-start | bytes 73736 | tf_op jit(solution)/shard_map/ppermute | solution.py:15
  7.6 2.0 %fusion.103 = (f32[1,1]{1,0:T(1,128)}, f32[1,1]{1,0:T(1,128)}, f32[1,1]{1,0:T(1,128)}, f32[1,1]{1,0:T(1,128)}, f32[1,1]{1,0:T(1,128)}, /*index=5*/f32[1,1]{1,0:T...) fusion(f32[2,8]{1,0:T(2,128)} %param.7), kind=kLoop, calls=%fused_computation.203 | loop fusion | bytes 128 | tf_op jit(solution)/shard_map/slice | solution.py:56
  9.5 5.9 %broadcast_multiply_fusion = (f32[8,8,256]{2,1,0:T(8,128)S(1)}, f32[8,8,256]{2,1,0:T(8,128)S(1)}, pred[8,8,256]{2,1,0:T(8,128)(4,1)S(1)}, pred[8,8,256]{2,1,0:T(...) fusion(f32[]{:T(128)} %bitcast.18, f32[]{:T(128)} %bitcast.17, ...), kind=kLoop, calls=%fused_computation.149 | loop fusion | flops 278528 | bytes 327712 | tf_op jit(solution)/shard_map/mul | solution.py:38
  15.5 5.1 %select_multiply_fusion = f32[8,8,256]{2,1,0:T(8,128)S(1)} fusion(pred[8,8,256]{2,1,0:T(8,128)(4,1)S(1)} %get-tuple-element.35, pred[8,8,256]{2,1,0:T(8,128)(4,1)S(1)} %get-tuple-element.34, pred[8,8,256]{2,1,0:T(8,128)(4,1)S(1)} %get-tuple-element.33, pred[8,8,256]{2,1,0:T(8,128)(4,1)S(1)} %get-tuple-element.32, ...), kind=kLoop, calls=%fused_computation.148 | loop fusion | flops 147456 | bytes 196640 | tf_op jit(solution)/shard_map/mul | solution.py:35
  20.5 0.8 slice_bitcast_fusion.28
  21.3 0.0 collective-permute-done
  21.3 0.9 %constant_dynamic-update-slice_fusion.1 = bf16[2,3,10,8,256]{4,3,2,1,0:T(8,128)(2,1)S(1)} fusion(bf16[2,3,10,8,256]{4,3,2,1,0:T(8,128)(2,1)S(1)} %constant_dynamic-update-slice_fusion.2, bf16[2,3,8,8,256]{4,3,2,1,0:T(8,128)(2,1)} %param.5), kind=kLoop, calls=%fused_computation.159 | loop fusion | bytes 393216
  22.3 0.0 collective-permute-done.1
  22.3 0.1 fusion.101
  22.4 1.5 %collective-permute-start.2 = (bf16[2,3,10,1,256]{4,3,2,1,0:T(2,128)(2,1)S(1)}, bf16[2,3,10,1,256]{4,3,2,1,0:T(2,128)(2,1)S(1)}, u32[]{:S(2)}, u32[]{:S(2)}) collective-permute-start(bf16[2,3,10,1,256]{4,3,2,1,0:T(2,128)(2,1)S(1)} %get-tuple-element.46), channel_id=1, source_target_pairs={{0,1},{2,3},{4,5},{6,7},{8,9},{10,11},{12,13},{14,15},{16,17},{18,... | collective-permute-start | bytes 92168 | tf_op jit(solution)/shard_map/ppermute | solution.py:15
  23.9 1.3 %collective-permute-start.3 = (bf16[2,3,10,1,256]{4,3,2,1,0:T(2,128)(2,1)S(1)}, bf16[2,3,10,1,256]{4,3,2,1,0:T(2,128)(2,1)S(1)}, u32[]{:S(2)}, u32[]{:S(2)}) collective-permute-start(bf16[2,3,10,1,256]{4,3,2,1,0:T(2,128)(2,1)S(1)} %get-tuple-element.47), channel_id=1, source_target_pairs={{1,0},{3,2},{5,4},{7,6},{9,8},{11,10},{13,12},{15,14},{17,16},{19,... | collective-permute-start | bytes 92168 | tf_op jit(solution)/shard_map/ppermute | solution.py:17
  25.2 0.1 fusion.68
  25.2 0.0 collective-permute-done.2
  25.2 1.8 %collective-permute-done.3 = bf16[2,3,10,1,256]{4,3,2,1,0:T(2,128)(2,1)S(1)} collective-permute-done((bf16[2,3,10,1,256]{4,3,2,1,0:T(2,128)(2,1)S(1)}, bf16[2,3,10,1,256]{4,3,2,1,0:T(2,128)(2,1)S(1)}, u32[]{:S(2)}, u32[]{:S(2)}) %collective-permute-start.3) | collective-permute-done | bytes 30752 | tf_op jit(solution)/shard_map/ppermute | solution.py:17
  27.0 0.7 fusion.54
  27.7 0.1 slice_bitcast_fusion.26
  27.9 0.5 multiply_convert_fusion
  28.3 0.4 fusion.66
  28.7 0.2 stack.24
  28.9 0.2 stack.23
  29.0 0.2 stack.21
  29.2 0.2 stack.22
  29.4 0.2 stack.26
  29.5 0.2 stack.25
  29.8 0.1 copy_dynamic-update-slice_fusion.4
  29.8 0.1 copy_dynamic-update-slice_fusion.3
  29.9 0.1 copy_dynamic-update-slice_fusion.2
  30.0 0.1 copy_dynamic-update-slice_fusion.1
  30.1 0.1 copy_dynamic-update-slice_fusion
  30.2 1.4 %reshape.210 = bf16[8,2,12288]{2,1,0:T(2,128)(2,1)S(1)} reshape(bf16[8,2,6,8,8,32]{5,4,3,2,1,0:T(8,128)(2,1)S(1)} %bitcast.383) | data formatting | bytes 786432
  31.6 18.9 %all_to_all.15 = bf16[8,2,12288]{2,1,0:T(2,128)(2,1)S(1)} all-to-all(bf16[8,2,12288]{2,1,0:T(2,128)(2,1)S(1)} %reshape.210), channel_id=1, replica_groups=mesh['case'=8,'bx'=2,'by'=2] {'case'}, dimensions={0} | all-to-all | bytes 786432 | tf_op jit(solution)/shard_map/all_to_all | solution.py:113
  50.5 0.8 reshape.211
  51.3 0.2 bitcast_bitcast_fusion
  51.5 0.0 copy-start
  51.5 1.6 %reshape.190 = bf16[16,12288]{1,0:T(8,128)(2,1)S(1)} reshape(bf16[8,2,6,8,8,1,32]{6,4,3,2,1,0,5:T(8,128)(2,1)S(1)} %bitcast_bitcast_fusion) | data formatting | bytes 786432 | tf_op jit(solution)/shard_map/reshape | solution.py:62
  53.1 0.0 copy-done
  53.1 3.7 %fusion.69 = f32[12288,128]{1,0:T(8,128)} fusion(bf16[16,12288]{1,0:T(8,128)(2,1)S(1)} %reshape.190, bf16[1024,16]{0,1:T(8,128)(2,1)S(1)} %copy-done), kind=kOutput, calls=%fused_computation.167 | convolution fusion | flops 50331648 | bytes 6688768 | tf_op jit(solution)/shard_map/dot_general | solution.py:68
  56.8 3.7 %fusion.71 = f32[12288,128]{1,0:T(8,128)} fusion(bf16[16,12288]{1,0:T(8,128)(2,1)S(1)} %reshape.190, bf16[1024,16]{0,1:T(8,128)(2,1)S(1)} %copy-done), kind=kOutput, calls=%fused_computation.169 | convolution fusion | flops 50331648 | bytes 6688768 | tf_op jit(solution)/shard_map/dot_general | solution.py:68
  60.5 1.0 %fusion.73 = f32[12288,128]{1,0:T(8,128)S(1)} fusion(bf16[16,12288]{1,0:T(8,128)(2,1)S(1)} %reshape.190, bf16[1024,16]{0,1:T(8,128)(2,1)S(1)} %copy-done), kind=kOutput, calls=%fused_computation.171 | convolution fusion | flops 50331648 | bytes 6688768 | tf_op jit(solution)/shard_map/dot_general | solution.py:68
  61.5 3.6 %fusion.75 = f32[12288,128]{1,0:T(8,128)} fusion(bf16[16,12288]{1,0:T(8,128)(2,1)S(1)} %reshape.190, bf16[1024,16]{0,1:T(8,128)(2,1)S(1)} %copy-done), kind=kOutput, calls=%fused_computation.173 | convolution fusion | flops 50331648 | bytes 6688768 | tf_op jit(solution)/shard_map/dot_general | solution.py:68
  65.2 1.0 %fusion.77 = f32[12288,128]{1,0:T(8,128)S(1)} fusion(bf16[16,12288]{1,0:T(8,128)(2,1)S(1)} %reshape.190, bf16[1024,16]{0,1:T(8,128)(2,1)S(1)} %copy-done), kind=kOutput, calls=%fused_computation.175 | convolution fusion | flops 50331648 | bytes 6688768 | tf_op jit(solution)/shard_map/dot_general | solution.py:68
  66.2 1.0 %fusion.79 = f32[12288,128]{1,0:T(8,128)S(1)} fusion(bf16[16,12288]{1,0:T(8,128)(2,1)S(1)} %reshape.190, bf16[1024,16]{0,1:T(8,128)(2,1)S(1)} %copy-done), kind=kOutput, calls=%fused_computation.177 | convolution fusion | flops 50331648 | bytes 6688768 | tf_op jit(solution)/shard_map/dot_general | solution.py:68
  67.2 1.0 %fusion.81 = f32[12288,128]{1,0:T(8,128)S(1)} fusion(bf16[16,12288]{1,0:T(8,128)(2,1)S(1)} %reshape.190, bf16[1024,16]{0,1:T(8,128)(2,1)S(1)} %copy-done), kind=kOutput, calls=%fused_computation.179 | convolution fusion | flops 50331648 | bytes 6688768 | tf_op jit(solution)/shard_map/dot_general | solution.py:68
  68.3 1.0 %fusion.83 = f32[12288,128]{1,0:T(8,128)S(1)} fusion(bf16[16,12288]{1,0:T(8,128)(2,1)S(1)} %reshape.190, bf16[1024,16]{0,1:T(8,128)(2,1)S(1)} %copy-done), kind=kOutput, calls=%fused_computation.181 | convolution fusion | flops 50331648 | bytes 6688768 | tf_op jit(solution)/shard_map/dot_general | solution.py:68
  69.3 0.0 slice-start
  69.3 0.0 slice-start.1
  69.3 6.0 %fusion.98 = (f32[2048]{0:T(1024)S(1)}, f32[2048]{0:T(1024)S(1)}, f32[2048]{0:T(1024)S(1)}, f32[2048]{0:T(1024)S(1)}, f32[2048]{0:T(1024)S(1)}, /*index=5*/f32[2048]{0:T(1024)S(1)}) fusion(f32[128,6,2048]{0,2,1:T(8,128)} %bitcast.382, f32[128,6,2048]{0,2,1:T(8,128)} %bitcast.381), kind=kLoop, calls=%fused_computation.198 | loop fusion | flops 11522048 | bytes 12632064 | tf_op jit(solution)/shard_map/reduce_max | solution.py:82
  75.4 0.0 slice-done
  75.4 0.5 slice-done.1
  75.8 2.6 %fusion.94 = (f32[2048]{0:T(1024)S(1)}, f32[2048]{0:T(1024)S(1)}, f32[2048]{0:T(1024)S(1)}, f32[2048]{0:T(1024)S(1)}, f32[2048]{0:T(1024)S(1)}, /*index=5*/f32[2048]{0:T(1024)S(1)}) fusion(f32[128,6,2048]{0,2,1:T(8,128)S(1)} %bitcast.380, f32[128,6,2048]{0,2,1:T(8,128)S(1)} %bitcast.377), kind=kLoop, calls=%fused_computation.194 | loop fusion | flops 11522048 | bytes 12632064 | tf_op jit(solution)/shard_map/reduce_max | solution.py:82
  78.5 2.6 %fusion.90 = (f32[2048]{0:T(1024)S(1)}, f32[2048]{0:T(1024)S(1)}, f32[2048]{0:T(1024)S(1)}, f32[2048]{0:T(1024)S(1)}, f32[2048]{0:T(1024)S(1)}, /*index=5*/f32[2048]{0:T(1024)S(1)}) fusion(f32[128,6,2048]{0,2,1:T(8,128)S(1)} %bitcast.376, f32[128,6,2048]{0,2,1:T(8,128)S(1)} %bitcast.375), kind=kLoop, calls=%fused_computation.190 | loop fusion | flops 11522048 | bytes 12632064 | tf_op jit(solution)/shard_map/reduce_max | solution.py:82
  81.1 2.6 %fusion.86 = (f32[2048]{0:T(1024)S(1)}, f32[2048]{0:T(1024)S(1)}, f32[2048]{0:T(1024)S(1)}, f32[2048]{0:T(1024)S(1)}, f32[2048]{0:T(1024)S(1)}, /*index=5*/f32[2048]{0:T(1024)S(1)}) fusion(f32[128,6,2048]{0,2,1:T(8,128)S(1)} %bitcast.374, f32[128,6,2048]{0,2,1:T(8,128)S(1)} %bitcast.373), kind=kLoop, calls=%fused_computation.186 | loop fusion | flops 11522048 | bytes 12632064 | tf_op jit(solution)/shard_map/reduce_max | solution.py:82
  83.7 0.7 reshape.209
  84.4 0.7 reshape.208
  (6 shorter events, 0.1 us)
Async XLA Ops:
  1.4 20.9 %collective-permute-start.1 = (bf16[2,3,1,8,256]{4,3,2,1,0:T(8,128)(2,1)S(1)}, bf16[2,3,1,8,256]{4,3,2,1,0:T(8,128)(2,1)S(1)}, u32[]{:S(2)}, u32[]{:S(2)}) collective-permute-start(bf16[2,3,1,8,256]{4,3,2,1,0:T(8,128)(2,1)S(1)} %get-tuple-element.48), channel_id=1, source_target_pairs={{2,0},{3,1},{6,4},{7,5},{10,8},{11,9},{14,12},{15,13},{18,16},{19,... | collective-permute-start | bytes 73736 | tf_op jit(solution)/shard_map/ppermute | solution.py:17
  2.7 18.6 %collective-permute-start = (bf16[2,3,1,8,256]{4,3,2,1,0:T(8,128)(2,1)S(1)}, bf16[2,3,1,8,256]{4,3,2,1,0:T(8,128)(2,1)S(1)}, u32[]{:S(2)}, u32[]{:S(2)}) collective-permute-start(bf16[2,3,1,8,256]{4,3,2,1,0:T(8,128)(2,1)S(1)} %get-tuple-element.49), channel_id=1, source_target_pairs={{0,2},{1,3},{4,6},{5,7},{8,10},{9,11},{12,14},{13,15},{16,18},{17,... | collective-permute-start | bytes 73736 | tf_op jit(solution)/shard_map/ppermute | solution.py:15
  22.4 2.9 %collective-permute-start.2 = (bf16[2,3,10,1,256]{4,3,2,1,0:T(2,128)(2,1)S(1)}, bf16[2,3,10,1,256]{4,3,2,1,0:T(2,128)(2,1)S(1)}, u32[]{:S(2)}, u32[]{:S(2)}) collective-permute-start(bf16[2,3,10,1,256]{4,3,2,1,0:T(2,128)(2,1)S(1)} %get-tuple-element.46), channel_id=1, source_target_pairs={{0,1},{2,3},{4,5},{6,7},{8,9},{10,11},{12,13},{14,15},{16,17},{18,... | collective-permute-start | bytes 92168 | tf_op jit(solution)/shard_map/ppermute | solution.py:15
  23.9 3.1 %collective-permute-start.3 = (bf16[2,3,10,1,256]{4,3,2,1,0:T(2,128)(2,1)S(1)}, bf16[2,3,10,1,256]{4,3,2,1,0:T(2,128)(2,1)S(1)}, u32[]{:S(2)}, u32[]{:S(2)}) collective-permute-start(bf16[2,3,10,1,256]{4,3,2,1,0:T(2,128)(2,1)S(1)} %get-tuple-element.47), channel_id=1, source_target_pairs={{1,0},{3,2},{5,4},{7,6},{9,8},{11,10},{13,12},{15,14},{17,16},{19,... | collective-permute-start | bytes 92168 | tf_op jit(solution)/shard_map/ppermute | solution.py:17
  51.5 1.6 %copy-start = (bf16[1024,16]{0,1:T(8,128)(2,1)S(1)}, bf16[1024,16]{0,1:T(8,128)(2,1)}, u32[]{:S(2)}) copy-start(bf16[1024,16]{0,1:T(8,128)(2,1)} %param.9) | copy-start | bytes 98308
  69.3 6.1 %slice-start = ((s8[6291456]{0:T(1024)(128)(4,1)}), s8[4194304]{0:T(1024)(128)(4,1)S(1)}, s32[]{:S(2)}) async-start(s8[6291456]{0:T(1024)(128)(4,1)} %bitcast.378), calls=%async_computation.1 | async-start | bytes 8388608
  69.3 6.5 %slice-start.1 = ((s8[6291456]{0:T(1024)(128)(4,1)}), s8[2097152]{0:T(1024)(128)(4,1)S(1)}, s32[]{:S(2)}) async-start(s8[6291456]{0:T(1024)(128)(4,1)} %bitcast.378), calls=%async_computation.2 | async-start | bytes 4194304
where the time goes:
time: 85.7 us; the launch traced here: 85.1 us
  other arithmetic  26.5 us (31%)
  blocking collectives  18.9 us (22%)
  matrix products  16.2 us (19%)
  local copies, waits for them, and re-layouts  11.9 us (14%)
  starting transfers between devices  8.92 us (10%)
  waiting for transfers between devices  1.77 us (2%)
  between operations  0.95 us (1%)
    all_to_all x1, blocking collectives, shards(): lax.all_to_all(blocks, 'case', split_axis=4, concat_axis=0, tiled=True)  18.9 us
    dot_general x8, matrix products, histories(): jnp.dot(factors, flat, preferred_element_type=jnp.float32)  16.2 us
    reduce_max x4, other arithmetic, histories(): block_high = jnp.max(hydro, axis=0)  13.9 us
    ppermute x2, starting transfers between devices, extended_2(): lax.ppermute(tail, axis, [(i, (i + 1) % count) for i in range(ends)])  6.34 us
    mul x1, other arithmetic, combine_stress(): shear_xy = shear_mod * (grads[0][1] + grads[1][0]) * weight  5.95 us
    mul x1, other arithmetic, combine_stress(): normal_x = (lame_first * trace + 2.0 * shear_mod * grads[0][0]) * weight  5.06 us
    unnamed x15, local copies, waits for them, and re-layouts  3.94 us
    ppermute x2, starting transfers between devices, extended_2(): lax.ppermute(head, axis, [((i + 1) % count, i) for i in range(ends)])  2.57 us
  transfers between devices with their start and end apart: 4, of which 1 were waited for; matrix products, arithmetic and copies ran while one was open for 17% of the time, Pallas kernels for 0%

commit v1 on v0

--- a/solution.py
+++ b/solution.py
@@ -1,6 +1,12 @@
+import functools
+import math
+
 import jax
 import jax.numpy as jnp
+import numpy as np
 from jax import lax
+from jax.experimental import pallas as pl
+from jax.experimental.pallas import tpu as pltpu
 from jax.sharding import PartitionSpec as P
 
 
@@ -115,7 +121,323 @@
     return (peak, spread)
 
 
+F32 = jnp.float32
+BF16 = jnp.bfloat16
+TILE = 128
+ROWS = 16
+SIDES = 2
+
+
+def pair_table(cases, groups):
+    per = cases // groups
+    place = np.array([(j % groups) * per + j // groups for j in range(cases)])
+    shifts = cases // 2 + 1
+    width = shifts * cases
+    total = -(-3 * width // 256) * 256
+    first = np.zeros((cases, total), np.float32)
+    second = np.zeros((cases, total), np.float32)
+    plain = np.zeros((cases, TILE), np.float32)
+    for copy in range(3):
+        for s in range(shifts):
+            for j in range(cases):
+                col = copy * width + s * cases + j
+                first[place[j], col] = 1.0
+                second[place[(j + s) % cases], col] = 1.0 if s in (0, cases // 2) else 2.0
+        for j in range(cases):
+            plain[place[j], copy * cases + j] = 1.0
+    return shifts, width, total, first, second, plain
+
+
+def prepare_kernel(width, slab, loads, first, second, plain, ids, lame, bounds, pairs, linear, moduli):
+    over = (((0,), (0,)), ((), ()))
+    table = loads[...]
+    prod = lax.dot_general(table, first[...], over, preferred_element_type=F32)
+    prod = prod * lax.dot_general(table, second[...], over, preferred_element_type=F32)
+    high = prod.astype(BF16)
+    low = (prod - high.astype(F32)).astype(BF16)
+    col = lax.broadcasted_iota(jnp.int32, prod.shape, 1)
+    pairs[...] = jnp.where(col < 2 * width, high.astype(F32), low.astype(F32)).astype(BF16)
+    linear[...] = lax.dot_general(table, plain[...], over, preferred_element_type=F32).astype(BF16)
+    group = lax.axis_index("case")
+    rows, depth = ids.shape
+    cols = ROWS // 2
+    depth_first = pltpu.roll(ids[...], (depth - group * slab) % depth, 1)[:, :TILE]
+    lane = lax.broadcasted_iota(jnp.int32, (ROWS, TILE), 1)
+    row = lax.broadcasted_iota(jnp.int32, (ROWS, TILE), 0)
+    level = group * slab + lane % slab
+    tile = jnp.zeros((ROWS, TILE), jnp.int32)
+    lower = jnp.zeros((ROWS, TILE), jnp.int32)
+    upper = jnp.zeros((ROWS, TILE), jnp.int32)
+    for i in range(TILE // slab):
+        here = lane // slab == i
+        piece = depth_first[i * ROWS : (i + 1) * ROWS]
+        tile = jnp.where(here, piece if i == 0 else pltpu.roll(piece, i * slab, 1), tile)
+        for p in range(2):
+            spot = here & (row // cols == p)
+            lower = jnp.where(spot, bounds[0, 2 * i + p], lower)
+            upper = jnp.where(spot, bounds[1, 2 * i + p], upper)
+    weight = jnp.where((lower <= level) & (level < upper), 1.0, 0.0).astype(F32)
+    for part in range(2):
+        value = jnp.zeros((ROWS, TILE), F32)
+        for material in range(lame.shape[1]):
+            value = jnp.where(tile == material, lame[part, material], value)
+        moduli[part] = value * weight
+
+
+def pack_kernel(slab, field, face_x, face_y, out):
+    groups = out.shape[0]
+    depth = field.shape[1]
+    quarters = TILE // slab
+    channels = field.shape[0] // (quarters * ROWS)
+    parts = [
+        [field[(m * quarters + i) * ROWS : (m * quarters + i + 1) * ROWS, :].astype(F32) for i in range(quarters)]
+        for m in range(channels)
+    ]
+    lane = lax.broadcasted_iota(jnp.int32, (ROWS, depth), 1)
+    ends = []
+    for i in range(quarters):
+        mixed = jnp.zeros((ROWS, depth), F32)
+        for m in range(channels):
+            below = pltpu.roll(parts[m][i], 2 * m + 1, 1)
+            above = pltpu.roll(parts[m][i], (2 * m + 1 - slab) % depth, 1)
+            mixed = jnp.where((lane % slab == 2 * m) & (lane >= slab), below, mixed)
+            mixed = jnp.where((lane % slab == 2 * m + 1) & (lane < depth - slab), above, mixed)
+        ends.append(mixed)
+    half = ROWS // 2
+    faces = [
+        jnp.concatenate([face_x[m * half : (m + 1) * half, :].astype(F32), face_y[m * half : (m + 1) * half, :].astype(F32)], axis=0)
+        for m in range(channels)
+    ]
+    for g in range(groups):
+        cut = slice(g * slab, (g + 1) * slab)
+        short = slice(g * slab, g * slab + slab // 2)
+        for m in range(channels):
+            out[g, m * ROWS : (m + 1) * ROWS, :] = jnp.concatenate([parts[m][i][:, cut] for i in range(quarters)], axis=1).astype(BF16)
+        top = channels * ROWS
+        out[g, top : top + ROWS, :] = jnp.concatenate([faces[q][:, cut] for q in range(4)], axis=1).astype(BF16)
+        out[g, top + ROWS : top + 2 * ROWS, :] = jnp.concatenate(
+            [faces[4][:, cut], faces[5][:, cut]] + [ends[i][:, short] for i in range(quarters)], axis=1
+        ).astype(BF16)
+
+
+def stress_kernel(shifts, slab, got, pairs, linear, moduli, peak, spread, plain, tiles, rhs, sums, best, high, low):
+    groups, rows, _ = got.shape
+    quarters = TILE // slab
+    channels = rows // ROWS - 2
+    per = channels // 3
+    cases = per * groups
+    cols = ROWS // 2
+    width = shifts * cases
+    has_lower_x = lax.axis_index("bx") == 1
+    has_lower_y = lax.axis_index("by") == 1
+    for g in range(groups):
+        plain[g * rows : (g + 1) * rows, :] = got[g].astype(F32)
+
+    def gather(row):
+        return plain[pl.ds(row, groups, stride=rows), :]
+
+    lane = lax.broadcasted_iota(jnp.int32, (groups, TILE), 1)
+    quarter = lane // slab
+    for k in range(3):
+        for c in range(per):
+            m = c * 3 + k
+            here = slice(c * groups, (c + 1) * groups)
+            for p in range(2):
+                for y in range(cols):
+                    tiles[k, p, y + 1, here, :] = gather(m * ROWS + p * cols + y)
+                edge = jnp.zeros((groups, TILE), F32)
+                for i in range(quarters):
+                    face = gather((channels + m // 4) * ROWS + cols + 2 * i + p)
+                    edge = jnp.where(quarter == i, pltpu.roll(face, (i - m % 4) * slab % TILE, 1), edge)
+                tiles[k, p, 0, here, :] = jnp.where(has_lower_y, edge, 0.0)
+                tiles[k, p, cols + 1, here, :] = jnp.where(has_lower_y, 0.0, edge)
+    rhs[3 * width :, :] = jnp.zeros((rhs.shape[0] - 3 * width, 2 * TILE), BF16)
+    wide = lax.broadcasted_iota(jnp.int32, (cases, TILE), 1)
+
+    def both(pieces):
+        return jnp.concatenate(pieces, axis=0)
+
+    def column(y, carry):
+        stack = []
+        face_rows = [gather((channels + j) * ROWS + y) for j in range(2)]
+        for p in range(2):
+            ends = gather((channels + 1) * ROWS + p * cols + y)
+            spaced = jnp.zeros((groups, TILE), F32)
+            for i in range(quarters):
+                spaced = jnp.where(quarter == i, pltpu.roll(ends, (i * slab - TILE // 2 - i * (slab // 2)) % TILE, 1), spaced)
+            grads = []
+            for k in range(3):
+                mine = tiles[k, p, y + 1]
+                other = tiles[k, 1 - p, y + 1]
+                beside = [face_rows[(c * 3 + k) // 4] for c in range(per)]
+                if p == 0:
+                    edge = both([pltpu.roll(beside[c], -((c * 3 + k) % 4) * slab % TILE, 1) for c in range(per)])
+                    edge = jnp.where(has_lower_x, edge, 0.0)
+                    before = jnp.where(wide < slab, edge, pltpu.roll(other, slab, 1))
+                    after = other
+                else:
+                    edge = both([pltpu.roll(beside[c], (quarters - 1 - (c * 3 + k) % 4) * slab % TILE, 1) for c in range(per)])
+                    edge = jnp.where(has_lower_x, 0.0, edge)
+                    before = other
+                    after = jnp.where(wide >= TILE - slab, edge, pltpu.roll(other, TILE - slab, 1))
+                grad_x = 0.5 * (after - before)
+                grad_y = 0.5 * (tiles[k, p, y + 2] - tiles[k, p, y])
+                below = both([pltpu.roll(spaced, -2 * (c * 3 + k) % TILE, 1) for c in range(per)])
+                above = both([pltpu.roll(spaced, (slab - 2 - 2 * (c * 3 + k)) % TILE, 1) for c in range(per)])
+                below = jnp.where(wide % slab == 0, below, pltpu.roll(mine, 1, 1))
+                above = jnp.where(wide % slab == slab - 1, above, pltpu.roll(mine, TILE - 1, 1))
+                grads.append((grad_x, grad_y, 0.5 * (above - below)))
+            shear = moduli[0, pl.ds(p * cols + y, 1), :]
+            first = moduli[1, pl.ds(p * cols + y, 1), :]
+            volume = first * (grads[0][0] + grads[1][1] + grads[2][2])
+            twice = 2.0 * shear
+            stack.append(
+                [
+                    volume + twice * grads[0][0],
+                    volume + twice * grads[1][1],
+                    volume + twice * grads[2][2],
+                    shear * (grads[0][1] + grads[1][0]),
+                    shear * (grads[1][2] + grads[2][1]),
+                    shear * (grads[2][0] + grads[0][2]),
+                ]
+            )
+        stress = [jnp.concatenate([stack[0][n], stack[1][n]], axis=1).astype(BF16) for n in range(6)]
+        for n in range(3):
+            sums[n * cases : (n + 1) * cases, :] = stress[n]
+        exact = [s.astype(F32) for s in stress]
+        root = math.sqrt(3.0)
+        parts = [
+            (0.5 * root) * (exact[0] - exact[1]),
+            0.5 * (exact[0] + exact[1]) - exact[2],
+            root * exact[3],
+            root * exact[4],
+            root * exact[5],
+        ]
+        for s in range(shifts):
+            form = None
+            for part in parts:
+                term = part * (part if s == 0 else pltpu.roll(part, cases - s, 0))
+                form = term if form is None else form + term
+            upper = form.astype(BF16)
+            lower = (form - upper.astype(F32)).astype(BF16)
+            at = s * cases
+            rhs[at : at + cases, :] = upper
+            rhs[width + at : width + at + cases, :] = lower
+            rhs[2 * width + at : 2 * width + at + cases, :] = upper
+        mises2 = jnp.dot(pairs[...], rhs[...], preferred_element_type=F32)
+        top = jnp.max(mises2, axis=0, keepdims=True)
+        hydro = jnp.dot(linear[:, : 3 * cases], sums[...], preferred_element_type=F32)
+        most = jnp.max(hydro, axis=0, keepdims=True)
+        least = jnp.min(hydro, axis=0, keepdims=True)
+        for p in range(2):
+            cut = slice(p * TILE, (p + 1) * TILE)
+            best[p, pl.ds(y, 1), :] = top[:, cut]
+            high[p, pl.ds(y, 1), :] = most[:, cut]
+            low[p, pl.ds(y, 1), :] = least[:, cut]
+        return carry
+
+    lax.fori_loop(0, cols, column, 0)
+    for p in range(2):
+        vm = jnp.sqrt(jnp.maximum(best[p], 0.0))
+        hyd = high[p] * (1.0 / 3.0) - low[p] * (1.0 / 3.0)
+        for i in range(quarters):
+            cut = slice(i * slab, (i + 1) * slab)
+            peak[2 * i + p] = vm[:, cut]
+            spread[2 * i + p] = hyd[:, cut]
+
+
+def swapped_faces(field):
+    received = []
+    for axis, dim in (("bx", 2), ("by", 3)):
+        size = field.shape[dim]
+        first = lax.slice_in_dim(field, 0, 1, axis=dim)
+        last = lax.slice_in_dim(field, size - 1, size, axis=dim)
+        face = jnp.where(lax.axis_index(axis) == 0, last, first)
+        face = face.reshape(face.shape[0] * 3 * 8, -1)
+        received.append(lax.ppermute(face, axis, [(0, 1), (1, 0)]))
+    return received
+
+
+def tiled_shards(displacements, material_ids, lame, slab_bounds, load_history):
+    per, _, rows, cols, depth = displacements.shape
+    groups = lax.axis_size("case")
+    slab = depth // groups
+    cases = per * groups
+    steps = load_history.shape[0]
+    channels = per * 3
+    vmem = pl.BlockSpec(memory_space=pltpu.VMEM)
+    smem = pl.BlockSpec(memory_space=pltpu.SMEM)
+    shifts, width, total, first, second, plain = pair_table(cases, groups)
+    params = pltpu.CompilerParams(vmem_limit_bytes=32 * 1024 * 1024)
+    with jax.named_scope("prepare"):
+        pairs, linear, moduli = pl.pallas_call(
+            functools.partial(prepare_kernel, width, slab),
+            out_shape=(
+                jax.ShapeDtypeStruct((steps, total), BF16),
+                jax.ShapeDtypeStruct((steps, TILE), BF16),
+                jax.ShapeDtypeStruct((2, ROWS, TILE), F32),
+            ),
+            in_specs=[vmem] * 5 + [smem] * 2,
+            out_specs=(vmem,) * 3,
+            compiler_params=params,
+        )(
+            load_history.T,
+            jnp.asarray(first, BF16),
+            jnp.asarray(second, BF16),
+            jnp.asarray(plain, BF16),
+            material_ids.reshape(rows * cols, depth),
+            lame,
+            slab_bounds,
+        )
+    face_x, face_y = swapped_faces(displacements)
+    lines = (channels + 2) * ROWS
+    with jax.named_scope("pack"):
+        packed = pl.pallas_call(
+            functools.partial(pack_kernel, slab),
+            out_shape=jax.ShapeDtypeStruct((groups, lines, TILE), BF16),
+            in_specs=[vmem] * 3,
+            out_specs=vmem,
+            compiler_params=params,
+        )(displacements.reshape(channels * rows * cols, depth), face_x, face_y)
+    got = lax.all_to_all(packed, "case", split_axis=0, concat_axis=0, tiled=True)
+    with jax.named_scope("stress"):
+        return pl.pallas_call(
+            functools.partial(stress_kernel, shifts, slab),
+            out_shape=(jax.ShapeDtypeStruct((rows, cols, slab), F32),) * 2,
+            in_specs=[vmem] * 4,
+            out_specs=(vmem,) * 2,
+            scratch_shapes=[
+                pltpu.VMEM((groups * lines, TILE), F32),
+                pltpu.VMEM((3, 2, cols + 2, cases, TILE), F32),
+                pltpu.VMEM((total, 2 * TILE), BF16),
+                pltpu.VMEM((3 * cases, 2 * TILE), BF16),
+                pltpu.VMEM((2, cols, TILE), F32),
+                pltpu.VMEM((2, cols, TILE), F32),
+                pltpu.VMEM((2, cols, TILE), F32),
+            ],
+            compiler_params=params,
+        )(got, pairs, linear, moduli)
+
+
+def fits_tiles(mesh, displacements, load_history):
+    groups, bricks_x, bricks_y = (mesh.shape[a] for a in ("case", "bx", "by"))
+    cases, comps, rows, cols, depth = displacements.shape
+    if bricks_x != 2 or bricks_y != 2 or cases % groups or depth % groups:
+        return False
+    per, rows, cols, slab = cases // groups, rows // 2, cols // 2, depth // groups
+    return (
+        groups == 8 and per == 2 and comps == 3 and rows == 8 and cols == 8 and slab == 32
+        and load_history.shape[0] % 16 == 0
+    )
+
+
 def solution(mesh):
     in_specs = (P("case", None, "bx", "by", None), P("bx", "by", None), P(), P(None, "bx"), P())
     out_specs = (P("bx", "by", "case"), P("bx", "by", "case"))
-    return jax.shard_map(shards, mesh=mesh, in_specs=in_specs, out_specs=out_specs, check_vma=False)
+
+    def run(displacements, material_ids, lame, slab_bounds, load_history):
+        body = tiled_shards if fits_tiles(mesh, displacements, load_history) else shards
+        placed = jax.shard_map(body, mesh=mesh, in_specs=in_specs, out_specs=out_specs, check_vma=False)
+        return placed(displacements, material_ids, lame, slab_bounds, load_history)
+
+    return run

time: 85.7 us -> 31.1 us (0.36)
  other arithmetic: 26.5 us -> 0.82 us
  blocking collectives: 18.9 us -> 0 us
  matrix products: 16.2 us -> 0 us
  local copies, waits for them, and re-layouts: 11.9 us -> 1.75 us
  Pallas kernels: 0 us -> 10.1 us
  waiting for transfers between devices: 1.77 us -> 8.38 us
    all_to_all x1 -> x0, blocking collectives: 18.9 us -> none  [shards(): lax.all_to_all(blocks, 'case', split_axis=4, concat_axis=0, tiled=True)]
    dot_general x8 -> x0, matrix products: 16.2 us -> none  [histories(): jnp.dot(factors, flat, preferred_element_type=jnp.float32)]
    reduce_max x4 -> x0, other arithmetic: 13.9 us -> none  [histories(): block_high = jnp.max(hydro, axis=0)]
    mul x2 -> x0, other arithmetic: 11 us -> none  [the longest x1 5.95 us: combine_stress(): shear_xy = shear_mod * (grads[0][1] + grads[1][0]) * weight]
    pallas_call x0 -> x3, Pallas kernels: none -> 10.1 us  [the longest x1 7.61 us: tiled_shards(): pl.pallas_call(functools.partial(stress_kernel, shifts, slab), out_shape=...]
    all_to_all x0 -> x1, waiting for transfers between devices: none -> 7.2 us  [tiled_shards(): lax.all_to_all(packed, 'case', split_axis=0, concat_axis=0, tiled=True)]
    all_to_all x0 -> x1, starting transfers between devices: none -> 5.95 us  [tiled_shards(): lax.all_to_all(packed, 'case', split_axis=0, concat_axis=0, tiled=True)]
    ppermute x4 -> x2, starting transfers between devices: 8.92 us -> 3.04 us  [swapped_faces(): received.append(lax.ppermute(face, axis, [(0, 1), (1, 0)]))]
  transfers between devices with their start and end apart: 4 -> 3, of which waited for: 1 -> 3; matrix products, arithmetic and copies ran while one was open for 17% -> 4% of each run, Pallas kernels for 0% -> 4%
where the time goes in v1:
time: 31.1 us; the launch traced here: 30.8 us
  Pallas kernels  10.1 us (32%)
  starting transfers between devices  8.99 us (29%)
  waiting for transfers between devices  8.38 us (27%)
  local copies, waits for them, and re-layouts  1.75 us (6%)
  other arithmetic  0.82 us (3%)
  between operations  0.75 us (2%)
    pallas_call x1, Pallas kernels, tiled_shards(): pl.pallas_call(functools.partial(stress_kernel, shifts, slab), out_shape=...  7.61 us
    all_to_all x1, waiting for transfers between devices, tiled_shards(): lax.all_to_all(packed, 'case', split_axis=0, concat_axis=0, tiled=True)  7.2 us
    all_to_all x1, starting transfers between devices, tiled_shards(): lax.all_to_all(packed, 'case', split_axis=0, concat_axis=0, tiled=True)  5.95 us
    ppermute x2, starting transfers between devices, swapped_faces(): received.append(lax.ppermute(face, axis, [(0, 1), (1, 0)]))  3.04 us
    pallas_call x1, Pallas kernels, tiled_shards(): pl.pallas_call(functools.partial(prepare_kernel, width, slab), out_shape=...  1.36 us
    ppermute x2, waiting for transfers between devices, swapped_faces(): received.append(lax.ppermute(face, axis, [(0, 1), (1, 0)]))  1.18 us
    pallas_call x1, Pallas kernels, tiled_shards(): pl.pallas_call(functools.partial(pack_kernel, slab), out_shape=jax.ShapeD...  1.15 us
    slice x1, local copies, waits for them, and re-layouts, swapped_faces(): last = lax.slice_in_dim(field, size - 1, size, axis=dim)  1.1 us
  transfers between devices with their start and end apart: 3, of which 3 were waited for; matrix products, arithmetic and copies ran while one was open for 4% of the time, Pallas kernels for 4%

profile of v1, /device:TPU:0, one launch (start us, length us, event | category | flops | bytes accessed | tf_op | source)
XLA Modules:
  0.0 30.8 jit_solution(13410010269420744796)
XLA Ops:
  0.6 0.0 copy-start
  0.6 0.8 %slice_select_fusion = bf16[2,3,1,8,256]{4,3,2,1,0:T(8,128)(2,1)S(1)} fusion(bf16[2,3,8,8,256]{4,3,2,1,0:T(8,128)(2,1)} %param.8, pred[]{:T(512)S(6)} %eq.6), kind=kLoop, calls=%fused_computation.1 | loop fusion | flops 12288 | bytes 73729 | tf_op jit(solution)/shard_map/jit(_where)/select_n | solution.py:355
  1.5 3.0 %collective-permute-start = (bf16[48,256]{1,0:T(8,128)(2,1)S(1)}, bf16[48,256]{1,0:T(8,128)(2,1)S(1)}, u32[]{:S(2)}, u32[]{:S(2)}) collective-permute-start(bf16[48,256]{1,0:T(8,128)(2,1)S(1)} %bitcast.8), channel_id=1, source_target_pairs={{0,2},{2,0},{1,3},{3,1},{4,6},{6,4},{5,7},{7,5},{8,10},{10,8},{9,1... | collective-permute-start | bytes 73736 | tf_op jit(solution)/shard_map/ppermute | solution.py:357
  4.4 1.1 %fusion = (bf16[2,3,8,1,256]{4,3,2,1,0:T(2,128)(2,1)S(1)}, bf16[2,3,8,1,256]{4,3,2,1,0:T(2,128)(2,1)S(1)}) fusion(bf16[2,3,8,8,256]{4,3,2,1,0:T(8,128)(2,1)} %param.8), kind=kLoop, calls=%fused_computation.2 | loop fusion | bytes 98304 | tf_op jit(solution)/shard_map/slice | solution.py:354
  5.6 0.1 collective-permute-start.1
  5.6 0.6 %collective-permute-done.face_x = bf16[48,256]{1,0:T(8,128)(2,1)S(1)} collective-permute-done((bf16[48,256]{1,0:T(8,128)(2,1)S(1)}, bf16[48,256]{1,0:T(8,128)(2,1)S(1)}, u32[]{:S(2)}, u32[]{:S(2)}) %collective-permute-start) | collective-permute-done | bytes 24608 | tf_op jit(solution)/shard_map/ppermute | solution.py:357
  6.2 0.6 %collective-permute-done.1.face_y = bf16[48,256]{1,0:T(8,128)(2,1)S(1)} collective-permute-done((bf16[48,256]{1,0:T(8,128)(2,1)S(1)}, bf16[48,256]{1,0:T(8,128)(2,1)S(1)}, u32[]{:S(2)}, u32[]{:S(2)}) %collective-permute-start.1) | collective-permute-done | bytes 24608 | tf_op jit(solution)/shard_map/ppermute | solution.py:357
  6.8 0.0 copy-done
  6.8 1.1 %pack.1 = bf16[8,128,128]{2,1,0:T(8,128)(2,1)} custom-call(bf16[384,256]{1,0:T(8,128)(2,1)S(1)} %bitcast.5, bf16[48,256]{1,0:T(8,128)(2,1)S(1)} %collective-permute-done.face_x, bf16[48,256]{1,0:T(8,128)(2,1)S(1)} %collective-permute-done.1.face_y), custom_call_target="tpu_custom_call" | custom-call | tf_op jit(solution)/shard_map/pack/pallas_call | solution.py:395
  8.0 0.0 copy-start.1
  8.0 0.0 copy-start.2
  8.0 0.0 copy-start.3
  8.0 0.0 copy-start.4
  8.0 0.0 copy-start.5
  8.0 0.0 copy-start.7
  8.0 5.9 %all-to-all-start = ((bf16[8,128,128]{2,1,0:T(8,128)(2,1)}), bf16[8,128,128]{2,1,0:T(8,128)(2,1)S(1)}, u32[]{:S(2)}, u32[]{:S(2)}) async-start(bf16[8,128,128]{2,1,0:T(8,128)(2,1)} %pack.1), calls=%async_computation | async-start | bytes 524288 | tf_op jit(solution)/shard_map/all_to_all | solution.py:402
  13.9 0.0 copy-start.6
  14.0 0.0 copy-done.1
  14.0 0.0 copy-done.2
  14.0 0.0 copy-done.3
  14.0 0.0 copy-done.4
  14.0 0.0 copy-done.5
  14.0 0.0 copy-done.7
  14.0 0.6 %copy-done.6 = f32[2,8]{1,0:T(2,128)S(1)} copy-done((f32[2,8]{1,0:T(2,128)S(1)}, f32[2,8]{1,0:T(2,128)}, u32[]{:S(2)}) %copy-start.6) | copy-done | bytes 88
  14.6 1.4 %prepare.1 = (bf16[1024,512]{1,0:T(8,128)(2,1)S(1)}, bf16[1024,128]{1,0:T(8,128)(2,1)S(1)}, f32[2,16,128]{2,1,0:T(8,128)S(1)}) custom-call(bf16[16,1024]{1,0:T(8,128)(2,1)S(1)} %bitcast.7, bf16[16,512]{1,0:T(8,128)(2,1)S(1)} %copy-done.4, bf16[16,512]{1,0:T(8,128)(2,1)S(1)} %copy-done.3, bf16[16,128]{1,0:T(8,128)(2,1)S(1)} %copy-done.5, ...), custom_call_target="tpu_custom_call" | custom-call | tf_op jit(solution)/shard_map/prepare/pallas_call | solution.py:373
  16.0 7.2 %all-to-all-done.got = bf16[8,128,128]{2,1,0:T(8,128)(2,1)S(1)} async-done(((bf16[8,128,128]{2,1,0:T(8,128)(2,1)}), bf16[8,128,128]{2,1,0:T(8,128)(2,1)S(1)}, u32[]{:S(2)}, u32[]{:S(2)}) %all-to-all-start) | async-done | bytes 262176 | tf_op jit(solution)/shard_map/all_to_all | solution.py:402
  23.2 7.6 %stress.1 = (f32[8,8,32]{2,1,0:T(8,128)}, f32[8,8,32]{2,1,0:T(8,128)}) custom-call(bf16[8,128,128]{2,1,0:T(8,128)(2,1)S(1)} %all-to-all-done.got, bf16[1024,512]{1,0:T(8,128)(2,1)S(1)} %get-tuple-element.5.pairs, bf16[1024,128]{1,0:T(8,128)(2,1)S(1)} %get-tuple-element.6.linear, f32[2,16,128]{2,1,0:T(8,128)S(1)} %get-tuple-element.7.moduli), custom_call_target="tpu_custom_call" | custom-call | tf_op jit(solution)/shard_map/stress/pallas_call | solution.py:404
  (1 shorter events, 0.0 us)
Async XLA Ops:
  0.6 6.2 %copy-start = (bf16[2,3,8,8,256]{4,3,2,1,0:T(8,128)(2,1)S(1)}, bf16[2,3,8,8,256]{4,3,2,1,0:T(8,128)(2,1)}, u32[]{:S(2)}) copy-start(bf16[2,3,8,8,256]{4,3,2,1,0:T(8,128)(2,1)} %param.8) | copy-start | bytes 589828
  1.5 4.8 %collective-permute-start = (bf16[48,256]{1,0:T(8,128)(2,1)S(1)}, bf16[48,256]{1,0:T(8,128)(2,1)S(1)}, u32[]{:S(2)}, u32[]{:S(2)}) collective-permute-start(bf16[48,256]{1,0:T(8,128)(2,1)S(1)} %bitcast.8), channel_id=1, source_target_pairs={{0,2},{2,0},{1,3},{3,1},{4,6},{6,4},{5,7},{7,5},{8,10},{10,8},{9,1... | collective-permute-start | bytes 73736 | tf_op jit(solution)/shard_map/ppermute | solution.py:357
  5.6 1.3 %collective-permute-start.1 = (bf16[48,256]{1,0:T(8,128)(2,1)S(1)}, bf16[48,256]{1,0:T(8,128)(2,1)S(1)}, u32[]{:S(2)}, u32[]{:S(2)}) collective-permute-start(bf16[48,256]{1,0:T(8,128)(2,1)S(1)} %bitcast.9), channel_id=1, source_target_pairs={{0,1},{1,0},{2,3},{3,2},{4,5},{5,4},{6,7},{7,6},{8,9},{9,8},{10,11... | collective-permute-start | bytes 73736 | tf_op jit(solution)/shard_map/ppermute | solution.py:357
  8.0 6.0 %copy-start.1 = (s32[8,8,256]{2,1,0:T(8,128)S(1)}, s32[8,8,256]{2,1,0:T(8,128)}, u32[]{:S(2)}) copy-start(s32[8,8,256]{2,1,0:T(8,128)} %param.9) | copy-start | bytes 196612
  8.0 6.0 %copy-start.2 = (bf16[1024,16]{0,1:T(8,128)(2,1)S(1)}, bf16[1024,16]{0,1:T(8,128)(2,1)}, u32[]{:S(2)}) copy-start(bf16[1024,16]{0,1:T(8,128)(2,1)} %param.12) | copy-start | bytes 98308
  8.0 6.0 %copy-start.3 = (bf16[16,512]{1,0:T(8,128)(2,1)S(1)}, bf16[16,512]{1,0:T(8,128)(2,1)}, u32[]{:S(2)}) copy-start(bf16[16,512]{1,0:T(8,128)(2,1)} %constant.15.clone.second) | copy-start | bytes 49156
  8.0 6.0 %copy-start.4 = (bf16[16,512]{1,0:T(8,128)(2,1)S(1)}, bf16[16,512]{1,0:T(8,128)(2,1)}, u32[]{:S(2)}) copy-start(bf16[16,512]{1,0:T(8,128)(2,1)} %constant.14.clone.first) | copy-start | bytes 49156
  8.0 6.0 %copy-start.5 = (bf16[16,128]{1,0:T(8,128)(2,1)S(1)}, bf16[16,128]{1,0:T(8,128)(2,1)}, u32[]{:S(2)}) copy-start(bf16[16,128]{1,0:T(8,128)(2,1)} %constant.16.clone.plain) | copy-start | bytes 12292
  8.0 6.0 %copy-start.7 = (s32[2,8]{1,0:T(2,128)S(1)}, s32[2,8]{1,0:T(2,128)}, u32[]{:S(2)}) copy-start(s32[2,8]{1,0:T(2,128)} %bounds.1) | copy-start | bytes 196
  8.0 15.2 %all-to-all-start = ((bf16[8,128,128]{2,1,0:T(8,128)(2,1)}), bf16[8,128,128]{2,1,0:T(8,128)(2,1)S(1)}, u32[]{:S(2)}, u32[]{:S(2)}) async-start(bf16[8,128,128]{2,1,0:T(8,128)(2,1)} %pack.1), calls=%async_computation | async-start | bytes 524288 | tf_op jit(solution)/shard_map/all_to_all | solution.py:402
  13.9 0.7 %copy-start.6 = (f32[2,8]{1,0:T(2,128)S(1)}, f32[2,8]{1,0:T(2,128)}, u32[]{:S(2)}) copy-start(f32[2,8]{1,0:T(2,128)} %lame.1) | copy-start | bytes 196

commit v2 on v1

--- a/solution.py
+++ b/solution.py
@@ -220,7 +220,8 @@
         ).astype(BF16)
 
 
-def stress_kernel(shifts, slab, got, pairs, linear, moduli, peak, spread, plain, tiles, rhs, sums, best, high, low):
+def stress_kernel(shifts, slab, got, pairs, linear, moduli, peak, spread, plain, tiles, rhs_even, rhs_odd, sums_even, sums_odd, best, high, low):
+    rhs, sums = (rhs_even, rhs_odd), (sums_even, sums_odd)
     groups, rows, _ = got.shape
     quarters = TILE // slab
     channels = rows // ROWS - 2
@@ -251,13 +252,14 @@
                     edge = jnp.where(quarter == i, pltpu.roll(face, (i - m % 4) * slab % TILE, 1), edge)
                 tiles[k, p, 0, here, :] = jnp.where(has_lower_y, edge, 0.0)
                 tiles[k, p, cols + 1, here, :] = jnp.where(has_lower_y, 0.0, edge)
-    rhs[3 * width :, :] = jnp.zeros((rhs.shape[0] - 3 * width, 2 * TILE), BF16)
+    for buffer in rhs:
+        buffer[3 * width :, :] = jnp.zeros((buffer.shape[0] - 3 * width, 2 * TILE), BF16)
     wide = lax.broadcasted_iota(jnp.int32, (cases, TILE), 1)
 
     def both(pieces):
         return jnp.concatenate(pieces, axis=0)
 
-    def column(y, carry):
+    def build(y, rhs, sums):
         stack = []
         face_rows = [gather((channels + j) * ROWS + y) for j in range(2)]
         for p in range(2):
@@ -324,6 +326,7 @@
             rhs[at : at + cases, :] = upper
             rhs[width + at : width + at + cases, :] = lower
             rhs[2 * width + at : 2 * width + at + cases, :] = upper
+    def reduce(y, rhs, sums):
         mises2 = jnp.dot(pairs[...], rhs[...], preferred_element_type=F32)
         top = jnp.max(mises2, axis=0, keepdims=True)
         hydro = jnp.dot(linear[:, : 3 * cases], sums[...], preferred_element_type=F32)
@@ -334,9 +337,12 @@
             best[p, pl.ds(y, 1), :] = top[:, cut]
             high[p, pl.ds(y, 1), :] = most[:, cut]
             low[p, pl.ds(y, 1), :] = least[:, cut]
-        return carry
-
-    lax.fori_loop(0, cols, column, 0)
+
+    build(0, rhs[0], sums[0])
+    for y in range(cols):
+        if y + 1 < cols:
+            build(y + 1, rhs[(y + 1) % 2], sums[(y + 1) % 2])
+        reduce(y, rhs[y % 2], sums[y % 2])
     for p in range(2):
         vm = jnp.sqrt(jnp.maximum(best[p], 0.0))
         hyd = high[p] * (1.0 / 3.0) - low[p] * (1.0 / 3.0)
@@ -410,6 +416,8 @@
                 pltpu.VMEM((groups * lines, TILE), F32),
                 pltpu.VMEM((3, 2, cols + 2, cases, TILE), F32),
                 pltpu.VMEM((total, 2 * TILE), BF16),
+                pltpu.VMEM((total, 2 * TILE), BF16),
+                pltpu.VMEM((3 * cases, 2 * TILE), BF16),
                 pltpu.VMEM((3 * cases, 2 * TILE), BF16),
                 pltpu.VMEM((2, cols, TILE), F32),
                 pltpu.VMEM((2, cols, TILE), F32),

time: 31.1 us -> 28 us (0.900)
  Pallas kernels: 10.1 us -> 7.04 us
    pallas_call x1, Pallas kernels: 7.61 us -> 4.53 us  [tiled_shards(): pl.pallas_call(functools.partial(stress_kernel, shifts, slab), out_shape=...]
  transfers between devices with their start and end apart: 3 -> 3, of which waited for: 3 -> 3; matrix products, arithmetic and copies ran while one was open for 4% -> 4% of each run, Pallas kernels for 4% -> 5%
where the time goes in v2:
time: 28 us; the launch traced here: 27.7 us
  starting transfers between devices  8.99 us (32%)
  waiting for transfers between devices  8.38 us (30%)
  Pallas kernels  7.04 us (25%)
  local copies, waits for them, and re-layouts  1.75 us (6%)
  other arithmetic  0.82 us (3%)
  between operations  0.75 us (3%)
    all_to_all x1, waiting for transfers between devices, tiled_shards(): lax.all_to_all(packed, 'case', split_axis=0, concat_axis=0, tiled=True)  7.2 us
    all_to_all x1, starting transfers between devices, tiled_shards(): lax.all_to_all(packed, 'case', split_axis=0, concat_axis=0, tiled=True)  5.95 us
    pallas_call x1, Pallas kernels, tiled_shards(): pl.pallas_call(functools.partial(stress_kernel, shifts, slab), out_shape=...  4.53 us
    ppermute x2, starting transfers between devices, swapped_faces(): received.append(lax.ppermute(face, axis, [(0, 1), (1, 0)]))  3.04 us
    pallas_call x1, Pallas kernels, tiled_shards(): pl.pallas_call(functools.partial(prepare_kernel, width, slab), out_shape=...  1.36 us
    ppermute x2, waiting for transfers between devices, swapped_faces(): received.append(lax.ppermute(face, axis, [(0, 1), (1, 0)]))  1.18 us
    pallas_call x1, Pallas kernels, tiled_shards(): pl.pallas_call(functools.partial(pack_kernel, slab), out_shape=jax.ShapeD...  1.15 us
    slice x1, local copies, waits for them, and re-layouts, swapped_faces(): last = lax.slice_in_dim(field, size - 1, size, axis=dim)  1.1 us
  transfers between devices with their start and end apart: 3, of which 3 were waited for; matrix products, arithmetic and copies ran while one was open for 4% of the time, Pallas kernels for 5%

profile of v2, /device:TPU:0, one launch (start us, length us, event | category | flops | bytes accessed | tf_op | source)
XLA Modules:
  0.0 27.7 jit_solution(8795497397631460062)
XLA Ops:
  0.6 0.0 copy-start
  0.6 0.8 %slice_select_fusion = bf16[2,3,1,8,256]{4,3,2,1,0:T(8,128)(2,1)S(1)} fusion(bf16[2,3,8,8,256]{4,3,2,1,0:T(8,128)(2,1)} %param.8, pred[]{:T(512)S(6)} %eq.6), kind=kLoop, calls=%fused_computation.1 | loop fusion | flops 12288 | bytes 73729 | tf_op jit(solution)/shard_map/jit(_where)/select_n | solution.py:361
  1.5 3.0 %collective-permute-start = (bf16[48,256]{1,0:T(8,128)(2,1)S(1)}, bf16[48,256]{1,0:T(8,128)(2,1)S(1)}, u32[]{:S(2)}, u32[]{:S(2)}) collective-permute-start(bf16[48,256]{1,0:T(8,128)(2,1)S(1)} %bitcast.8), channel_id=1, source_target_pairs={{0,2},{2,0},{1,3},{3,1},{4,6},{6,4},{5,7},{7,5},{8,10},{10,8},{9,1... | collective-permute-start | bytes 73736 | tf_op jit(solution)/shard_map/ppermute | solution.py:363
  4.4 1.1 %fusion = (bf16[2,3,8,1,256]{4,3,2,1,0:T(2,128)(2,1)S(1)}, bf16[2,3,8,1,256]{4,3,2,1,0:T(2,128)(2,1)S(1)}) fusion(bf16[2,3,8,8,256]{4,3,2,1,0:T(8,128)(2,1)} %param.8), kind=kLoop, calls=%fused_computation.2 | loop fusion | bytes 98304 | tf_op jit(solution)/shard_map/slice | solution.py:360
  5.6 0.1 collective-permute-start.1
  5.6 0.6 %collective-permute-done.face_x = bf16[48,256]{1,0:T(8,128)(2,1)S(1)} collective-permute-done((bf16[48,256]{1,0:T(8,128)(2,1)S(1)}, bf16[48,256]{1,0:T(8,128)(2,1)S(1)}, u32[]{:S(2)}, u32[]{:S(2)}) %collective-permute-start) | collective-permute-done | bytes 24608 | tf_op jit(solution)/shard_map/ppermute | solution.py:363
  6.2 0.6 %collective-permute-done.1.face_y = bf16[48,256]{1,0:T(8,128)(2,1)S(1)} collective-permute-done((bf16[48,256]{1,0:T(8,128)(2,1)S(1)}, bf16[48,256]{1,0:T(8,128)(2,1)S(1)}, u32[]{:S(2)}, u32[]{:S(2)}) %collective-permute-start.1) | collective-permute-done | bytes 24608 | tf_op jit(solution)/shard_map/ppermute | solution.py:363
  6.8 0.0 copy-done
  6.8 1.1 %pack.1 = bf16[8,128,128]{2,1,0:T(8,128)(2,1)} custom-call(bf16[384,256]{1,0:T(8,128)(2,1)S(1)} %bitcast.5, bf16[48,256]{1,0:T(8,128)(2,1)S(1)} %collective-permute-done.face_x, bf16[48,256]{1,0:T(8,128)(2,1)S(1)} %collective-permute-done.1.face_y), custom_call_target="tpu_custom_call" | custom-call | tf_op jit(solution)/shard_map/pack/pallas_call | solution.py:401
  8.0 0.0 copy-start.1
  8.0 0.0 copy-start.2
  8.0 0.0 copy-start.3
  8.0 0.0 copy-start.4
  8.0 0.0 copy-start.5
  8.0 0.0 copy-start.7
  8.0 5.9 %all-to-all-start = ((bf16[8,128,128]{2,1,0:T(8,128)(2,1)}), bf16[8,128,128]{2,1,0:T(8,128)(2,1)S(1)}, u32[]{:S(2)}, u32[]{:S(2)}) async-start(bf16[8,128,128]{2,1,0:T(8,128)(2,1)} %pack.1), calls=%async_computation | async-start | bytes 524288 | tf_op jit(solution)/shard_map/all_to_all | solution.py:408
  13.9 0.0 copy-start.6
  14.0 0.0 copy-done.1
  14.0 0.0 copy-done.2
  14.0 0.0 copy-done.3
  14.0 0.0 copy-done.4
  14.0 0.0 copy-done.5
  14.0 0.0 copy-done.7
  14.0 0.6 %copy-done.6 = f32[2,8]{1,0:T(2,128)S(1)} copy-done((f32[2,8]{1,0:T(2,128)S(1)}, f32[2,8]{1,0:T(2,128)}, u32[]{:S(2)}) %copy-start.6) | copy-done | bytes 88
  14.6 1.4 %prepare.1 = (bf16[1024,512]{1,0:T(8,128)(2,1)S(1)}, bf16[1024,128]{1,0:T(8,128)(2,1)S(1)}, f32[2,16,128]{2,1,0:T(8,128)S(1)}) custom-call(bf16[16,1024]{1,0:T(8,128)(2,1)S(1)} %bitcast.7, bf16[16,512]{1,0:T(8,128)(2,1)S(1)} %copy-done.4, bf16[16,512]{1,0:T(8,128)(2,1)S(1)} %copy-done.3, bf16[16,128]{1,0:T(8,128)(2,1)S(1)} %copy-done.5, ...), custom_call_target="tpu_custom_call" | custom-call | tf_op jit(solution)/shard_map/prepare/pallas_call | solution.py:379
  16.0 7.2 %all-to-all-done.got = bf16[8,128,128]{2,1,0:T(8,128)(2,1)S(1)} async-done(((bf16[8,128,128]{2,1,0:T(8,128)(2,1)}), bf16[8,128,128]{2,1,0:T(8,128)(2,1)S(1)}, u32[]{:S(2)}, u32[]{:S(2)}) %all-to-all-start) | async-done | bytes 262176 | tf_op jit(solution)/shard_map/all_to_all | solution.py:408
  23.2 4.5 %stress.1 = (f32[8,8,32]{2,1,0:T(8,128)}, f32[8,8,32]{2,1,0:T(8,128)}) custom-call(bf16[8,128,128]{2,1,0:T(8,128)(2,1)S(1)} %all-to-all-done.got, bf16[1024,512]{1,0:T(8,128)(2,1)S(1)} %get-tuple-element.5.pairs, bf16[1024,128]{1,0:T(8,128)(2,1)S(1)} %get-tuple-element.6.linear, f32[2,16,128]{2,1,0:T(8,128)S(1)} %get-tuple-element.7.moduli), custom_call_target="tpu_custom_call" | custom-call | tf_op jit(solution)/shard_map/stress/pallas_call | solution.py:410
  (1 shorter events, 0.0 us)
Async XLA Ops:
  0.6 6.2 %copy-start = (bf16[2,3,8,8,256]{4,3,2,1,0:T(8,128)(2,1)S(1)}, bf16[2,3,8,8,256]{4,3,2,1,0:T(8,128)(2,1)}, u32[]{:S(2)}) copy-start(bf16[2,3,8,8,256]{4,3,2,1,0:T(8,128)(2,1)} %param.8) | copy-start | bytes 589828
  1.5 4.8 %collective-permute-start = (bf16[48,256]{1,0:T(8,128)(2,1)S(1)}, bf16[48,256]{1,0:T(8,128)(2,1)S(1)}, u32[]{:S(2)}, u32[]{:S(2)}) collective-permute-start(bf16[48,256]{1,0:T(8,128)(2,1)S(1)} %bitcast.8), channel_id=1, source_target_pairs={{0,2},{2,0},{1,3},{3,1},{4,6},{6,4},{5,7},{7,5},{8,10},{10,8},{9,1... | collective-permute-start | bytes 73736 | tf_op jit(solution)/shard_map/ppermute | solution.py:363
  5.6 1.3 %collective-permute-start.1 = (bf16[48,256]{1,0:T(8,128)(2,1)S(1)}, bf16[48,256]{1,0:T(8,128)(2,1)S(1)}, u32[]{:S(2)}, u32[]{:S(2)}) collective-permute-start(bf16[48,256]{1,0:T(8,128)(2,1)S(1)} %bitcast.9), channel_id=1, source_target_pairs={{0,1},{1,0},{2,3},{3,2},{4,5},{5,4},{6,7},{7,6},{8,9},{9,8},{10,11... | collective-permute-start | bytes 73736 | tf_op jit(solution)/shard_map/ppermute | solution.py:363
  8.0 6.0 %copy-start.1 = (s32[8,8,256]{2,1,0:T(8,128)S(1)}, s32[8,8,256]{2,1,0:T(8,128)}, u32[]{:S(2)}) copy-start(s32[8,8,256]{2,1,0:T(8,128)} %param.9) | copy-start | bytes 196612
  8.0 6.0 %copy-start.2 = (bf16[1024,16]{0,1:T(8,128)(2,1)S(1)}, bf16[1024,16]{0,1:T(8,128)(2,1)}, u32[]{:S(2)}) copy-start(bf16[1024,16]{0,1:T(8,128)(2,1)} %param.12) | copy-start | bytes 98308
  8.0 6.0 %copy-start.3 = (bf16[16,512]{1,0:T(8,128)(2,1)S(1)}, bf16[16,512]{1,0:T(8,128)(2,1)}, u32[]{:S(2)}) copy-start(bf16[16,512]{1,0:T(8,128)(2,1)} %constant.15.clone.second) | copy-start | bytes 49156
  8.0 6.0 %copy-start.4 = (bf16[16,512]{1,0:T(8,128)(2,1)S(1)}, bf16[16,512]{1,0:T(8,128)(2,1)}, u32[]{:S(2)}) copy-start(bf16[16,512]{1,0:T(8,128)(2,1)} %constant.14.clone.first) | copy-start | bytes 49156
  8.0 6.0 %copy-start.5 = (bf16[16,128]{1,0:T(8,128)(2,1)S(1)}, bf16[16,128]{1,0:T(8,128)(2,1)}, u32[]{:S(2)}) copy-start(bf16[16,128]{1,0:T(8,128)(2,1)} %constant.16.clone.plain) | copy-start | bytes 12292
  8.0 6.0 %copy-start.7 = (s32[2,8]{1,0:T(2,128)S(1)}, s32[2,8]{1,0:T(2,128)}, u32[]{:S(2)}) copy-start(s32[2,8]{1,0:T(2,128)} %bounds.1) | copy-start | bytes 196
  8.0 15.2 %all-to-all-start = ((bf16[8,128,128]{2,1,0:T(8,128)(2,1)}), bf16[8,128,128]{2,1,0:T(8,128)(2,1)S(1)}, u32[]{:S(2)}, u32[]{:S(2)}) async-start(bf16[8,128,128]{2,1,0:T(8,128)(2,1)} %pack.1), calls=%async_computation | async-start | bytes 524288 | tf_op jit(solution)/shard_map/all_to_all | solution.py:408
  13.9 0.7 %copy-start.6 = (f32[2,8]{1,0:T(2,128)S(1)}, f32[2,8]{1,0:T(2,128)}, u32[]{:S(2)}) copy-start(f32[2,8]{1,0:T(2,128)} %lame.1) | copy-start | bytes 196

commit v3 on v1

--- a/solution.py
+++ b/solution.py
@@ -184,7 +184,7 @@
         moduli[part] = value * weight
 
 
-def pack_kernel(slab, field, face_x, face_y, out):
+def pack_kernel(slab, field, out):
     groups = out.shape[0]
     depth = field.shape[1]
     quarters = TILE // slab
@@ -203,104 +203,102 @@
             mixed = jnp.where((lane % slab == 2 * m) & (lane >= slab), below, mixed)
             mixed = jnp.where((lane % slab == 2 * m + 1) & (lane < depth - slab), above, mixed)
         ends.append(mixed)
-    half = ROWS // 2
-    faces = [
-        jnp.concatenate([face_x[m * half : (m + 1) * half, :].astype(F32), face_y[m * half : (m + 1) * half, :].astype(F32)], axis=0)
-        for m in range(channels)
-    ]
     for g in range(groups):
         cut = slice(g * slab, (g + 1) * slab)
-        short = slice(g * slab, g * slab + slab // 2)
-        for m in range(channels):
-            out[g, m * ROWS : (m + 1) * ROWS, :] = jnp.concatenate([parts[m][i][:, cut] for i in range(quarters)], axis=1).astype(BF16)
-        top = channels * ROWS
-        out[g, top : top + ROWS, :] = jnp.concatenate([faces[q][:, cut] for q in range(4)], axis=1).astype(BF16)
-        out[g, top + ROWS : top + 2 * ROWS, :] = jnp.concatenate(
-            [faces[4][:, cut], faces[5][:, cut]] + [ends[i][:, short] for i in range(quarters)], axis=1
-        ).astype(BF16)
-
-
-def stress_kernel(shifts, slab, got, pairs, linear, moduli, peak, spread, plain, tiles, rhs, sums, best, high, low):
+        for m, pieces in enumerate(parts + [ends]):
+            out[g, m * ROWS : (m + 1) * ROWS, :] = jnp.concatenate([piece[:, cut] for piece in pieces], axis=1).astype(BF16)
+
+
+def gather_kernel(slab, got, tiles, ends, face_x, face_y, plain):
     groups, rows, _ = got.shape
     quarters = TILE // slab
-    channels = rows // ROWS - 2
-    per = channels // 3
+    per = (rows // ROWS - 1) // 3
     cases = per * groups
     cols = ROWS // 2
-    width = shifts * cases
-    has_lower_x = lax.axis_index("bx") == 1
-    has_lower_y = lax.axis_index("by") == 1
+    brick_x = lax.axis_index("bx")
+    brick_y = lax.axis_index("by")
     for g in range(groups):
         plain[g * rows : (g + 1) * rows, :] = got[g].astype(F32)
 
     def gather(row):
         return plain[pl.ds(row, groups, stride=rows), :]
 
-    lane = lax.broadcasted_iota(jnp.int32, (groups, TILE), 1)
-    quarter = lane // slab
-    for k in range(3):
-        for c in range(per):
-            m = c * 3 + k
-            here = slice(c * groups, (c + 1) * groups)
-            for p in range(2):
-                for y in range(cols):
-                    tiles[k, p, y + 1, here, :] = gather(m * ROWS + p * cols + y)
-                edge = jnp.zeros((groups, TILE), F32)
-                for i in range(quarters):
-                    face = gather((channels + m // 4) * ROWS + cols + 2 * i + p)
-                    edge = jnp.where(quarter == i, pltpu.roll(face, (i - m % 4) * slab % TILE, 1), edge)
-                tiles[k, p, 0, here, :] = jnp.where(has_lower_y, edge, 0.0)
-                tiles[k, p, cols + 1, here, :] = jnp.where(has_lower_y, 0.0, edge)
-    rhs[3 * width :, :] = jnp.zeros((rhs.shape[0] - 3 * width, 2 * TILE), BF16)
+    def column(k, p, y):
+        return jnp.concatenate([gather((c * 3 + k) * ROWS + p * cols + y) for c in range(per)], axis=0)
+
+    lane = lax.broadcasted_iota(jnp.int32, (cases, TILE), 1)
+    for y in range(cols):
+        packed = jnp.zeros((cases, TILE), F32)
+        for k in range(3):
+            even, odd = column(k, 0, y), column(k, 1, y)
+            tiles[k, 0, y] = even
+            tiles[k, 1, y] = odd
+            even = pltpu.roll(even, k * slab, 1) if k else even
+            odd = pltpu.roll(odd, (k + 1 - quarters) * slab % TILE, 1)
+            packed = jnp.where(lane // slab == k, jnp.where(brick_x == 0, odd, even), packed)
+            if y == 0:
+                firsts = (tiles[k, 0, 0], tiles[k, 1, 0])
+                for p in range(2):
+                    face_y[k, p] = firsts[p].astype(BF16)
+            if y == cols - 1:
+                for p in range(2):
+                    face_y[k, p] = jnp.where(brick_y == 0, tiles[k, p, y], face_y[k, p].astype(F32)).astype(BF16)
+        face_x[y] = packed.astype(BF16)
+        for p in range(2):
+            ends[p, y] = gather(3 * per * ROWS + p * cols + y)
+
+
+def column_steps(shifts, slab, tiles, ends, pairs, linear, moduli, face_x, face_y, best, high, low):
+    cases = tiles.shape[3]
+    groups = ends.shape[2]
+    per = cases // groups
+    quarters = TILE // slab
+    cols = ROWS // 2
+    width = shifts * cases
     wide = lax.broadcasted_iota(jnp.int32, (cases, TILE), 1)
+    lower_y = lax.axis_index("by") == 1
 
     def both(pieces):
         return jnp.concatenate(pieces, axis=0)
 
-    def column(y, carry):
-        stack = []
-        face_rows = [gather((channels + j) * ROWS + y) for j in range(2)]
-        for p in range(2):
-            ends = gather((channels + 1) * ROWS + p * cols + y)
-            spaced = jnp.zeros((groups, TILE), F32)
-            for i in range(quarters):
-                spaced = jnp.where(quarter == i, pltpu.roll(ends, (i * slab - TILE // 2 - i * (slab // 2)) % TILE, 1), spaced)
-            grads = []
-            for k in range(3):
-                mine = tiles[k, p, y + 1]
-                other = tiles[k, 1 - p, y + 1]
-                beside = [face_rows[(c * 3 + k) // 4] for c in range(per)]
-                if p == 0:
-                    edge = both([pltpu.roll(beside[c], -((c * 3 + k) % 4) * slab % TILE, 1) for c in range(per)])
-                    edge = jnp.where(has_lower_x, edge, 0.0)
-                    before = jnp.where(wide < slab, edge, pltpu.roll(other, slab, 1))
-                    after = other
-                else:
-                    edge = both([pltpu.roll(beside[c], (quarters - 1 - (c * 3 + k) % 4) * slab % TILE, 1) for c in range(per)])
-                    edge = jnp.where(has_lower_x, 0.0, edge)
-                    before = other
-                    after = jnp.where(wide >= TILE - slab, edge, pltpu.roll(other, TILE - slab, 1))
-                grad_x = 0.5 * (after - before)
-                grad_y = 0.5 * (tiles[k, p, y + 2] - tiles[k, p, y])
-                below = both([pltpu.roll(spaced, -2 * (c * 3 + k) % TILE, 1) for c in range(per)])
-                above = both([pltpu.roll(spaced, (slab - 2 - 2 * (c * 3 + k)) % TILE, 1) for c in range(per)])
-                below = jnp.where(wide % slab == 0, below, pltpu.roll(mine, 1, 1))
-                above = jnp.where(wide % slab == slab - 1, above, pltpu.roll(mine, TILE - 1, 1))
-                grads.append((grad_x, grad_y, 0.5 * (above - below)))
-            shear = moduli[0, pl.ds(p * cols + y, 1), :]
-            first = moduli[1, pl.ds(p * cols + y, 1), :]
-            volume = first * (grads[0][0] + grads[1][1] + grads[2][2])
-            twice = 2.0 * shear
-            stack.append(
-                [
-                    volume + twice * grads[0][0],
-                    volume + twice * grads[1][1],
-                    volume + twice * grads[2][2],
-                    shear * (grads[0][1] + grads[1][0]),
-                    shear * (grads[1][2] + grads[2][1]),
-                    shear * (grads[2][0] + grads[0][2]),
-                ]
-            )
+    def stress_of(p, y, beside):
+        last = jnp.where(p == 0, 0, quarters - 1)
+        at_edge = wide // slab == last
+        sign = jnp.where(p == 0, 0.5, -0.5).astype(F32)
+        grads = []
+        for k in range(3):
+            mine = tiles[k, p, y]
+            other = tiles[k, 1 - p, y]
+            shifted = pltpu.roll(other, jnp.where(p == 0, slab, TILE - slab), 1)
+            if beside:
+                edge = pltpu.roll(face_x[y].astype(F32), lax.rem((last - k) * slab + TILE, TILE), 1)
+            else:
+                edge = jnp.zeros((cases, TILE), F32)
+            grad_x = sign * (other - jnp.where(at_edge, edge, shifted))
+            before = tiles[k, p, y - 1] if y else jnp.where(lower_y, face_y[k, p].astype(F32), 0.0)
+            after = tiles[k, p, y + 1] if y + 1 < cols else jnp.where(lower_y, 0.0, face_y[k, p].astype(F32))
+            outside = ends[p, y]
+            below = both([pltpu.roll(outside, -2 * (c * 3 + k) % TILE, 1) for c in range(per)])
+            above = both([pltpu.roll(outside, (slab - 2 - 2 * (c * 3 + k)) % TILE, 1) for c in range(per)])
+            below = jnp.where(wide % slab == 0, below, pltpu.roll(mine, 1, 1))
+            above = jnp.where(wide % slab == slab - 1, above, pltpu.roll(mine, TILE - 1, 1))
+            grads.append((grad_x, 0.5 * (after - before), 0.5 * (above - below)))
+        shear = moduli[0, pl.ds(p * cols + y, 1), :]
+        first = moduli[1, pl.ds(p * cols + y, 1), :]
+        volume = first * (grads[0][0] + grads[1][1] + grads[2][2])
+        twice = 2.0 * shear
+        return [
+            volume + twice * grads[0][0],
+            volume + twice * grads[1][1],
+            volume + twice * grads[2][2],
+            shear * (grads[0][1] + grads[1][0]),
+            shear * (grads[1][2] + grads[2][1]),
+            shear * (grads[2][0] + grads[0][2]),
+        ]
+
+    def build(step, rhs, sums):
+        p, columns, beside, _ = step
+        stack = [stress_of(p, y, beside) for y in columns]
         stress = [jnp.concatenate([stack[0][n], stack[1][n]], axis=1).astype(BF16) for n in range(6)]
         for n in range(3):
             sums[n * cases : (n + 1) * cases, :] = stress[n]
@@ -324,38 +322,55 @@
             rhs[at : at + cases, :] = upper
             rhs[width + at : width + at + cases, :] = lower
             rhs[2 * width + at : 2 * width + at + cases, :] = upper
+
+    def reduce(step, rhs, sums):
+        _, columns, _, slot = step
         mises2 = jnp.dot(pairs[...], rhs[...], preferred_element_type=F32)
-        top = jnp.max(mises2, axis=0, keepdims=True)
         hydro = jnp.dot(linear[:, : 3 * cases], sums[...], preferred_element_type=F32)
-        most = jnp.max(hydro, axis=0, keepdims=True)
-        least = jnp.min(hydro, axis=0, keepdims=True)
-        for p in range(2):
-            cut = slice(p * TILE, (p + 1) * TILE)
-            best[p, pl.ds(y, 1), :] = top[:, cut]
-            high[p, pl.ds(y, 1), :] = most[:, cut]
-            low[p, pl.ds(y, 1), :] = least[:, cut]
-        return carry
-
-    lax.fori_loop(0, cols, column, 0)
-    for p in range(2):
-        vm = jnp.sqrt(jnp.maximum(best[p], 0.0))
-        hyd = high[p] * (1.0 / 3.0) - low[p] * (1.0 / 3.0)
-        for i in range(quarters):
+        tops = (jnp.max(mises2, axis=0, keepdims=True), jnp.max(hydro, axis=0, keepdims=True), jnp.min(hydro, axis=0, keepdims=True))
+        for half, y in enumerate(columns):
+            for into, row in zip((best, high, low), tops):
+                into[slot, y : y + 1, :] = row[:, half * TILE : (half + 1) * TILE]
+
+    return build, reduce
+
+
+def run_steps(build, reduce, steps, width, rhs, sums):
+    for buffer in rhs:
+        buffer[3 * width :, :] = jnp.zeros((buffer.shape[0] - 3 * width, 2 * TILE), BF16)
+    build(steps[0], rhs[0], sums[0])
+    for n, step in enumerate(steps):
+        if n + 1 < len(steps):
+            build(steps[n + 1], rhs[(n + 1) % 2], sums[(n + 1) % 2])
+        reduce(step, rhs[n % 2], sums[n % 2])
+
+
+def inner_kernel(shifts, slab, tiles, ends, pairs, linear, moduli, best, high, low, rhs_even, rhs_odd, sums_even, sums_odd):
+    p = lax.axis_index("bx")
+    cols = ROWS // 2
+    build, reduce = column_steps(shifts, slab, tiles, ends, pairs, linear, moduli, None, None, best, high, low)
+    steps = [(p, (y, y + 1), False, 0) for y in range(1, cols - 1, 2)]
+    run_steps(build, reduce, steps, shifts * tiles.shape[3], (rhs_even, rhs_odd), (sums_even, sums_odd))
+
+
+def outer_kernel(
+    shifts, slab, tiles, ends, pairs, linear, moduli, face_x, face_y, inner_best, inner_high, inner_low,
+    peak, spread, rhs_even, rhs_odd, sums_even, sums_odd, best, high, low,
+):
+    p = lax.axis_index("bx")
+    cols = ROWS // 2
+    build, reduce = column_steps(shifts, slab, tiles, ends, pairs, linear, moduli, face_x, face_y, best, high, low)
+    steps = [(p, (0, cols - 1), False, 0)] + [(1 - p, (y, y + 1), True, 1) for y in range(0, cols, 2)]
+    run_steps(build, reduce, steps, shifts * tiles.shape[3], (rhs_even, rhs_odd), (sums_even, sums_odd))
+    for into, inner in ((best, inner_best), (high, inner_high), (low, inner_low)):
+        into[0, 1 : cols - 1, :] = inner[0, 1 : cols - 1, :]
+    for slot, parity in ((0, p), (1, 1 - p)):
+        vm = jnp.sqrt(jnp.maximum(best[slot], 0.0))
+        hyd = high[slot] * (1.0 / 3.0) - low[slot] * (1.0 / 3.0)
+        for i in range(TILE // slab):
             cut = slice(i * slab, (i + 1) * slab)
-            peak[2 * i + p] = vm[:, cut]
-            spread[2 * i + p] = hyd[:, cut]
-
-
-def swapped_faces(field):
-    received = []
-    for axis, dim in (("bx", 2), ("by", 3)):
-        size = field.shape[dim]
-        first = lax.slice_in_dim(field, 0, 1, axis=dim)
-        last = lax.slice_in_dim(field, size - 1, size, axis=dim)
-        face = jnp.where(lax.axis_index(axis) == 0, last, first)
-        face = face.reshape(face.shape[0] * 3 * 8, -1)
-        received.append(lax.ppermute(face, axis, [(0, 1), (1, 0)]))
-    return received
+            peak[2 * i + parity] = vm[:, cut]
+            spread[2 * i + parity] = hyd[:, cut]
 
 
 def tiled_shards(displacements, material_ids, lame, slab_bounds, load_history):
@@ -369,14 +384,11 @@
     smem = pl.BlockSpec(memory_space=pltpu.SMEM)
     shifts, width, total, first, second, plain = pair_table(cases, groups)
     params = pltpu.CompilerParams(vmem_limit_bytes=32 * 1024 * 1024)
+    like = jax.ShapeDtypeStruct
     with jax.named_scope("prepare"):
         pairs, linear, moduli = pl.pallas_call(
             functools.partial(prepare_kernel, width, slab),
-            out_shape=(
-                jax.ShapeDtypeStruct((steps, total), BF16),
-                jax.ShapeDtypeStruct((steps, TILE), BF16),
-                jax.ShapeDtypeStruct((2, ROWS, TILE), F32),
-            ),
+            out_shape=(like((steps, total), BF16), like((steps, TILE), BF16), like((2, ROWS, TILE), F32)),
             in_specs=[vmem] * 5 + [smem] * 2,
             out_specs=(vmem,) * 3,
             compiler_params=params,
@@ -389,34 +401,51 @@
             lame,
             slab_bounds,
         )
-    face_x, face_y = swapped_faces(displacements)
-    lines = (channels + 2) * ROWS
+    lines = (channels + 1) * ROWS
     with jax.named_scope("pack"):
         packed = pl.pallas_call(
             functools.partial(pack_kernel, slab),
-            out_shape=jax.ShapeDtypeStruct((groups, lines, TILE), BF16),
-            in_specs=[vmem] * 3,
+            out_shape=like((groups, lines, TILE), BF16),
+            in_specs=[vmem],
             out_specs=vmem,
             compiler_params=params,
-        )(displacements.reshape(channels * rows * cols, depth), face_x, face_y)
+        )(displacements.reshape(channels * rows * cols, depth))
     got = lax.all_to_all(packed, "case", split_axis=0, concat_axis=0, tiled=True)
-    with jax.named_scope("stress"):
+    with jax.named_scope("gather"):
+        tiles, ends, face_x, face_y = pl.pallas_call(
+            functools.partial(gather_kernel, slab),
+            out_shape=(
+                like((3, 2, cols, cases, TILE), F32),
+                like((2, cols, groups, TILE), F32),
+                like((cols, cases, TILE), BF16),
+                like((3, 2, cases, TILE), BF16),
+            ),
+            in_specs=[vmem],
+            out_specs=(vmem,) * 4,
+            scratch_shapes=[pltpu.VMEM((groups * lines, TILE), F32)],
+            compiler_params=params,
+        )(got)
+    face_x = lax.ppermute(face_x, "bx", [(0, 1), (1, 0)])
+    face_y = lax.ppermute(face_y, "by", [(0, 1), (1, 0)])
+    buffers = [pltpu.VMEM((total, 2 * TILE), BF16)] * 2 + [pltpu.VMEM((3 * cases, 2 * TILE), BF16)] * 2
+    with jax.named_scope("inner"):
+        inner = pl.pallas_call(
+            functools.partial(inner_kernel, shifts, slab),
+            out_shape=(like((1, cols, TILE), F32),) * 3,
+            in_specs=[vmem] * 5,
+            out_specs=(vmem,) * 3,
+            scratch_shapes=buffers,
+            compiler_params=params,
+        )(tiles, ends, pairs, linear, moduli)
+    with jax.named_scope("outer"):
         return pl.pallas_call(
-            functools.partial(stress_kernel, shifts, slab),
-            out_shape=(jax.ShapeDtypeStruct((rows, cols, slab), F32),) * 2,
-            in_specs=[vmem] * 4,
+            functools.partial(outer_kernel, shifts, slab),
+            out_shape=(like((rows, cols, slab), F32),) * 2,
+            in_specs=[vmem] * 10,
             out_specs=(vmem,) * 2,
-            scratch_shapes=[
-                pltpu.VMEM((groups * lines, TILE), F32),
-                pltpu.VMEM((3, 2, cols + 2, cases, TILE), F32),
-                pltpu.VMEM((total, 2 * TILE), BF16),
-                pltpu.VMEM((3 * cases, 2 * TILE), BF16),
-                pltpu.VMEM((2, cols, TILE), F32),
-                pltpu.VMEM((2, cols, TILE), F32),
-                pltpu.VMEM((2, cols, TILE), F32),
-            ],
+            scratch_shapes=buffers + [pltpu.VMEM((2, cols, TILE), F32)] * 3,
             compiler_params=params,
-        )(got, pairs, linear, moduli)
+        )(tiles, ends, pairs, linear, moduli, face_x, face_y, *inner)
 
 
 def fits_tiles(mesh, displacements, load_history):

time: 31.1 us -> 26.4 us (0.85)
  blocking collectives: 0 us -> 15.5 us
  waiting for transfers between devices: 8.38 us -> 0.01 us
  starting transfers between devices: 8.99 us -> 1.59 us
  Pallas kernels: 10.1 us -> 6.77 us
  other arithmetic: 0.82 us -> 0 us
    all_to_all x0 -> x1, blocking collectives: none -> 15.5 us  [tiled_shards(): lax.all_to_all(packed, 'case', split_axis=0, concat_axis=0, tiled=True)]
    all_to_all x1 -> x0, waiting for transfers between devices: 7.2 us -> none  [tiled_shards(): lax.all_to_all(packed, 'case', split_axis=0, concat_axis=0, tiled=True)]
    all_to_all x1 -> x0, starting transfers between devices: 5.95 us -> none  [tiled_shards(): lax.all_to_all(packed, 'case', split_axis=0, concat_axis=0, tiled=True)]
    pallas_call x2 -> x4, Pallas kernels: 8.76 us -> 5.41 us  [the longest x1 3.18 us: tiled_shards(): pl.pallas_call(functools.partial(outer_kernel, shifts, slab), out_shape=(...]
    ppermute x2, starting transfers between devices: 3.04 us -> 1.59 us  [the longest x1 1.58 us: tiled_shards(): face_x = lax.ppermute(face_x, 'bx', [(0, 1), (1, 0)])]
    ppermute x2, waiting for transfers between devices: 1.18 us -> 0.01 us  [the longest x1 0.01 us: tiled_shards(): face_x = lax.ppermute(face_x, 'bx', [(0, 1), (1, 0)])]
    slice x1 -> x0, local copies, waits for them, and re-layouts: 1.1 us -> none  [swapped_faces(): last = lax.slice_in_dim(field, size - 1, size, axis=dim)]
    unnamed x16, local copies, waits for them, and re-layouts: 0.65 us -> 1.58 us
  transfers between devices with their start and end apart: 3 -> 2, of which waited for: 3 -> 0; matrix products, arithmetic and copies ran while one was open for 4% -> 0% of each run, Pallas kernels for 4% -> 11%
where the time goes in v3:
time: 26.4 us; the launch traced here: 26.2 us
  blocking collectives  15.5 us (59%)
  Pallas kernels  6.77 us (26%)
  starting transfers between devices  1.59 us (6%)
  local copies, waits for them, and re-layouts  1.58 us (6%)
  between operations  0.73 us (3%)
    all_to_all x1, blocking collectives, tiled_shards(): lax.all_to_all(packed, 'case', split_axis=0, concat_axis=0, tiled=True)  15.5 us
    pallas_call x1, Pallas kernels, tiled_shards(): pl.pallas_call(functools.partial(outer_kernel, shifts, slab), out_shape=(...  3.18 us
    pallas_call x1, Pallas kernels, tiled_shards(): pl.pallas_call(functools.partial(inner_kernel, shifts, slab), out_shape=(...  1.62 us
    ppermute x1, starting transfers between devices, tiled_shards(): face_x = lax.ppermute(face_x, 'bx', [(0, 1), (1, 0)])  1.58 us
    unnamed x16, local copies, waits for them, and re-layouts  1.58 us
    pallas_call x1, Pallas kernels, tiled_shards(): pl.pallas_call(functools.partial(prepare_kernel, width, slab), out_shape=...  1.36 us
  transfers between devices with their start and end apart: 2, of which 0 were waited for; matrix products, arithmetic and copies ran while one was open for 0% of the time, Pallas kernels for 11%

profile of v3, /device:TPU:0, one launch (start us, length us, event | category | flops | bytes accessed | tf_op | source)
XLA Modules:
  0.0 26.2 jit_solution(12510068257331007930)
XLA Ops:
  0.6 0.0 copy-start
  0.6 0.9 %copy-done = bf16[2,3,8,8,256]{4,3,2,1,0:T(8,128)(2,1)S(1)} copy-done((bf16[2,3,8,8,256]{4,3,2,1,0:T(8,128)(2,1)S(1)}, bf16[2,3,8,8,256]{4,3,2,1,0:T(8,128)(2,1)}, u32[]{:S(2)}) %copy-start) | copy-done | bytes 196632
  1.6 0.4 %pack.1 = bf16[8,112,128]{2,1,0:T(8,128)(2,1)S(1)} custom-call(bf16[384,256]{1,0:T(8,128)(2,1)S(1)} %bitcast.3), custom_call_target="tpu_custom_call" | custom-call | tf_op jit(solution)/shard_map/pack/pallas_call | solution.py:406
  2.0 15.5 %all_to_all.5.got = bf16[8,112,128]{2,1,0:T(8,128)(2,1)S(1)} all-to-all(bf16[8,112,128]{2,1,0:T(8,128)(2,1)S(1)} %pack.1), channel_id=1, replica_groups=mesh['case'=8,'bx'=2,'by'=2] {'case'}, dimensions={0} | all-to-all | bytes 458752 | tf_op jit(solution)/shard_map/all_to_all | solution.py:413
  17.5 0.0 copy-start.1
  17.5 0.0 copy-start.2
  17.5 0.0 copy-start.3
  17.5 0.0 copy-start.4
  17.5 0.0 copy-start.7
  17.5 0.2 gather.1
  17.7 0.0 copy-start.5
  17.7 1.6 %collective-permute-start = (bf16[8,16,128]{2,1,0:T(8,128)(2,1)S(1)}, bf16[8,16,128]{2,1,0:T(8,128)(2,1)S(1)}, u32[]{:S(2)}, u32[]{:S(2)}) collective-permute-start(bf16[8,16,128]{2,1,0:T(8,128)(2,1)S(1)} %get-tuple-element.17), channel_id=1, source_target_pairs={{0,2},{2,0},{1,3},{3,1},{4,6},{6,4},{5,7},{7,5},{8,10},{10,8},{9,1... | collective-permute-start | bytes 98312 | tf_op jit(solution)/shard_map/ppermute | solution.py:428
  19.3 0.0 collective-permute-start.1
  19.3 0.0 copy-start.6
  19.3 0.0 copy-done.1
  19.3 0.0 copy-done.2
  19.3 0.0 copy-done.3
  19.3 0.0 copy-done.4
  19.3 0.0 copy-done.7
  19.3 0.0 copy-done.5
  19.3 0.6 %copy-done.6 = f32[2,8]{1,0:T(2,128)S(1)} copy-done((f32[2,8]{1,0:T(2,128)S(1)}, f32[2,8]{1,0:T(2,128)}, u32[]{:S(2)}) %copy-start.6) | copy-done | bytes 88
  20.0 1.4 %prepare.1 = (bf16[1024,512]{1,0:T(8,128)(2,1)S(1)}, bf16[1024,128]{1,0:T(8,128)(2,1)S(1)}, f32[2,16,128]{2,1,0:T(8,128)S(1)}) custom-call(bf16[16,1024]{1,0:T(8,128)(2,1)S(1)} %bitcast.5, bf16[16,512]{1,0:T(8,128)(2,1)S(1)} %copy-done.4, bf16[16,512]{1,0:T(8,128)(2,1)S(1)} %copy-done.3, bf16[16,128]{1,0:T(8,128)(2,1)S(1)} %copy-done.5, ...), custom_call_target="tpu_custom_call" | custom-call | tf_op jit(solution)/shard_map/prepare/pallas_call | solution.py:389
  21.3 1.6 %inner.1 = (f32[1,8,128]{2,1,0:T(8,128)S(1)}, f32[1,8,128]{2,1,0:T(8,128)S(1)}, f32[1,8,128]{2,1,0:T(8,128)S(1)}) custom-call(f32[3,2,8,16,128]{4,3,2,1,0:T(8,128)S(1)} %get-tuple-element.12.tiles, f32[2,8,8,128]{3,2,1,0:T(8,128)S(1)} %get-tuple-element.13.ends, bf16[1024,512]{1,0:T(8,128)(2,1)S(1)} %get-tuple-element.14.pairs, ...), custom_call_target="tpu_custom_call" | custom-call | tf_op jit(solution)/shard_map/inner/pallas_call | solution.py:432
  23.0 0.0 collective-permute-done.1.face_y
  23.0 0.0 collective-permute-done.face_x
  23.0 3.2 %outer.1 = (f32[8,8,32]{2,1,0:T(8,128)}, f32[8,8,32]{2,1,0:T(8,128)}) custom-call(f32[3,2,8,16,128]{4,3,2,1,0:T(8,128)S(1)} %get-tuple-element.12.tiles, f32[2,8,8,128]{3,2,1,0:T(8,128)S(1)} %get-tuple-element.13.ends, bf16[1024,512]{1,0:T(8,128)(2,1)S(1)} %get-tuple-element.14.pairs, bf16[1024,128]{1,0:T(8,128)(2,1)S(1)} %get-tuple-element.15.linear, ...), custom_call_target="tpu_custom_call" | custom-call | tf_op jit(solution)/shard_map/outer/pallas_call | solution.py:441
Async XLA Ops:
  0.6 0.9 %copy-start = (bf16[2,3,8,8,256]{4,3,2,1,0:T(8,128)(2,1)S(1)}, bf16[2,3,8,8,256]{4,3,2,1,0:T(8,128)(2,1)}, u32[]{:S(2)}) copy-start(bf16[2,3,8,8,256]{4,3,2,1,0:T(8,128)(2,1)} %param.8) | copy-start | bytes 589828
  17.5 1.8 %copy-start.1 = (s32[8,8,256]{2,1,0:T(8,128)S(1)}, s32[8,8,256]{2,1,0:T(8,128)}, u32[]{:S(2)}) copy-start(s32[8,8,256]{2,1,0:T(8,128)} %param.9) | copy-start | bytes 196612
  17.5 1.8 %copy-start.2 = (bf16[1024,16]{0,1:T(8,128)(2,1)S(1)}, bf16[1024,16]{0,1:T(8,128)(2,1)}, u32[]{:S(2)}) copy-start(bf16[1024,16]{0,1:T(8,128)(2,1)} %param.12) | copy-start | bytes 98308
  17.5 1.8 %copy-start.3 = (bf16[16,512]{1,0:T(8,128)(2,1)S(1)}, bf16[16,512]{1,0:T(8,128)(2,1)}, u32[]{:S(2)}) copy-start(bf16[16,512]{1,0:T(8,128)(2,1)} %constant.7.clone.second) | copy-start | bytes 49156
  17.5 1.8 %copy-start.4 = (bf16[16,512]{1,0:T(8,128)(2,1)S(1)}, bf16[16,512]{1,0:T(8,128)(2,1)}, u32[]{:S(2)}) copy-start(bf16[16,512]{1,0:T(8,128)(2,1)} %constant.6.clone.first) | copy-start | bytes 49156
  17.5 1.9 %copy-start.7 = (s32[2,8]{1,0:T(2,128)S(1)}, s32[2,8]{1,0:T(2,128)}, u32[]{:S(2)}) copy-start(s32[2,8]{1,0:T(2,128)} %bounds.1) | copy-start | bytes 196
  17.7 1.6 %copy-start.5 = (bf16[16,128]{1,0:T(8,128)(2,1)S(1)}, bf16[16,128]{1,0:T(8,128)(2,1)}, u32[]{:S(2)}) copy-start(bf16[16,128]{1,0:T(8,128)(2,1)} %constant.8.clone.plain) | copy-start | bytes 12292
  17.7 5.3 %collective-permute-start = (bf16[8,16,128]{2,1,0:T(8,128)(2,1)S(1)}, bf16[8,16,128]{2,1,0:T(8,128)(2,1)S(1)}, u32[]{:S(2)}, u32[]{:S(2)}) collective-permute-start(bf16[8,16,128]{2,1,0:T(8,128)(2,1)S(1)} %get-tuple-element.17), channel_id=1, source_target_pairs={{0,2},{2,0},{1,3},{3,1},{4,6},{6,4},{5,7},{7,5},{8,10},{10,8},{9,1... | collective-permute-start | bytes 98312 | tf_op jit(solution)/shard_map/ppermute | solution.py:428
  19.3 3.7 %collective-permute-start.1 = (bf16[3,2,16,128]{3,2,1,0:T(8,128)(2,1)S(1)}, bf16[3,2,16,128]{3,2,1,0:T(8,128)(2,1)S(1)}, u32[]{:S(2)}, u32[]{:S(2)}) collective-permute-start(bf16[3,2,16,128]{3,2,1,0:T(8,128)(2,1)S(1)} %get-tuple-element.18), channel_id=1, source_target_pairs={{0,1},{1,0},{2,3},{3,2},{4,5},{5,4},{6,7},{7,6},{8,9},{9,8},{10,11... | collective-permute-start | bytes 73736 | tf_op jit(solution)/shard_map/ppermute | solution.py:429
  19.3 0.7 %copy-start.6 = (f32[2,8]{1,0:T(2,128)S(1)}, f32[2,8]{1,0:T(2,128)}, u32[]{:S(2)}) copy-start(f32[2,8]{1,0:T(2,128)} %lame.1) | copy-start | bytes 196

commit v4 on v3

--- a/solution.py
+++ b/solution.py
@@ -125,39 +125,45 @@
 BF16 = jnp.bfloat16
 TILE = 128
 ROWS = 16
-SIDES = 2
-
-
-def pair_table(cases, groups):
+EXCHANGE_ORDER = (5, 6, 4, 1, 7, 3, 2, 0)
+
+
+def pair_table(cases, order):
+    groups = len(order)
     per = cases // groups
-    place = np.array([(j % groups) * per + j // groups for j in range(cases)])
-    shifts = cases // 2 + 1
-    width = shifts * cases
-    total = -(-3 * width // 256) * 256
-    first = np.zeros((cases, total), np.float32)
-    second = np.zeros((cases, total), np.float32)
+    place = np.array([order[j % groups] * per + j // groups for j in range(cases)])
+    half = cases // 2
+    main = half * cases
+    first = np.zeros((cases, main + TILE), np.float32)
+    second = np.zeros((cases, main + TILE), np.float32)
     plain = np.zeros((cases, TILE), np.float32)
-    for copy in range(3):
-        for s in range(shifts):
-            for j in range(cases):
-                col = copy * width + s * cases + j
-                first[place[j], col] = 1.0
-                second[place[(j + s) % cases], col] = 1.0 if s in (0, cases // 2) else 2.0
-        for j in range(cases):
+    for j in range(cases):
+        for s in range(half):
+            first[place[j], s * cases + j] = 1.0
+            second[place[(j + s) % cases], s * cases + j] = 2.0 if s else 1.0
+        for copy in range(3):
+            first[place[j], main + copy * cases + j] = 1.0
+            second[place[(j + half) % cases], main + copy * cases + j] = 1.0
             plain[place[j], copy * cases + j] = 1.0
-    return shifts, width, total, first, second, plain
-
-
-def prepare_kernel(width, slab, loads, first, second, plain, ids, lame, bounds, pairs, linear, moduli):
+    return main, np.concatenate([first, second, plain], axis=1)
+
+
+def prepare_kernel(main, slab, loads, picks, ids, lame, bounds, pairs, linear, moduli):
     over = (((0,), (0,)), ((), ()))
     table = loads[...]
-    prod = lax.dot_general(table, first[...], over, preferred_element_type=F32)
-    prod = prod * lax.dot_general(table, second[...], over, preferred_element_type=F32)
-    high = prod.astype(BF16)
-    low = (prod - high.astype(F32)).astype(BF16)
-    col = lax.broadcasted_iota(jnp.int32, prod.shape, 1)
-    pairs[...] = jnp.where(col < 2 * width, high.astype(F32), low.astype(F32)).astype(BF16)
-    linear[...] = lax.dot_general(table, plain[...], over, preferred_element_type=F32).astype(BF16)
+    factor = lax.dot_general(table, picks[...], over, preferred_element_type=F32)
+    wide = main + TILE
+    prod = factor[:, :wide] * factor[:, wide : 2 * wide]
+    most = prod[:, :main]
+    high = most.astype(BF16)
+    pairs[:, :main] = high
+    pairs[:, main : 2 * main] = high
+    pairs[:, 2 * main : 3 * main] = (most - high.astype(F32)).astype(BF16)
+    last = prod[:, main:]
+    high = last.astype(BF16).astype(F32)
+    col = lax.broadcasted_iota(jnp.int32, last.shape, 1)
+    pairs[:, 3 * main :] = jnp.where(col < 2 * table.shape[0], high, last - high).astype(BF16)
+    linear[...] = factor[:, 2 * wide :].astype(BF16)
     group = lax.axis_index("case")
     rows, depth = ids.shape
     cols = ROWS // 2
@@ -174,18 +180,17 @@
         tile = jnp.where(here, piece if i == 0 else pltpu.roll(piece, i * slab, 1), tile)
         for p in range(2):
             spot = here & (row // cols == p)
-            lower = jnp.where(spot, bounds[0, 2 * i + p], lower)
-            upper = jnp.where(spot, bounds[1, 2 * i + p], upper)
+            lower = jnp.where(spot, bounds[0:1, 2 * i + p : 2 * i + p + 1], lower)
+            upper = jnp.where(spot, bounds[1:2, 2 * i + p : 2 * i + p + 1], upper)
     weight = jnp.where((lower <= level) & (level < upper), 1.0, 0.0).astype(F32)
     for part in range(2):
         value = jnp.zeros((ROWS, TILE), F32)
         for material in range(lame.shape[1]):
-            value = jnp.where(tile == material, lame[part, material], value)
+            value = jnp.where(tile == material, lame[part : part + 1, material : material + 1], value)
         moduli[part] = value * weight
 
 
-def pack_kernel(slab, field, out):
-    groups = out.shape[0]
+def pack_kernel(slab, order, field, out):
     depth = field.shape[1]
     quarters = TILE // slab
     channels = field.shape[0] // (quarters * ROWS)
@@ -203,16 +208,20 @@
             mixed = jnp.where((lane % slab == 2 * m) & (lane >= slab), below, mixed)
             mixed = jnp.where((lane % slab == 2 * m + 1) & (lane < depth - slab), above, mixed)
         ends.append(mixed)
-    for g in range(groups):
+    cols = ROWS // 2
+    for at, g in enumerate(order):
         cut = slice(g * slab, (g + 1) * slab)
-        for m, pieces in enumerate(parts + [ends]):
-            out[g, m * ROWS : (m + 1) * ROWS, :] = jnp.concatenate([piece[:, cut] for piece in pieces], axis=1).astype(BF16)
+        short = slice(g * slab, g * slab + slab // 2)
+        for m, pieces in enumerate(parts):
+            out[at, m * ROWS : (m + 1) * ROWS, :] = jnp.concatenate([piece[:, cut] for piece in pieces], axis=1).astype(BF16)
+        outer = [end[p * cols : (p + 1) * cols, short] for p in range(2) for end in ends]
+        out[at, channels * ROWS :, :] = jnp.concatenate(outer, axis=1).astype(BF16)
 
 
 def gather_kernel(slab, got, tiles, ends, face_x, face_y, plain):
     groups, rows, _ = got.shape
     quarters = TILE // slab
-    per = (rows // ROWS - 1) // 3
+    per = rows // ROWS // 3
     cases = per * groups
     cols = ROWS // 2
     brick_x = lax.axis_index("bx")
@@ -244,17 +253,22 @@
                 for p in range(2):
                     face_y[k, p] = jnp.where(brick_y == 0, tiles[k, p, y], face_y[k, p].astype(F32)).astype(BF16)
         face_x[y] = packed.astype(BF16)
+        outer = gather(3 * per * ROWS + y)
         for p in range(2):
-            ends[p, y] = gather(3 * per * ROWS + p * cols + y)
-
-
-def column_steps(shifts, slab, tiles, ends, pairs, linear, moduli, face_x, face_y, best, high, low):
+            spaced = jnp.zeros((groups, TILE), F32)
+            for i in range(quarters):
+                moved = pltpu.roll(outer, (i * slab - (p * quarters + i) * (slab // 2)) % TILE, 1)
+                spaced = jnp.where(lane[:groups] // slab == i, moved, spaced)
+            ends[p, y] = spaced
+
+
+def column_steps(slab, tiles, ends, pairs, linear, moduli, face_x, face_y, best, high, low):
     cases = tiles.shape[3]
     groups = ends.shape[2]
     per = cases // groups
     quarters = TILE // slab
     cols = ROWS // 2
-    width = shifts * cases
+    main = cases // 2 * cases
     wide = lax.broadcasted_iota(jnp.int32, (cases, TILE), 1)
     lower_y = lax.axis_index("by") == 1
 
@@ -311,17 +325,17 @@
             root * exact[4],
             root * exact[5],
         ]
-        for s in range(shifts):
+        for s in range(cases // 2 + 1):
             form = None
             for part in parts:
                 term = part * (part if s == 0 else pltpu.roll(part, cases - s, 0))
                 form = term if form is None else form + term
             upper = form.astype(BF16)
             lower = (form - upper.astype(F32)).astype(BF16)
-            at = s * cases
+            at, apart = (s * cases, main) if s < cases // 2 else (3 * main, cases)
             rhs[at : at + cases, :] = upper
-            rhs[width + at : width + at + cases, :] = lower
-            rhs[2 * width + at : 2 * width + at + cases, :] = upper
+            rhs[at + apart : at + apart + cases, :] = lower
+            rhs[at + 2 * apart : at + 2 * apart + cases, :] = upper
 
     def reduce(step, rhs, sums):
         _, columns, _, slot = step
@@ -335,9 +349,9 @@
     return build, reduce
 
 
-def run_steps(build, reduce, steps, width, rhs, sums):
+def run_steps(build, reduce, steps, used, rhs, sums):
     for buffer in rhs:
-        buffer[3 * width :, :] = jnp.zeros((buffer.shape[0] - 3 * width, 2 * TILE), BF16)
+        buffer[used:, :] = jnp.zeros((buffer.shape[0] - used, 2 * TILE), BF16)
     build(steps[0], rhs[0], sums[0])
     for n, step in enumerate(steps):
         if n + 1 < len(steps):
@@ -345,23 +359,23 @@
         reduce(step, rhs[n % 2], sums[n % 2])
 
 
-def inner_kernel(shifts, slab, tiles, ends, pairs, linear, moduli, best, high, low, rhs_even, rhs_odd, sums_even, sums_odd):
+def inner_kernel(slab, tiles, ends, pairs, linear, moduli, best, high, low, rhs_even, rhs_odd, sums_even, sums_odd):
     p = lax.axis_index("bx")
     cols = ROWS // 2
-    build, reduce = column_steps(shifts, slab, tiles, ends, pairs, linear, moduli, None, None, best, high, low)
+    build, reduce = column_steps(slab, tiles, ends, pairs, linear, moduli, None, None, best, high, low)
     steps = [(p, (y, y + 1), False, 0) for y in range(1, cols - 1, 2)]
-    run_steps(build, reduce, steps, shifts * tiles.shape[3], (rhs_even, rhs_odd), (sums_even, sums_odd))
+    run_steps(build, reduce, steps, 3 * (tiles.shape[3] // 2 + 1) * tiles.shape[3], (rhs_even, rhs_odd), (sums_even, sums_odd))
 
 
 def outer_kernel(
-    shifts, slab, tiles, ends, pairs, linear, moduli, face_x, face_y, inner_best, inner_high, inner_low,
+    slab, tiles, ends, pairs, linear, moduli, face_x, face_y, inner_best, inner_high, inner_low,
     peak, spread, rhs_even, rhs_odd, sums_even, sums_odd, best, high, low,
 ):
     p = lax.axis_index("bx")
     cols = ROWS // 2
-    build, reduce = column_steps(shifts, slab, tiles, ends, pairs, linear, moduli, face_x, face_y, best, high, low)
+    build, reduce = column_steps(slab, tiles, ends, pairs, linear, moduli, face_x, face_y, best, high, low)
     steps = [(p, (0, cols - 1), False, 0)] + [(1 - p, (y, y + 1), True, 1) for y in range(0, cols, 2)]
-    run_steps(build, reduce, steps, shifts * tiles.shape[3], (rhs_even, rhs_odd), (sums_even, sums_odd))
+    run_steps(build, reduce, steps, 3 * (tiles.shape[3] // 2 + 1) * tiles.shape[3], (rhs_even, rhs_odd), (sums_even, sums_odd))
     for into, inner in ((best, inner_best), (high, inner_high), (low, inner_low)):
         into[0, 1 : cols - 1, :] = inner[0, 1 : cols - 1, :]
     for slot, parity in ((0, p), (1, 1 - p)):
@@ -376,41 +390,40 @@
 def tiled_shards(displacements, material_ids, lame, slab_bounds, load_history):
     per, _, rows, cols, depth = displacements.shape
     groups = lax.axis_size("case")
+    order = list(EXCHANGE_ORDER)
     slab = depth // groups
     cases = per * groups
     steps = load_history.shape[0]
     channels = per * 3
     vmem = pl.BlockSpec(memory_space=pltpu.VMEM)
-    smem = pl.BlockSpec(memory_space=pltpu.SMEM)
-    shifts, width, total, first, second, plain = pair_table(cases, groups)
-    params = pltpu.CompilerParams(vmem_limit_bytes=32 * 1024 * 1024)
+    main, picks = pair_table(cases, order)
+    total = 3 * main + TILE
+    params = pltpu.CompilerParams(vmem_limit_bytes=16 * 1024 * 1024)
     like = jax.ShapeDtypeStruct
     with jax.named_scope("prepare"):
         pairs, linear, moduli = pl.pallas_call(
-            functools.partial(prepare_kernel, width, slab),
+            functools.partial(prepare_kernel, main, slab),
             out_shape=(like((steps, total), BF16), like((steps, TILE), BF16), like((2, ROWS, TILE), F32)),
-            in_specs=[vmem] * 5 + [smem] * 2,
+            in_specs=[vmem] * 5,
             out_specs=(vmem,) * 3,
             compiler_params=params,
         )(
             load_history.T,
-            jnp.asarray(first, BF16),
-            jnp.asarray(second, BF16),
-            jnp.asarray(plain, BF16),
+            jnp.asarray(picks, BF16),
             material_ids.reshape(rows * cols, depth),
             lame,
             slab_bounds,
         )
-    lines = (channels + 1) * ROWS
+    lines = channels * ROWS + cols
     with jax.named_scope("pack"):
         packed = pl.pallas_call(
-            functools.partial(pack_kernel, slab),
+            functools.partial(pack_kernel, slab, order),
             out_shape=like((groups, lines, TILE), BF16),
             in_specs=[vmem],
             out_specs=vmem,
             compiler_params=params,
         )(displacements.reshape(channels * rows * cols, depth))
-    got = lax.all_to_all(packed, "case", split_axis=0, concat_axis=0, tiled=True)
+    got = lax.all_to_all(packed, "case", split_axis=0, concat_axis=0, axis_index_groups=[order], tiled=True)
     with jax.named_scope("gather"):
         tiles, ends, face_x, face_y = pl.pallas_call(
             functools.partial(gather_kernel, slab),
@@ -430,7 +443,7 @@
     buffers = [pltpu.VMEM((total, 2 * TILE), BF16)] * 2 + [pltpu.VMEM((3 * cases, 2 * TILE), BF16)] * 2
     with jax.named_scope("inner"):
         inner = pl.pallas_call(
-            functools.partial(inner_kernel, shifts, slab),
+            functools.partial(inner_kernel, slab),
             out_shape=(like((1, cols, TILE), F32),) * 3,
             in_specs=[vmem] * 5,
             out_specs=(vmem,) * 3,
@@ -439,7 +452,7 @@
         )(tiles, ends, pairs, linear, moduli)
     with jax.named_scope("outer"):
         return pl.pallas_call(
-            functools.partial(outer_kernel, shifts, slab),
+            functools.partial(outer_kernel, slab),
             out_shape=(like((rows, cols, slab), F32),) * 2,
             in_specs=[vmem] * 10,
             out_specs=(vmem,) * 2,
@@ -455,7 +468,7 @@
         return False
     per, rows, cols, slab = cases // groups, rows // 2, cols // 2, depth // groups
     return (
-        groups == 8 and per == 2 and comps == 3 and rows == 8 and cols == 8 and slab == 32
+        groups == len(EXCHANGE_ORDER) and per == 2 and comps == 3 and rows == 8 and cols == 8 and slab == 32
         and load_history.shape[0] % 16 == 0
     )
 

time: 26.4 us -> 21.8 us (0.83)
  blocking collectives: 15.5 us -> 11.7 us
  Pallas kernels: 6.77 us -> 5.97 us
    all_to_all x1, blocking collectives: 15.5 us -> 11.7 us  [tiled_shards(): lax.all_to_all(packed, 'case', split_axis=0, concat_axis=0, axis_index_gr...]
    pallas_call x4, Pallas kernels: 6.57 us -> 5.75 us  [the longest x1 3.18 us: tiled_shards(): pl.pallas_call(functools.partial(outer_kernel, slab), out_shape=(like((ro...]
    unnamed x16 -> x12, local copies, waits for them, and re-layouts: 1.58 us -> 1.59 us
  transfers between devices with their start and end apart: 2 -> 2, of which waited for: 0 -> 0; matrix products, arithmetic and copies ran while one was open for 0% -> 0% of each run, Pallas kernels for 11% -> 10%
where the time goes in v4:
time: 21.8 us; the launch traced here: 21.6 us
  blocking collectives  11.7 us (54%)
  Pallas kernels  5.97 us (27%)
  local copies, waits for them, and re-layouts  1.59 us (7%)
  starting transfers between devices  1.59 us (7%)
  between operations  0.71 us (3%)
    all_to_all x1, blocking collectives, tiled_shards(): lax.all_to_all(packed, 'case', split_axis=0, concat_axis=0, axis_index_gr...  11.7 us
    pallas_call x1, Pallas kernels, tiled_shards(): pl.pallas_call(functools.partial(outer_kernel, slab), out_shape=(like((ro...  3.18 us
    pallas_call x1, Pallas kernels, tiled_shards(): pl.pallas_call(functools.partial(inner_kernel, slab), out_shape=(like((1,...  1.6 us
    unnamed x12, local copies, waits for them, and re-layouts  1.59 us
    ppermute x1, starting transfers between devices, tiled_shards(): face_x = lax.ppermute(face_x, 'bx', [(0, 1), (1, 0)])  1.58 us
    pallas_call x1, Pallas kernels, tiled_shards(): pl.pallas_call(functools.partial(prepare_kernel, main, slab), out_shape=(...  0.54 us
  transfers between devices with their start and end apart: 2, of which 0 were waited for; matrix products, arithmetic and copies ran while one was open for 0% of the time, Pallas kernels for 10%

profile of v4, /device:TPU:0, one launch (start us, length us, event | category | flops | bytes accessed | tf_op | source)
XLA Modules:
  0.0 21.6 jit_solution(17113255605474309188)
XLA Ops:
  0.6 0.0 copy-start
  0.6 0.9 %copy-done = bf16[2,3,8,8,256]{4,3,2,1,0:T(8,128)(2,1)S(1)} copy-done((bf16[2,3,8,8,256]{4,3,2,1,0:T(8,128)(2,1)S(1)}, bf16[2,3,8,8,256]{4,3,2,1,0:T(8,128)(2,1)}, u32[]{:S(2)}) %copy-start) | copy-done | bytes 196632
  1.6 0.4 %pack.1 = bf16[8,104,128]{2,1,0:T(8,128)(2,1)S(1)} custom-call(bf16[384,256]{1,0:T(8,128)(2,1)S(1)} %bitcast.3), custom_call_target="tpu_custom_call" | custom-call | tf_op jit(solution)/shard_map/pack/pallas_call | solution.py:419
  2.0 11.7 %all_to_all.5.got = bf16[8,104,128]{2,1,0:T(8,128)(2,1)S(1)} all-to-all(bf16[8,104,128]{2,1,0:T(8,128)(2,1)S(1)} %pack.1), channel_id=1, replica_groups={{20,24,16,4,28,12,8,0},{21,25,17,5,29,13,9,1},{22,26,18,6,30,14,10,2},{..., dimensions={0} | all-to-all | bytes 425984 | tf_op jit(solution)/shard_map/all_to_all | solution.py:426
  13.7 0.0 copy-start.1
  13.7 0.0 copy-start.2
  13.7 0.0 copy-start.3
  13.7 0.0 copy-start.5
  13.7 0.2 %gather.1 = (f32[3,2,8,16,128]{4,3,2,1,0:T(8,128)S(1)}, f32[2,8,8,128]{3,2,1,0:T(8,128)S(1)}, bf16[8,16,128]{2,1,0:T(8,128)(2,1)S(1)}, bf16[3,2,16,128]{3,2,1,0:T(8,128)(2,1)S(1)}) custom-call(bf16[8,104,128]{2,1,0:T(8,128)(2,1)S(1)} %all_to_all.5.got), custom_call_target="tpu_custom_call" | custom-call | tf_op jit(solution)/shard_map/gather/pallas_call | solution.py:428
  13.9 1.6 %collective-permute-start = (bf16[8,16,128]{2,1,0:T(8,128)(2,1)S(1)}, bf16[8,16,128]{2,1,0:T(8,128)(2,1)S(1)}, u32[]{:S(2)}, u32[]{:S(2)}) collective-permute-start(bf16[8,16,128]{2,1,0:T(8,128)(2,1)S(1)} %get-tuple-element.17), channel_id=1, source_target_pairs={{0,2},{2,0},{1,3},{3,1},{4,6},{6,4},{5,7},{7,5},{8,10},{10,8},{9,1... | collective-permute-start | bytes 98312 | tf_op jit(solution)/shard_map/ppermute | solution.py:441
  15.5 0.0 collective-permute-start.1
  15.5 0.0 copy-start.4
  15.5 0.0 copy-done.1
  15.5 0.0 copy-done.2
  15.5 0.0 copy-done.3
  15.5 0.0 copy-done.5
  15.6 0.6 %copy-done.4 = f32[2,8]{1,0:T(2,128)S(1)} copy-done((f32[2,8]{1,0:T(2,128)S(1)}, f32[2,8]{1,0:T(2,128)}, u32[]{:S(2)}) %copy-start.4) | copy-done | bytes 88
  16.2 0.5 %prepare.1 = (bf16[1024,512]{1,0:T(8,128)(2,1)S(1)}, bf16[1024,128]{1,0:T(8,128)(2,1)S(1)}, f32[2,16,128]{2,1,0:T(8,128)S(1)}) custom-call(bf16[16,1024]{1,0:T(8,128)(2,1)S(1)} %bitcast.5, bf16[16,640]{1,0:T(8,128)(2,1)S(1)} %copy-done.3, s32[64,256]{1,0:T(8,128)S(1)} %bitcast.4, f32[2,8]{1,0:T(2,128)S(1)} %copy-done.4, s32[2,8]{1,0:T(2,128)S(1)} %copy-done.5), custom_call_target="tpu_custom_call" | custom-call | tf_op jit(solution)/shard_map/prepare/pallas_call | solution.py:404
  16.8 1.6 %inner.1 = (f32[1,8,128]{2,1,0:T(8,128)S(1)}, f32[1,8,128]{2,1,0:T(8,128)S(1)}, f32[1,8,128]{2,1,0:T(8,128)S(1)}) custom-call(f32[3,2,8,16,128]{4,3,2,1,0:T(8,128)S(1)} %get-tuple-element.12.tiles, f32[2,8,8,128]{3,2,1,0:T(8,128)S(1)} %get-tuple-element.13.ends, bf16[1024,512]{1,0:T(8,128)(2,1)S(1)} %get-tuple-element.14.pairs, ...), custom_call_target="tpu_custom_call" | custom-call | tf_op jit(solution)/shard_map/inner/pallas_call | solution.py:445
  18.4 0.0 collective-permute-done.1.face_y
  18.4 0.0 collective-permute-done.face_x
  18.4 3.2 %outer.1 = (f32[8,8,32]{2,1,0:T(8,128)}, f32[8,8,32]{2,1,0:T(8,128)}) custom-call(f32[3,2,8,16,128]{4,3,2,1,0:T(8,128)S(1)} %get-tuple-element.12.tiles, f32[2,8,8,128]{3,2,1,0:T(8,128)S(1)} %get-tuple-element.13.ends, bf16[1024,512]{1,0:T(8,128)(2,1)S(1)} %get-tuple-element.14.pairs, bf16[1024,128]{1,0:T(8,128)(2,1)S(1)} %get-tuple-element.15.linear, ...), custom_call_target="tpu_custom_call" | custom-call | tf_op jit(solution)/shard_map/outer/pallas_call | solution.py:454
Async XLA Ops:
  0.6 0.9 %copy-start = (bf16[2,3,8,8,256]{4,3,2,1,0:T(8,128)(2,1)S(1)}, bf16[2,3,8,8,256]{4,3,2,1,0:T(8,128)(2,1)}, u32[]{:S(2)}) copy-start(bf16[2,3,8,8,256]{4,3,2,1,0:T(8,128)(2,1)} %param.6) | copy-start | bytes 589828
  13.7 1.8 %copy-start.1 = (s32[8,8,256]{2,1,0:T(8,128)S(1)}, s32[8,8,256]{2,1,0:T(8,128)}, u32[]{:S(2)}) copy-start(s32[8,8,256]{2,1,0:T(8,128)} %param.7) | copy-start | bytes 196612
  13.7 1.8 %copy-start.2 = (bf16[1024,16]{0,1:T(8,128)(2,1)S(1)}, bf16[1024,16]{0,1:T(8,128)(2,1)}, u32[]{:S(2)}) copy-start(bf16[1024,16]{0,1:T(8,128)(2,1)} %param.10) | copy-start | bytes 98308
  13.7 1.8 %copy-start.3 = (bf16[16,640]{1,0:T(8,128)(2,1)S(1)}, bf16[16,640]{1,0:T(8,128)(2,1)}, u32[]{:S(2)}) copy-start(bf16[16,640]{1,0:T(8,128)(2,1)} %constant.2.clone.picks) | copy-start | bytes 61444
  13.7 1.8 %copy-start.5 = (s32[2,8]{1,0:T(2,128)S(1)}, s32[2,8]{1,0:T(2,128)}, u32[]{:S(2)}) copy-start(s32[2,8]{1,0:T(2,128)} %bounds.1) | copy-start | bytes 196
  13.9 4.4 %collective-permute-start = (bf16[8,16,128]{2,1,0:T(8,128)(2,1)S(1)}, bf16[8,16,128]{2,1,0:T(8,128)(2,1)S(1)}, u32[]{:S(2)}, u32[]{:S(2)}) collective-permute-start(bf16[8,16,128]{2,1,0:T(8,128)(2,1)S(1)} %get-tuple-element.17), channel_id=1, source_target_pairs={{0,2},{2,0},{1,3},{3,1},{4,6},{6,4},{5,7},{7,5},{8,10},{10,8},{9,1... | collective-permute-start | bytes 98312 | tf_op jit(solution)/shard_map/ppermute | solution.py:441
  15.5 2.8 %collective-permute-start.1 = (bf16[3,2,16,128]{3,2,1,0:T(8,128)(2,1)S(1)}, bf16[3,2,16,128]{3,2,1,0:T(8,128)(2,1)S(1)}, u32[]{:S(2)}, u32[]{:S(2)}) collective-permute-start(bf16[3,2,16,128]{3,2,1,0:T(8,128)(2,1)S(1)} %get-tuple-element.18), channel_id=1, source_target_pairs={{0,1},{1,0},{2,3},{3,2},{4,5},{5,4},{6,7},{7,6},{8,9},{9,8},{10,11... | collective-permute-start | bytes 73736 | tf_op jit(solution)/shard_map/ppermute | solution.py:442
  15.5 0.7 %copy-start.4 = (f32[2,8]{1,0:T(2,128)S(1)}, f32[2,8]{1,0:T(2,128)}, u32[]{:S(2)}) copy-start(f32[2,8]{1,0:T(2,128)} %lame.1) | copy-start | bytes 196

commit v5 on v4

--- a/solution.py
+++ b/solution.py
@@ -190,14 +190,17 @@
         moduli[part] = value * weight
 
 
-def pack_kernel(slab, order, field, out):
+def pack_field(slab, order, arrivals, field, out):
     depth = field.shape[1]
     quarters = TILE // slab
-    channels = field.shape[0] // (quarters * ROWS)
-    parts = [
-        [field[(m * quarters + i) * ROWS : (m * quarters + i + 1) * ROWS, :].astype(F32) for i in range(quarters)]
-        for m in range(channels)
-    ]
+    height = quarters * ROWS
+    channels = field.shape[0] // height
+    parts = []
+    for m in range(channels):
+        parts.append([field[m * height + i * ROWS : m * height + (i + 1) * ROWS, :].astype(F32) for i in range(quarters)])
+        for at, g in enumerate(order):
+            pieces = [piece[:, g * slab : (g + 1) * slab] for piece in parts[m]]
+            out[at, m * ROWS : (m + 1) * ROWS, :] = jnp.concatenate(pieces, axis=1).astype(BF16)
     lane = lax.broadcasted_iota(jnp.int32, (ROWS, depth), 1)
     ends = []
     for i in range(quarters):
@@ -210,12 +213,28 @@
         ends.append(mixed)
     cols = ROWS // 2
     for at, g in enumerate(order):
-        cut = slice(g * slab, (g + 1) * slab)
         short = slice(g * slab, g * slab + slab // 2)
-        for m, pieces in enumerate(parts):
-            out[at, m * ROWS : (m + 1) * ROWS, :] = jnp.concatenate([piece[:, cut] for piece in pieces], axis=1).astype(BF16)
         outer = [end[p * cols : (p + 1) * cols, short] for p in range(2) for end in ends]
         out[at, channels * ROWS :, :] = jnp.concatenate(outer, axis=1).astype(BF16)
+
+
+def front_kernel(slab, order, source, *rest):
+    count = (len(rest) - 4) // 2
+    far, out, near = rest[:count], rest[count], rest[count + 1 : 2 * count + 1]
+    field, arrived, landed = rest[2 * count + 1 :]
+    height = TILE // slab * ROWS
+    arrivals = []
+    for m in range(field.shape[0] // height):
+        rows = pl.ds(m * height, height)
+        arrivals.append(pltpu.make_async_copy(source.at[rows, :], field.at[rows, :], arrived.at[m]))
+    fetches = [pltpu.make_async_copy(a, b, landed.at[n]) for n, (a, b) in enumerate(zip(far, near))]
+    for copy in arrivals + fetches:
+        copy.start()
+    for copy in arrivals:
+        copy.wait()
+    pack_field(slab, order, arrivals, field, out)
+    for copy in fetches:
+        copy.wait()
 
 
 def gather_kernel(slab, got, tiles, ends, face_x, face_y, plain):
@@ -400,29 +419,39 @@
     total = 3 * main + TILE
     params = pltpu.CompilerParams(vmem_limit_bytes=16 * 1024 * 1024)
     like = jax.ShapeDtypeStruct
-    with jax.named_scope("prepare"):
-        pairs, linear, moduli = pl.pallas_call(
-            functools.partial(prepare_kernel, main, slab),
-            out_shape=(like((steps, total), BF16), like((steps, TILE), BF16), like((2, ROWS, TILE), F32)),
-            in_specs=[vmem] * 5,
-            out_specs=(vmem,) * 3,
-            compiler_params=params,
-        )(
+    lines = channels * ROWS + cols
+    far = [
+        pltpu.with_memory_space_constraint(a, pltpu.HBM)
+        for a in (
+            displacements.reshape(channels * rows * cols, depth),
             load_history.T,
             jnp.asarray(picks, BF16),
             material_ids.reshape(rows * cols, depth),
             lame,
             slab_bounds,
         )
-    lines = channels * ROWS + cols
-    with jax.named_scope("pack"):
-        packed = pl.pallas_call(
-            functools.partial(pack_kernel, slab, order),
-            out_shape=like((groups, lines, TILE), BF16),
-            in_specs=[vmem],
-            out_specs=vmem,
+    ]
+    with jax.named_scope("front"):
+        packed, *near = pl.pallas_call(
+            functools.partial(front_kernel, slab, order),
+            out_shape=(pltpu.VMEM((groups, lines, TILE), BF16),) + tuple(pltpu.VMEM(a.shape, a.dtype) for a in far[1:]),
+            in_specs=[pl.BlockSpec(memory_space=pltpu.HBM)] * len(far),
+            out_specs=(vmem,) * len(far),
+            scratch_shapes=[
+                pltpu.VMEM(far[0].shape, BF16),
+                pltpu.SemaphoreType.DMA((channels,)),
+                pltpu.SemaphoreType.DMA((len(far) - 1,)),
+            ],
             compiler_params=params,
-        )(displacements.reshape(channels * rows * cols, depth))
+        )(*far)
+    with jax.named_scope("prepare"):
+        pairs, linear, moduli = pl.pallas_call(
+            functools.partial(prepare_kernel, main, slab),
+            out_shape=(like((steps, total), BF16), like((steps, TILE), BF16), like((2, ROWS, TILE), F32)),
+            in_specs=[vmem] * len(near),
+            out_specs=(vmem,) * 3,
+            compiler_params=params,
+        )(*near)
     got = lax.all_to_all(packed, "case", split_axis=0, concat_axis=0, axis_index_groups=[order], tiled=True)
     with jax.named_scope("gather"):
         tiles, ends, face_x, face_y = pl.pallas_call(

time: 21.8 us -> 21.4 us (0.982)
  local copies, waits for them, and re-layouts: 1.59 us -> 0 us
  Pallas kernels: 5.97 us -> 7 us
    unnamed x12 -> x0, local copies, waits for them, and re-layouts: 1.59 us -> none
    pallas_call x1, Pallas kernels: 0.43 us -> 1.47 us  [tiled_shards(): pl.pallas_call(functools.partial(front_kernel, slab, order), out_shape=(p...]
  transfers between devices with their start and end apart: 2 -> 2, of which waited for: 0 -> 1; matrix products, arithmetic and copies ran while one was open for 0% -> 0% of each run, Pallas kernels for 10% -> 10%
where the time goes in v5:
time: 21.4 us; the launch traced here: 21.2 us
  blocking collectives  11.7 us (55%)
  Pallas kernels  7 us (33%)
  starting transfers between devices  1.59 us (7%)
  between operations  0.67 us (3%)
  waiting for transfers between devices  0.22 us (1%)
    all_to_all x1, blocking collectives, tiled_shards(): lax.all_to_all(packed, 'case', split_axis=0, concat_axis=0, axis_index_gr...  11.7 us
    pallas_call x1, Pallas kernels, tiled_shards(): pl.pallas_call(functools.partial(outer_kernel, slab), out_shape=(like((ro...  3.17 us
    pallas_call x1, Pallas kernels, tiled_shards(): pl.pallas_call(functools.partial(inner_kernel, slab), out_shape=(like((1,...  1.61 us
    ppermute x1, starting transfers between devices, tiled_shards(): face_x = lax.ppermute(face_x, 'bx', [(0, 1), (1, 0)])  1.58 us
    pallas_call x1, Pallas kernels, tiled_shards(): pl.pallas_call(functools.partial(front_kernel, slab, order), out_shape=(p...  1.47 us
    pallas_call x1, Pallas kernels, tiled_shards(): pl.pallas_call(functools.partial(prepare_kernel, main, slab), out_shape=(...  0.54 us
  transfers between devices with their start and end apart: 2, of which 1 were waited for; matrix products, arithmetic and copies ran while one was open for 0% of the time, Pallas kernels for 10%

profile of v5, /device:TPU:0, one launch (start us, length us, event | category | flops | bytes accessed | tf_op | source)
XLA Modules:
  0.0 21.2 jit_solution(3925516003078199862)
XLA Ops:
  0.6 1.5 %front.1 = (bf16[8,104,128]{2,1,0:T(8,128)(2,1)S(1)}, bf16[16,1024]{1,0:T(8,128)(2,1)S(1)}, bf16[16,640]{1,0:T(8,128)(2,1)S(1)}, s32[64,256]{1,0:T(8,128)S(1)}, f32[2,8]{1,0:T(2,128)S(1)}, /*index=5*/s32[2,8]{1,0:T(2,128)S(1)}) custom-call(bf16[384,256]{1,0:T(8,128)(2,1)} %bitcast.3, bf16[16,1024]{1,0:T(8,128)(2,1)} %bitcast.5, ...), custom_call_target="tpu_custom_call" | custom-call | tf_op jit(solution)/shard_map/front/pallas_call | solution.py:435
  2.1 11.7 %all_to_all.5.got = bf16[8,104,128]{2,1,0:T(8,128)(2,1)S(1)} all-to-all(bf16[8,104,128]{2,1,0:T(8,128)(2,1)S(1)} %get-tuple-element.18), channel_id=1, replica_groups={{20,24,16,4,28,12,8,0},{21,25,17,5,29,13,9,1},{22,26,18,6,30,14,10,2},{..., dimensions={0} | all-to-all | bytes 425984 | tf_op jit(solution)/shard_map/all_to_all | solution.py:455
  13.8 0.2 %gather.1 = (f32[3,2,8,16,128]{4,3,2,1,0:T(8,128)S(1)}, f32[2,8,8,128]{3,2,1,0:T(8,128)S(1)}, bf16[8,16,128]{2,1,0:T(8,128)(2,1)S(1)}, bf16[3,2,16,128]{3,2,1,0:T(8,128)(2,1)S(1)}) custom-call(bf16[8,104,128]{2,1,0:T(8,128)(2,1)S(1)} %all_to_all.5.got), custom_call_target="tpu_custom_call" | custom-call | tf_op jit(solution)/shard_map/gather/pallas_call | solution.py:457
  14.0 1.6 %collective-permute-start = (bf16[8,16,128]{2,1,0:T(8,128)(2,1)S(1)}, bf16[8,16,128]{2,1,0:T(8,128)(2,1)S(1)}, u32[]{:S(2)}, u32[]{:S(2)}) collective-permute-start(bf16[8,16,128]{2,1,0:T(8,128)(2,1)S(1)} %get-tuple-element.29), channel_id=1, source_target_pairs={{0,2},{2,0},{1,3},{3,1},{4,6},{6,4},{5,7},{7,5},{8,10},{10,8},{9,1... | collective-permute-start | bytes 98312 | tf_op jit(solution)/shard_map/ppermute | solution.py:470
  15.6 0.0 collective-permute-start.1
  15.6 0.5 %prepare.1 = (bf16[1024,512]{1,0:T(8,128)(2,1)S(1)}, bf16[1024,128]{1,0:T(8,128)(2,1)S(1)}, f32[2,16,128]{2,1,0:T(8,128)S(1)}) custom-call(bf16[16,1024]{1,0:T(8,128)(2,1)S(1)} %get-tuple-element.21.loads, bf16[16,640]{1,0:T(8,128)(2,1)S(1)} %get-tuple-element.22.picks, s32[64,256]{1,0:T(8,128)S(1)} %get-tuple-element.23.ids, ...), custom_call_target="tpu_custom_call" | custom-call | tf_op jit(solution)/shard_map/prepare/pallas_call | solution.py:448
  16.2 1.6 %inner.1 = (f32[1,8,128]{2,1,0:T(8,128)S(1)}, f32[1,8,128]{2,1,0:T(8,128)S(1)}, f32[1,8,128]{2,1,0:T(8,128)S(1)}) custom-call(f32[3,2,8,16,128]{4,3,2,1,0:T(8,128)S(1)} %get-tuple-element.19.tiles, f32[2,8,8,128]{3,2,1,0:T(8,128)S(1)} %get-tuple-element.20.ends, bf16[1024,512]{1,0:T(8,128)(2,1)S(1)} %get-tuple-element.26.pairs, ...), custom_call_target="tpu_custom_call" | custom-call | tf_op jit(solution)/shard_map/inner/pallas_call | solution.py:474
  17.8 0.0 collective-permute-done.1.face_y
  17.8 0.2 %collective-permute-done.face_x = bf16[8,16,128]{2,1,0:T(8,128)(2,1)S(1)} collective-permute-done((bf16[8,16,128]{2,1,0:T(8,128)(2,1)S(1)}, bf16[8,16,128]{2,1,0:T(8,128)(2,1)S(1)}, u32[]{:S(2)}, u32[]{:S(2)}) %collective-permute-start) | collective-permute-done | bytes 32800 | tf_op jit(solution)/shard_map/ppermute | solution.py:470
  18.0 3.2 %outer.1 = (f32[8,8,32]{2,1,0:T(8,128)}, f32[8,8,32]{2,1,0:T(8,128)}) custom-call(f32[3,2,8,16,128]{4,3,2,1,0:T(8,128)S(1)} %get-tuple-element.19.tiles, f32[2,8,8,128]{3,2,1,0:T(8,128)S(1)} %get-tuple-element.20.ends, bf16[1024,512]{1,0:T(8,128)(2,1)S(1)} %get-tuple-element.26.pairs, bf16[1024,128]{1,0:T(8,128)(2,1)S(1)} %get-tuple-element.27.linear, ...), custom_call_target="tpu_custom_call" | custom-call | tf_op jit(solution)/shard_map/outer/pallas_call | solution.py:483
Async XLA Ops:
  14.0 4.0 %collective-permute-start = (bf16[8,16,128]{2,1,0:T(8,128)(2,1)S(1)}, bf16[8,16,128]{2,1,0:T(8,128)(2,1)S(1)}, u32[]{:S(2)}, u32[]{:S(2)}) collective-permute-start(bf16[8,16,128]{2,1,0:T(8,128)(2,1)S(1)} %get-tuple-element.29), channel_id=1, source_target_pairs={{0,2},{2,0},{1,3},{3,1},{4,6},{6,4},{5,7},{7,5},{8,10},{10,8},{9,1... | collective-permute-start | bytes 98312 | tf_op jit(solution)/shard_map/ppermute | solution.py:470
  15.6 2.2 %collective-permute-start.1 = (bf16[3,2,16,128]{3,2,1,0:T(8,128)(2,1)S(1)}, bf16[3,2,16,128]{3,2,1,0:T(8,128)(2,1)S(1)}, u32[]{:S(2)}, u32[]{:S(2)}) collective-permute-start(bf16[3,2,16,128]{3,2,1,0:T(8,128)(2,1)S(1)} %get-tuple-element.30), channel_id=1, source_target_pairs={{0,1},{1,0},{2,3},{3,2},{4,5},{5,4},{6,7},{7,6},{8,9},{9,8},{10,11... | collective-permute-start | bytes 73736 | tf_op jit(solution)/shard_map/ppermute | solution.py:471

commit v6 on v5

--- a/solution.py
+++ b/solution.py
@@ -134,36 +134,29 @@
     place = np.array([order[j % groups] * per + j // groups for j in range(cases)])
     half = cases // 2
     main = half * cases
-    first = np.zeros((cases, main + TILE), np.float32)
-    second = np.zeros((cases, main + TILE), np.float32)
-    plain = np.zeros((cases, TILE), np.float32)
-    for j in range(cases):
-        for s in range(half):
-            first[place[j], s * cases + j] = 1.0
-            second[place[(j + s) % cases], s * cases + j] = 2.0 if s else 1.0
-        for copy in range(3):
-            first[place[j], main + copy * cases + j] = 1.0
-            second[place[(j + half) % cases], main + copy * cases + j] = 1.0
-            plain[place[j], copy * cases + j] = 1.0
-    return main, np.concatenate([first, second, plain], axis=1)
+    picks = np.zeros((cases, 2 * main), np.float32)
+    for s in range(half):
+        for j in range(cases):
+            picks[place[j], s * cases + j] = 1.0
+            picks[place[(j + s + 1) % cases], main + s * cases + j] = 2.0 if s + 1 < half else 1.0
+    return main, picks
 
 
 def prepare_kernel(main, slab, loads, picks, ids, lame, bounds, pairs, linear, moduli):
     over = (((0,), (0,)), ((), ()))
-    table = loads[...]
-    factor = lax.dot_general(table, picks[...], over, preferred_element_type=F32)
-    wide = main + TILE
-    prod = factor[:, :wide] * factor[:, wide : 2 * wide]
-    most = prod[:, :main]
-    high = most.astype(BF16)
+    cases = loads.shape[0]
+    factor = lax.dot_general(loads[...], picks[...], over, preferred_element_type=F32)
+    single, other = factor[:, :main], factor[:, main:]
+    linear[...] = single[:, :TILE].astype(BF16)
+    mixed = single * other
+    high = mixed.astype(BF16)
     pairs[:, :main] = high
     pairs[:, main : 2 * main] = high
-    pairs[:, 2 * main : 3 * main] = (most - high.astype(F32)).astype(BF16)
-    last = prod[:, main:]
-    high = last.astype(BF16).astype(F32)
-    col = lax.broadcasted_iota(jnp.int32, last.shape, 1)
-    pairs[:, 3 * main :] = jnp.where(col < 2 * table.shape[0], high, last - high).astype(BF16)
-    linear[...] = factor[:, 2 * wide :].astype(BF16)
+    pairs[:, 2 * main : 3 * main] = (mixed - high.astype(F32)).astype(BF16)
+    square = single[:, :TILE] * single[:, :TILE]
+    high = square.astype(BF16).astype(F32)
+    col = lax.broadcasted_iota(jnp.int32, square.shape, 1)
+    pairs[:, 3 * main :] = jnp.where(col < 2 * cases, high, square - high).astype(BF16)
     group = lax.axis_index("case")
     rows, depth = ids.shape
     cols = ROWS // 2
@@ -351,7 +344,7 @@
                 form = term if form is None else form + term
             upper = form.astype(BF16)
             lower = (form - upper.astype(F32)).astype(BF16)
-            at, apart = (s * cases, main) if s < cases // 2 else (3 * main, cases)
+            at, apart = ((s - 1) * cases, main) if s else (3 * main, cases)
             rhs[at : at + cases, :] = upper
             rhs[at + apart : at + apart + cases, :] = lower
             rhs[at + 2 * apart : at + 2 * apart + cases, :] = upper
@@ -467,8 +460,8 @@
             scratch_shapes=[pltpu.VMEM((groups * lines, TILE), F32)],
             compiler_params=params,
         )(got)
+    face_y = lax.ppermute(face_y, "by", [(0, 1), (1, 0)])
     face_x = lax.ppermute(face_x, "bx", [(0, 1), (1, 0)])
-    face_y = lax.ppermute(face_y, "by", [(0, 1), (1, 0)])
     buffers = [pltpu.VMEM((total, 2 * TILE), BF16)] * 2 + [pltpu.VMEM((3 * cases, 2 * TILE), BF16)] * 2
     with jax.named_scope("inner"):
         inner = pl.pallas_call(

time: 21.4 us -> 21.4 us (level)
  no operation moved by 1% of the time
where the time goes in v6:
time: 21.4 us; the launch traced here: 21.2 us
  blocking collectives  11.7 us (55%)
  Pallas kernels  6.92 us (32%)
  starting transfers between devices  1.59 us (7%)
  between operations  0.67 us (3%)
  waiting for transfers between devices  0.29 us (1%)
    all_to_all x1, blocking collectives, tiled_shards(): lax.all_to_all(packed, 'case', split_axis=0, concat_axis=0, axis_index_gr...  11.7 us
    pallas_call x1, Pallas kernels, tiled_shards(): pl.pallas_call(functools.partial(outer_kernel, slab), out_shape=(like((ro...  3.16 us
    pallas_call x1, Pallas kernels, tiled_shards(): pl.pallas_call(functools.partial(inner_kernel, slab), out_shape=(like((1,...  1.62 us
    ppermute x1, starting transfers between devices, tiled_shards(): face_x = lax.ppermute(face_x, 'bx', [(0, 1), (1, 0)])  1.58 us
    pallas_call x1, Pallas kernels, tiled_shards(): pl.pallas_call(functools.partial(front_kernel, slab, order), out_shape=(p...  1.47 us
    pallas_call x1, Pallas kernels, tiled_shards(): pl.pallas_call(functools.partial(prepare_kernel, main, slab), out_shape=(...  0.46 us
  transfers between devices with their start and end apart: 2, of which 1 were waited for; matrix products, arithmetic and copies ran while one was open for 0% of the time, Pallas kernels for 10%

profile of v6, /device:TPU:0, one launch (start us, length us, event | category | flops | bytes accessed | tf_op | source)
XLA Modules:
  0.0 21.2 jit_solution(11286879875674919678)
XLA Ops:
  0.6 1.5 %front.1 = (bf16[8,104,128]{2,1,0:T(8,128)(2,1)S(1)}, bf16[16,1024]{1,0:T(8,128)(2,1)S(1)}, bf16[16,256]{1,0:T(8,128)(2,1)S(1)}, s32[64,256]{1,0:T(8,128)S(1)}, f32[2,8]{1,0:T(2,128)S(1)}, /*index=5*/s32[2,8]{1,0:T(2,128)S(1)}) custom-call(bf16[384,256]{1,0:T(8,128)(2,1)} %bitcast.3, bf16[16,1024]{1,0:T(8,128)(2,1)} %bitcast.5, ...), custom_call_target="tpu_custom_call" | custom-call | tf_op jit(solution)/shard_map/front/pallas_call | solution.py:428
  2.1 11.7 %all_to_all.5.got = bf16[8,104,128]{2,1,0:T(8,128)(2,1)S(1)} all-to-all(bf16[8,104,128]{2,1,0:T(8,128)(2,1)S(1)} %get-tuple-element.18), channel_id=1, replica_groups={{20,24,16,4,28,12,8,0},{21,25,17,5,29,13,9,1},{22,26,18,6,30,14,10,2},{..., dimensions={0} | all-to-all | bytes 425984 | tf_op jit(solution)/shard_map/all_to_all | solution.py:448
  13.8 0.2 %gather.1 = (f32[3,2,8,16,128]{4,3,2,1,0:T(8,128)S(1)}, f32[2,8,8,128]{3,2,1,0:T(8,128)S(1)}, bf16[8,16,128]{2,1,0:T(8,128)(2,1)S(1)}, bf16[3,2,16,128]{3,2,1,0:T(8,128)(2,1)S(1)}) custom-call(bf16[8,104,128]{2,1,0:T(8,128)(2,1)S(1)} %all_to_all.5.got), custom_call_target="tpu_custom_call" | custom-call | tf_op jit(solution)/shard_map/gather/pallas_call | solution.py:450
  14.0 1.6 %collective-permute-start = (bf16[8,16,128]{2,1,0:T(8,128)(2,1)S(1)}, bf16[8,16,128]{2,1,0:T(8,128)(2,1)S(1)}, u32[]{:S(2)}, u32[]{:S(2)}) collective-permute-start(bf16[8,16,128]{2,1,0:T(8,128)(2,1)S(1)} %get-tuple-element.29), channel_id=1, source_target_pairs={{0,2},{2,0},{1,3},{3,1},{4,6},{6,4},{5,7},{7,5},{8,10},{10,8},{9,1... | collective-permute-start | bytes 98312 | tf_op jit(solution)/shard_map/ppermute | solution.py:464
  15.6 0.0 collective-permute-start.1
  15.6 0.5 %prepare.1 = (bf16[1024,512]{1,0:T(8,128)(2,1)S(1)}, bf16[1024,128]{1,0:T(8,128)(2,1)S(1)}, f32[2,16,128]{2,1,0:T(8,128)S(1)}) custom-call(bf16[16,1024]{1,0:T(8,128)(2,1)S(1)} %get-tuple-element.21.loads, bf16[16,256]{1,0:T(8,128)(2,1)S(1)} %get-tuple-element.22.picks, s32[64,256]{1,0:T(8,128)S(1)} %get-tuple-element.23.ids, ...), custom_call_target="tpu_custom_call" | custom-call | tf_op jit(solution)/shard_map/prepare/pallas_call | solution.py:441
  16.1 1.6 %inner.1 = (f32[1,8,128]{2,1,0:T(8,128)S(1)}, f32[1,8,128]{2,1,0:T(8,128)S(1)}, f32[1,8,128]{2,1,0:T(8,128)S(1)}) custom-call(f32[3,2,8,16,128]{4,3,2,1,0:T(8,128)S(1)} %get-tuple-element.19.tiles, f32[2,8,8,128]{3,2,1,0:T(8,128)S(1)} %get-tuple-element.20.ends, bf16[1024,512]{1,0:T(8,128)(2,1)S(1)} %get-tuple-element.26.pairs, ...), custom_call_target="tpu_custom_call" | custom-call | tf_op jit(solution)/shard_map/inner/pallas_call | solution.py:467
  17.7 0.0 collective-permute-done.1.face_y
  17.7 0.3 %collective-permute-done.face_x = bf16[8,16,128]{2,1,0:T(8,128)(2,1)S(1)} collective-permute-done((bf16[8,16,128]{2,1,0:T(8,128)(2,1)S(1)}, bf16[8,16,128]{2,1,0:T(8,128)(2,1)S(1)}, u32[]{:S(2)}, u32[]{:S(2)}) %collective-permute-start) | collective-permute-done | bytes 32800 | tf_op jit(solution)/shard_map/ppermute | solution.py:464
  18.0 3.2 %outer.1 = (f32[8,8,32]{2,1,0:T(8,128)}, f32[8,8,32]{2,1,0:T(8,128)}) custom-call(f32[3,2,8,16,128]{4,3,2,1,0:T(8,128)S(1)} %get-tuple-element.19.tiles, f32[2,8,8,128]{3,2,1,0:T(8,128)S(1)} %get-tuple-element.20.ends, bf16[1024,512]{1,0:T(8,128)(2,1)S(1)} %get-tuple-element.26.pairs, bf16[1024,128]{1,0:T(8,128)(2,1)S(1)} %get-tuple-element.27.linear, ...), custom_call_target="tpu_custom_call" | custom-call | tf_op jit(solution)/shard_map/outer/pallas_call | solution.py:476
Async XLA Ops:
  14.0 4.0 %collective-permute-start = (bf16[8,16,128]{2,1,0:T(8,128)(2,1)S(1)}, bf16[8,16,128]{2,1,0:T(8,128)(2,1)S(1)}, u32[]{:S(2)}, u32[]{:S(2)}) collective-permute-start(bf16[8,16,128]{2,1,0:T(8,128)(2,1)S(1)} %get-tuple-element.29), channel_id=1, source_target_pairs={{0,2},{2,0},{1,3},{3,1},{4,6},{6,4},{5,7},{7,5},{8,10},{10,8},{9,1... | collective-permute-start | bytes 98312 | tf_op jit(solution)/shard_map/ppermute | solution.py:464
  15.6 2.1 %collective-permute-start.1 = (bf16[3,2,16,128]{3,2,1,0:T(8,128)(2,1)S(1)}, bf16[3,2,16,128]{3,2,1,0:T(8,128)(2,1)S(1)}, u32[]{:S(2)}, u32[]{:S(2)}) collective-permute-start(bf16[3,2,16,128]{3,2,1,0:T(8,128)(2,1)S(1)} %get-tuple-element.30), channel_id=1, source_target_pairs={{0,1},{1,0},{2,3},{3,2},{4,5},{5,4},{6,7},{7,6},{8,9},{9,8},{10,11... | collective-permute-start | bytes 73736 | tf_op jit(solution)/shard_map/ppermute | solution.py:463

commit v7 on v6

--- a/solution.py
+++ b/solution.py
@@ -248,15 +248,18 @@
         return jnp.concatenate([gather((c * 3 + k) * ROWS + p * cols + y) for c in range(per)], axis=0)
 
     lane = lax.broadcasted_iota(jnp.int32, (cases, TILE), 1)
+    packed = [jnp.zeros((cases, TILE), F32) for _ in range(3)]
     for y in range(cols):
-        packed = jnp.zeros((cases, TILE), F32)
+        at = y % quarters
         for k in range(3):
             even, odd = column(k, 0, y), column(k, 1, y)
             tiles[k, 0, y] = even
             tiles[k, 1, y] = odd
-            even = pltpu.roll(even, k * slab, 1) if k else even
-            odd = pltpu.roll(odd, (k + 1 - quarters) * slab % TILE, 1)
-            packed = jnp.where(lane // slab == k, jnp.where(brick_x == 0, odd, even), packed)
+            even = pltpu.roll(even, at * slab, 1) if at else even
+            odd = pltpu.roll(odd, (at + 1 - quarters) * slab % TILE, 1) if at + 1 < quarters else odd
+            packed[k] = jnp.where(lane // slab == at, jnp.where(brick_x == 0, odd, even), packed[k])
+            if at == quarters - 1:
+                face_x[k, y // quarters] = packed[k].astype(BF16)
             if y == 0:
                 firsts = (tiles[k, 0, 0], tiles[k, 1, 0])
                 for p in range(2):
@@ -264,7 +267,6 @@
             if y == cols - 1:
                 for p in range(2):
                     face_y[k, p] = jnp.where(brick_y == 0, tiles[k, p, y], face_y[k, p].astype(F32)).astype(BF16)
-        face_x[y] = packed.astype(BF16)
         outer = gather(3 * per * ROWS + y)
         for p in range(2):
             spaced = jnp.zeros((groups, TILE), F32)
@@ -297,7 +299,7 @@
             other = tiles[k, 1 - p, y]
             shifted = pltpu.roll(other, jnp.where(p == 0, slab, TILE - slab), 1)
             if beside:
-                edge = pltpu.roll(face_x[y].astype(F32), lax.rem((last - k) * slab + TILE, TILE), 1)
+                edge = pltpu.roll(face_x[k, y // quarters].astype(F32), lax.rem((last - y % quarters) * slab + TILE, TILE), 1)
             else:
                 edge = jnp.zeros((cases, TILE), F32)
             grad_x = sign * (other - jnp.where(at_edge, edge, shifted))
@@ -452,7 +454,7 @@
             out_shape=(
                 like((3, 2, cols, cases, TILE), F32),
                 like((2, cols, groups, TILE), F32),
-                like((cols, cases, TILE), BF16),
+                like((3, cols * slab // TILE, cases, TILE), BF16),
                 like((3, 2, cases, TILE), BF16),
             ),
             in_specs=[vmem],

time: 21.4 us -> 21.3 us (level)
  no operation moved by 1% of the time
where the time goes in v7:
time: 21.3 us; the launch traced here: 21.1 us
  blocking collectives  11.7 us (55%)
  Pallas kernels  6.91 us (32%)
  starting transfers between devices  1.59 us (7%)
  between operations  0.66 us (3%)
  waiting for transfers between devices  0.22 us (1%)
    all_to_all x1, blocking collectives, tiled_shards(): lax.all_to_all(packed, 'case', split_axis=0, concat_axis=0, axis_index_gr...  11.7 us
    pallas_call x1, Pallas kernels, tiled_shards(): pl.pallas_call(functools.partial(outer_kernel, slab), out_shape=(like((ro...  3.16 us
    pallas_call x1, Pallas kernels, tiled_shards(): pl.pallas_call(functools.partial(inner_kernel, slab), out_shape=(like((1,...  1.61 us
    ppermute x1, starting transfers between devices, tiled_shards(): face_x = lax.ppermute(face_x, 'bx', [(0, 1), (1, 0)])  1.58 us
    pallas_call x1, Pallas kernels, tiled_shards(): pl.pallas_call(functools.partial(front_kernel, slab, order), out_shape=(p...  1.47 us
    pallas_call x1, Pallas kernels, tiled_shards(): pl.pallas_call(functools.partial(prepare_kernel, main, slab), out_shape=(...  0.46 us
  transfers between devices with their start and end apart: 2, of which 1 were waited for; matrix products, arithmetic and copies ran while one was open for 0% of the time, Pallas kernels for 10%

profile of v7, /device:TPU:0, one launch (start us, length us, event | category | flops | bytes accessed | tf_op | source)
XLA Modules:
  0.0 21.1 jit_solution(11097992671259352867)
XLA Ops:
  0.6 1.5 %front.1 = (bf16[8,104,128]{2,1,0:T(8,128)(2,1)S(1)}, bf16[16,1024]{1,0:T(8,128)(2,1)S(1)}, bf16[16,256]{1,0:T(8,128)(2,1)S(1)}, s32[64,256]{1,0:T(8,128)S(1)}, f32[2,8]{1,0:T(2,128)S(1)}, /*index=5*/s32[2,8]{1,0:T(2,128)S(1)}) custom-call(bf16[384,256]{1,0:T(8,128)(2,1)} %bitcast.3, bf16[16,1024]{1,0:T(8,128)(2,1)} %bitcast.5, ...), custom_call_target="tpu_custom_call" | custom-call | tf_op jit(solution)/shard_map/front/pallas_call | solution.py:430
  2.1 11.7 %all_to_all.5.got = bf16[8,104,128]{2,1,0:T(8,128)(2,1)S(1)} all-to-all(bf16[8,104,128]{2,1,0:T(8,128)(2,1)S(1)} %get-tuple-element.18), channel_id=1, replica_groups={{20,24,16,4,28,12,8,0},{21,25,17,5,29,13,9,1},{22,26,18,6,30,14,10,2},{..., dimensions={0} | all-to-all | bytes 425984 | tf_op jit(solution)/shard_map/all_to_all | solution.py:450
  13.8 0.2 gather.1
  14.0 1.6 %collective-permute-start = (bf16[3,2,16,128]{3,2,1,0:T(8,128)(2,1)S(1)}, bf16[3,2,16,128]{3,2,1,0:T(8,128)(2,1)S(1)}, u32[]{:S(2)}, u32[]{:S(2)}) collective-permute-start(bf16[3,2,16,128]{3,2,1,0:T(8,128)(2,1)S(1)} %get-tuple-element.29), channel_id=1, source_target_pairs={{0,2},{2,0},{1,3},{3,1},{4,6},{6,4},{5,7},{7,5},{8,10},{10,8},{9,1... | collective-permute-start | bytes 73736 | tf_op jit(solution)/shard_map/ppermute | solution.py:466
  15.6 0.0 collective-permute-start.1
  15.6 0.5 %prepare.1 = (bf16[1024,512]{1,0:T(8,128)(2,1)S(1)}, bf16[1024,128]{1,0:T(8,128)(2,1)S(1)}, f32[2,16,128]{2,1,0:T(8,128)S(1)}) custom-call(bf16[16,1024]{1,0:T(8,128)(2,1)S(1)} %get-tuple-element.21.loads, bf16[16,256]{1,0:T(8,128)(2,1)S(1)} %get-tuple-element.22.picks, s32[64,256]{1,0:T(8,128)S(1)} %get-tuple-element.23.ids, ...), custom_call_target="tpu_custom_call" | custom-call | tf_op jit(solution)/shard_map/prepare/pallas_call | solution.py:443
  16.1 1.6 %inner.1 = (f32[1,8,128]{2,1,0:T(8,128)S(1)}, f32[1,8,128]{2,1,0:T(8,128)S(1)}, f32[1,8,128]{2,1,0:T(8,128)S(1)}) custom-call(f32[3,2,8,16,128]{4,3,2,1,0:T(8,128)S(1)} %get-tuple-element.19.tiles, f32[2,8,8,128]{3,2,1,0:T(8,128)S(1)} %get-tuple-element.20.ends, bf16[1024,512]{1,0:T(8,128)(2,1)S(1)} %get-tuple-element.26.pairs, ...), custom_call_target="tpu_custom_call" | custom-call | tf_op jit(solution)/shard_map/inner/pallas_call | solution.py:469
  17.7 0.2 %collective-permute-done.face_x = bf16[3,2,16,128]{3,2,1,0:T(8,128)(2,1)S(1)} collective-permute-done((bf16[3,2,16,128]{3,2,1,0:T(8,128)(2,1)S(1)}, bf16[3,2,16,128]{3,2,1,0:T(8,128)(2,1)S(1)}, u32[]{:S(2)}, u32[]{:S(2)}) %collective-permute-start) | collective-permute-done | bytes 24608 | tf_op jit(solution)/shard_map/ppermute | solution.py:466
  17.9 0.0 collective-permute-done.1.face_y
  17.9 3.2 %outer.1 = (f32[8,8,32]{2,1,0:T(8,128)}, f32[8,8,32]{2,1,0:T(8,128)}) custom-call(f32[3,2,8,16,128]{4,3,2,1,0:T(8,128)S(1)} %get-tuple-element.19.tiles, f32[2,8,8,128]{3,2,1,0:T(8,128)S(1)} %get-tuple-element.20.ends, bf16[1024,512]{1,0:T(8,128)(2,1)S(1)} %get-tuple-element.26.pairs, bf16[1024,128]{1,0:T(8,128)(2,1)S(1)} %get-tuple-element.27.linear, ...), custom_call_target="tpu_custom_call" | custom-call | tf_op jit(solution)/shard_map/outer/pallas_call | solution.py:478
Async XLA Ops:
  14.0 3.9 %collective-permute-start = (bf16[3,2,16,128]{3,2,1,0:T(8,128)(2,1)S(1)}, bf16[3,2,16,128]{3,2,1,0:T(8,128)(2,1)S(1)}, u32[]{:S(2)}, u32[]{:S(2)}) collective-permute-start(bf16[3,2,16,128]{3,2,1,0:T(8,128)(2,1)S(1)} %get-tuple-element.29), channel_id=1, source_target_pairs={{0,2},{2,0},{1,3},{3,1},{4,6},{6,4},{5,7},{7,5},{8,10},{10,8},{9,1... | collective-permute-start | bytes 73736 | tf_op jit(solution)/shard_map/ppermute | solution.py:466
  15.6 2.3 %collective-permute-start.1 = (bf16[3,2,16,128]{3,2,1,0:T(8,128)(2,1)S(1)}, bf16[3,2,16,128]{3,2,1,0:T(8,128)(2,1)S(1)}, u32[]{:S(2)}, u32[]{:S(2)}) collective-permute-start(bf16[3,2,16,128]{3,2,1,0:T(8,128)(2,1)S(1)} %get-tuple-element.30), channel_id=1, source_target_pairs={{0,1},{1,0},{2,3},{3,2},{4,5},{5,4},{6,7},{7,6},{8,9},{9,8},{10,11... | collective-permute-start | bytes 73736 | tf_op jit(solution)/shard_map/ppermute | solution.py:465

commit v8 on v7

--- a/solution.py
+++ b/solution.py
@@ -142,7 +142,7 @@
     return main, picks
 
 
-def prepare_kernel(main, slab, loads, picks, ids, lame, bounds, pairs, linear, moduli):
+def prepare(main, slab, loads, picks, ids, lame, bounds, pairs, linear, moduli):
     over = (((0,), (0,)), ((), ()))
     cases = loads.shape[0]
     factor = lax.dot_general(loads[...], picks[...], over, preferred_element_type=F32)
@@ -230,13 +230,12 @@
         copy.wait()
 
 
-def gather_kernel(slab, got, tiles, ends, face_x, face_y, plain):
+def gather_kernel(slab, got, tiles, ends, face_y, plain):
     groups, rows, _ = got.shape
     quarters = TILE // slab
     per = rows // ROWS // 3
     cases = per * groups
     cols = ROWS // 2
-    brick_x = lax.axis_index("bx")
     brick_y = lax.axis_index("by")
     for g in range(groups):
         plain[g * rows : (g + 1) * rows, :] = got[g].astype(F32)
@@ -248,18 +247,10 @@
         return jnp.concatenate([gather((c * 3 + k) * ROWS + p * cols + y) for c in range(per)], axis=0)
 
     lane = lax.broadcasted_iota(jnp.int32, (cases, TILE), 1)
-    packed = [jnp.zeros((cases, TILE), F32) for _ in range(3)]
     for y in range(cols):
-        at = y % quarters
         for k in range(3):
-            even, odd = column(k, 0, y), column(k, 1, y)
-            tiles[k, 0, y] = even
-            tiles[k, 1, y] = odd
-            even = pltpu.roll(even, at * slab, 1) if at else even
-            odd = pltpu.roll(odd, (at + 1 - quarters) * slab % TILE, 1) if at + 1 < quarters else odd
-            packed[k] = jnp.where(lane // slab == at, jnp.where(brick_x == 0, odd, even), packed[k])
-            if at == quarters - 1:
-                face_x[k, y // quarters] = packed[k].astype(BF16)
+            tiles[k, 0, y] = column(k, 0, y)
+            tiles[k, 1, y] = column(k, 1, y)
             if y == 0:
                 firsts = (tiles[k, 0, 0], tiles[k, 1, 0])
                 for p in range(2):
@@ -274,6 +265,21 @@
                 moved = pltpu.roll(outer, (i * slab - (p * quarters + i) * (slab // 2)) % TILE, 1)
                 spaced = jnp.where(lane[:groups] // slab == i, moved, spaced)
             ends[p, y] = spaced
+
+
+def face_kernel(slab, tiles, face_x):
+    cases, cols = tiles.shape[3], tiles.shape[2]
+    quarters = TILE // slab
+    lane = lax.broadcasted_iota(jnp.int32, (cases, TILE), 1)
+    p = 1 - lax.axis_index("bx")
+    shift = jnp.where(p == 0, 0, slab)
+    for k in range(3):
+        for h in range(cols // quarters):
+            packed = jnp.zeros((cases, TILE), F32)
+            for at in range(quarters):
+                moved = pltpu.roll(tiles[k, p, h * quarters + at], lax.rem(shift + at * slab, TILE), 1)
+                packed = jnp.where(lane // slab == at, moved, packed)
+            face_x[k, h] = packed.astype(BF16)
 
 
 def column_steps(slab, tiles, ends, pairs, linear, moduli, face_x, face_y, best, high, low):
@@ -373,11 +379,15 @@
         reduce(step, rhs[n % 2], sums[n % 2])
 
 
-def inner_kernel(slab, tiles, ends, pairs, linear, moduli, best, high, low, rhs_even, rhs_odd, sums_even, sums_odd):
+def inner_kernel(
+    main, slab, tiles, ends, loads, picks, ids, lame, bounds, face_y,
+    pairs, linear, moduli, best, high, low, rhs_even, rhs_odd, sums_even, sums_odd,
+):
+    prepare(main, slab, loads, picks, ids, lame, bounds, pairs, linear, moduli)
     p = lax.axis_index("bx")
     cols = ROWS // 2
-    build, reduce = column_steps(slab, tiles, ends, pairs, linear, moduli, None, None, best, high, low)
-    steps = [(p, (y, y + 1), False, 0) for y in range(1, cols - 1, 2)]
+    build, reduce = column_steps(slab, tiles, ends, pairs, linear, moduli, None, face_y, best, high, low)
+    steps = [(p, (y, y + 1), False, 0) for y in range(0, cols, 2)]
     run_steps(build, reduce, steps, 3 * (tiles.shape[3] // 2 + 1) * tiles.shape[3], (rhs_even, rhs_odd), (sums_even, sums_odd))
 
 
@@ -388,13 +398,11 @@
     p = lax.axis_index("bx")
     cols = ROWS // 2
     build, reduce = column_steps(slab, tiles, ends, pairs, linear, moduli, face_x, face_y, best, high, low)
-    steps = [(p, (0, cols - 1), False, 0)] + [(1 - p, (y, y + 1), True, 1) for y in range(0, cols, 2)]
+    steps = [(1 - p, (y, y + 1), True, 0) for y in range(0, cols, 2)]
     run_steps(build, reduce, steps, 3 * (tiles.shape[3] // 2 + 1) * tiles.shape[3], (rhs_even, rhs_odd), (sums_even, sums_odd))
-    for into, inner in ((best, inner_best), (high, inner_high), (low, inner_low)):
-        into[0, 1 : cols - 1, :] = inner[0, 1 : cols - 1, :]
-    for slot, parity in ((0, p), (1, 1 - p)):
-        vm = jnp.sqrt(jnp.maximum(best[slot], 0.0))
-        hyd = high[slot] * (1.0 / 3.0) - low[slot] * (1.0 / 3.0)
+    for parity, top, most, least in ((p, inner_best, inner_high, inner_low), (1 - p, best, high, low)):
+        vm = jnp.sqrt(jnp.maximum(top[0], 0.0))
+        hyd = most[0] * (1.0 / 3.0) - least[0] * (1.0 / 3.0)
         for i in range(TILE // slab):
             cut = slice(i * slab, (i + 1) * slab)
             peak[2 * i + parity] = vm[:, cut]
@@ -439,48 +447,48 @@
             ],
             compiler_params=params,
         )(*far)
-    with jax.named_scope("prepare"):
-        pairs, linear, moduli = pl.pallas_call(
-            functools.partial(prepare_kernel, main, slab),
-            out_shape=(like((steps, total), BF16), like((steps, TILE), BF16), like((2, ROWS, TILE), F32)),
-            in_specs=[vmem] * len(near),
-            out_specs=(vmem,) * 3,
-            compiler_params=params,
-        )(*near)
     got = lax.all_to_all(packed, "case", split_axis=0, concat_axis=0, axis_index_groups=[order], tiled=True)
     with jax.named_scope("gather"):
-        tiles, ends, face_x, face_y = pl.pallas_call(
+        tiles, ends, face_y = pl.pallas_call(
             functools.partial(gather_kernel, slab),
             out_shape=(
                 like((3, 2, cols, cases, TILE), F32),
                 like((2, cols, groups, TILE), F32),
-                like((3, cols * slab // TILE, cases, TILE), BF16),
                 like((3, 2, cases, TILE), BF16),
             ),
             in_specs=[vmem],
-            out_specs=(vmem,) * 4,
+            out_specs=(vmem,) * 3,
             scratch_shapes=[pltpu.VMEM((groups * lines, TILE), F32)],
             compiler_params=params,
         )(got)
     face_y = lax.ppermute(face_y, "by", [(0, 1), (1, 0)])
+    with jax.named_scope("face"):
+        face_x = pl.pallas_call(
+            functools.partial(face_kernel, slab),
+            out_shape=like((3, cols * slab // TILE, cases, TILE), BF16),
+            in_specs=[vmem],
+            out_specs=vmem,
+            compiler_params=params,
+        )(tiles)
     face_x = lax.ppermute(face_x, "bx", [(0, 1), (1, 0)])
     buffers = [pltpu.VMEM((total, 2 * TILE), BF16)] * 2 + [pltpu.VMEM((3 * cases, 2 * TILE), BF16)] * 2
     with jax.named_scope("inner"):
-        inner = pl.pallas_call(
-            functools.partial(inner_kernel, slab),
-            out_shape=(like((1, cols, TILE), F32),) * 3,
-            in_specs=[vmem] * 5,
-            out_specs=(vmem,) * 3,
+        pairs, linear, moduli, *inner = pl.pallas_call(
+            functools.partial(inner_kernel, main, slab),
+            out_shape=(like((steps, total), BF16), like((steps, TILE), BF16), like((2, ROWS, TILE), F32))
+            + (like((1, cols, TILE), F32),) * 3,
+            in_specs=[vmem] * (3 + len(near)),
+            out_specs=(vmem,) * 6,
             scratch_shapes=buffers,
             compiler_params=params,
-        )(tiles, ends, pairs, linear, moduli)
+        )(tiles, ends, *near, face_y)
     with jax.named_scope("outer"):
         return pl.pallas_call(
             functools.partial(outer_kernel, slab),
             out_shape=(like((rows, cols, slab), F32),) * 2,
             in_specs=[vmem] * 10,
             out_specs=(vmem,) * 2,
-            scratch_shapes=buffers + [pltpu.VMEM((2, cols, TILE), F32)] * 3,
+            scratch_shapes=buffers + [pltpu.VMEM((1, cols, TILE), F32)] * 3,
             compiler_params=params,
         )(tiles, ends, pairs, linear, moduli, face_x, face_y, *inner)
 

time: 21.3 us -> 21.2 us (level)
    pallas_call x2, Pallas kernels: 2.07 us -> 2.49 us  [the longest x1 2.39 us: tiled_shards(): pl.pallas_call(functools.partial(inner_kernel, main, slab), out_shape=(li...]
    pallas_call x1, Pallas kernels: 3.16 us -> 2.75 us  [tiled_shards(): pl.pallas_call(functools.partial(outer_kernel, slab), out_shape=(like((ro...]
    ppermute x1, waiting for transfers between devices: 0.22 us -> 0.01 us  [tiled_shards(): face_x = lax.ppermute(face_x, 'bx', [(0, 1), (1, 0)])]
  transfers between devices with their start and end apart: 2 -> 2, of which waited for: 1 -> 0; matrix products, arithmetic and copies ran while one was open for 0% -> 0% of each run, Pallas kernels for 10% -> 12%
where the time goes in v8:
time: 21.2 us; the launch traced here: 21 us
  blocking collectives  11.7 us (55%)
  Pallas kernels  6.91 us (33%)
  starting transfers between devices  1.66 us (8%)
  between operations  0.68 us (3%)
    all_to_all x1, blocking collectives, tiled_shards(): lax.all_to_all(packed, 'case', split_axis=0, concat_axis=0, axis_index_gr...  11.7 us
    pallas_call x1, Pallas kernels, tiled_shards(): pl.pallas_call(functools.partial(outer_kernel, slab), out_shape=(like((ro...  2.75 us
    pallas_call x1, Pallas kernels, tiled_shards(): pl.pallas_call(functools.partial(inner_kernel, main, slab), out_shape=(li...  2.39 us
    ppermute x1, starting transfers between devices, tiled_shards(): face_x = lax.ppermute(face_x, 'bx', [(0, 1), (1, 0)])  1.58 us
    pallas_call x1, Pallas kernels, tiled_shards(): pl.pallas_call(functools.partial(front_kernel, slab, order), out_shape=(p...  1.47 us
  transfers between devices with their start and end apart: 2, of which 0 were waited for; matrix products, arithmetic and copies ran while one was open for 0% of the time, Pallas kernels for 12%

profile of v8, /device:TPU:0, one launch (start us, length us, event | category | flops | bytes accessed | tf_op | source)
XLA Modules:
  0.0 21.0 jit_solution(1890042515239201759)
XLA Ops:
  0.6 1.5 %front.1 = (bf16[8,104,128]{2,1,0:T(8,128)(2,1)S(1)}, bf16[16,1024]{1,0:T(8,128)(2,1)S(1)}, bf16[16,256]{1,0:T(8,128)(2,1)S(1)}, s32[64,256]{1,0:T(8,128)S(1)}, f32[2,8]{1,0:T(2,128)S(1)}, /*index=5*/s32[2,8]{1,0:T(2,128)S(1)}) custom-call(bf16[384,256]{1,0:T(8,128)(2,1)} %bitcast.3, bf16[16,1024]{1,0:T(8,128)(2,1)} %bitcast.5, ...), custom_call_target="tpu_custom_call" | custom-call | tf_op jit(solution)/shard_map/front/pallas_call | solution.py:438
  2.1 11.7 %all_to_all.5.got = bf16[8,104,128]{2,1,0:T(8,128)(2,1)S(1)} all-to-all(bf16[8,104,128]{2,1,0:T(8,128)(2,1)S(1)} %get-tuple-element.17), channel_id=1, replica_groups={{20,24,16,4,28,12,8,0},{21,25,17,5,29,13,9,1},{22,26,18,6,30,14,10,2},{..., dimensions={0} | all-to-all | bytes 425984 | tf_op jit(solution)/shard_map/all_to_all | solution.py:450
  13.8 0.2 gather.1
  14.0 0.1 collective-permute-start
  14.1 0.1 face.1
  14.2 1.6 %collective-permute-start.1 = (bf16[3,2,16,128]{3,2,1,0:T(8,128)(2,1)S(1)}, bf16[3,2,16,128]{3,2,1,0:T(8,128)(2,1)S(1)}, u32[]{:S(2)}, u32[]{:S(2)}) collective-permute-start(bf16[3,2,16,128]{3,2,1,0:T(8,128)(2,1)S(1)} %face.1), channel_id=1, source_target_pairs={{0,2},{2,0},{1,3},{3,1},{4,6},{6,4},{5,7},{7,5},{8,10},{10,8},{9,1... | collective-permute-start | bytes 73736 | tf_op jit(solution)/shard_map/ppermute | solution.py:473
  15.8 0.0 collective-permute-done.face_y
  15.8 2.4 %inner.1 = (bf16[1024,512]{1,0:T(8,128)(2,1)S(1)}, bf16[1024,128]{1,0:T(8,128)(2,1)S(1)}, f32[2,16,128]{2,1,0:T(8,128)S(1)}, f32[1,8,128]{2,1,0:T(8,128)S(1)}, f...) custom-call(f32[3,2,8,16,128]{4,3,2,1,0:T(8,128)S(1)} %get-tuple-element.18.tiles, ...), custom_call_target="tpu_custom_call" | custom-call | tf_op jit(solution)/shard_map/inner/pallas_call | solution.py:476
  18.2 0.0 collective-permute-done.1.face_x
  18.2 2.7 %outer.1 = (f32[8,8,32]{2,1,0:T(8,128)}, f32[8,8,32]{2,1,0:T(8,128)}) custom-call(f32[3,2,8,16,128]{4,3,2,1,0:T(8,128)S(1)} %get-tuple-element.18.tiles, f32[2,8,8,128]{3,2,1,0:T(8,128)S(1)} %get-tuple-element.19.ends, bf16[1024,512]{1,0:T(8,128)(2,1)S(1)} %get-tuple-element.26.pairs, bf16[1024,128]{1,0:T(8,128)(2,1)S(1)} %get-tuple-element.27.linear, ...), custom_call_target="tpu_custom_call" | custom-call | tf_op jit(solution)/shard_map/outer/pallas_call | solution.py:486
Async XLA Ops:
  14.0 1.8 %collective-permute-start = (bf16[3,2,16,128]{3,2,1,0:T(8,128)(2,1)S(1)}, bf16[3,2,16,128]{3,2,1,0:T(8,128)(2,1)S(1)}, u32[]{:S(2)}, u32[]{:S(2)}) collective-permute-start(bf16[3,2,16,128]{3,2,1,0:T(8,128)(2,1)S(1)} %get-tuple-element.25), channel_id=1, source_target_pairs={{0,1},{1,0},{2,3},{3,2},{4,5},{5,4},{6,7},{7,6},{8,9},{9,8},{10,11... | collective-permute-start | bytes 73736 | tf_op jit(solution)/shard_map/ppermute | solution.py:464
  14.2 4.0 %collective-permute-start.1 = (bf16[3,2,16,128]{3,2,1,0:T(8,128)(2,1)S(1)}, bf16[3,2,16,128]{3,2,1,0:T(8,128)(2,1)S(1)}, u32[]{:S(2)}, u32[]{:S(2)}) collective-permute-start(bf16[3,2,16,128]{3,2,1,0:T(8,128)(2,1)S(1)} %face.1), channel_id=1, source_target_pairs={{0,2},{2,0},{1,3},{3,1},{4,6},{6,4},{5,7},{7,5},{8,10},{10,8},{9,1... | collective-permute-start | bytes 73736 | tf_op jit(solution)/shard_map/ppermute | solution.py:473

commit v9 on v8

--- a/solution.py
+++ b/solution.py
@@ -208,7 +208,8 @@
     for at, g in enumerate(order):
         short = slice(g * slab, g * slab + slab // 2)
         outer = [end[p * cols : (p + 1) * cols, short] for p in range(2) for end in ends]
-        out[at, channels * ROWS :, :] = jnp.concatenate(outer, axis=1).astype(BF16)
+        packed = jnp.concatenate(outer, axis=1)
+        out[at, channels * ROWS :, :] = jnp.concatenate([packed, packed], axis=0).astype(BF16)
 
 
 def front_kernel(slab, order, source, *rest):
@@ -422,7 +423,7 @@
     total = 3 * main + TILE
     params = pltpu.CompilerParams(vmem_limit_bytes=16 * 1024 * 1024)
     like = jax.ShapeDtypeStruct
-    lines = channels * ROWS + cols
+    lines = (channels + 1) * ROWS
     far = [
         pltpu.with_memory_space_constraint(a, pltpu.HBM)
         for a in (

time: 21.2 us -> 22 us (1.038)
  blocking collectives: 11.7 us -> 12.5 us
    all_to_all x1, blocking collectives: 11.7 us -> 12.5 us  [tiled_shards(): lax.all_to_all(packed, 'case', split_axis=0, concat_axis=0, axis_index_gr...]
  transfers between devices with their start and end apart: 2 -> 2, of which waited for: 0 -> 0; matrix products, arithmetic and copies ran while one was open for 0% -> 0% of each run, Pallas kernels for 12% -> 11%
where the time goes in v9:
time: 22 us; the launch traced here: 21.8 us
  blocking collectives  12.5 us (57%)
  Pallas kernels  6.97 us (32%)
  starting transfers between devices  1.66 us (8%)
  between operations  0.68 us (3%)
    all_to_all x1, blocking collectives, tiled_shards(): lax.all_to_all(packed, 'case', split_axis=0, concat_axis=0, axis_index_gr...  12.5 us
    pallas_call x1, Pallas kernels, tiled_shards(): pl.pallas_call(functools.partial(outer_kernel, slab), out_shape=(like((ro...  2.75 us
    pallas_call x1, Pallas kernels, tiled_shards(): pl.pallas_call(functools.partial(inner_kernel, main, slab), out_shape=(li...  2.39 us
    ppermute x1, starting transfers between devices, tiled_shards(): face_x = lax.ppermute(face_x, 'bx', [(0, 1), (1, 0)])  1.58 us
    pallas_call x1, Pallas kernels, tiled_shards(): pl.pallas_call(functools.partial(front_kernel, slab, order), out_shape=(p...  1.47 us
  transfers between devices with their start and end apart: 2, of which 0 were waited for; matrix products, arithmetic and copies ran while one was open for 0% of the time, Pallas kernels for 11%

profile of v9, /device:TPU:0, one launch (start us, length us, event | category | flops | bytes accessed | tf_op | source)
XLA Modules:
  0.0 21.8 jit_solution(14129471326319292816)
XLA Ops:
  0.6 1.5 %front.1 = (bf16[8,112,128]{2,1,0:T(8,128)(2,1)S(1)}, bf16[16,1024]{1,0:T(8,128)(2,1)S(1)}, bf16[16,256]{1,0:T(8,128)(2,1)S(1)}, s32[64,256]{1,0:T(8,128)S(1)}, f32[2,8]{1,0:T(2,128)S(1)}, /*index=5*/s32[2,8]{1,0:T(2,128)S(1)}) custom-call(bf16[384,256]{1,0:T(8,128)(2,1)} %bitcast.3, bf16[16,1024]{1,0:T(8,128)(2,1)} %bitcast.5, ...), custom_call_target="tpu_custom_call" | custom-call | tf_op jit(solution)/shard_map/front/pallas_call | solution.py:439
  2.1 12.5 %all_to_all.5.got = bf16[8,112,128]{2,1,0:T(8,128)(2,1)S(1)} all-to-all(bf16[8,112,128]{2,1,0:T(8,128)(2,1)S(1)} %get-tuple-element.17), channel_id=1, replica_groups={{20,24,16,4,28,12,8,0},{21,25,17,5,29,13,9,1},{22,26,18,6,30,14,10,2},{..., dimensions={0} | all-to-all | bytes 458752 | tf_op jit(solution)/shard_map/all_to_all | solution.py:451
  14.6 0.3 %gather.1 = (f32[3,2,8,16,128]{4,3,2,1,0:T(8,128)S(1)}, f32[2,8,8,128]{3,2,1,0:T(8,128)S(1)}, bf16[3,2,16,128]{3,2,1,0:T(8,128)(2,1)S(1)}) custom-call(bf16[8,112,128]{2,1,0:T(8,128)(2,1)S(1)} %all_to_all.5.got), custom_call_target="tpu_custom_call" | custom-call | tf_op jit(solution)/shard_map/gather/pallas_call | solution.py:453
  14.9 0.1 collective-permute-start
  15.0 0.1 face.1
  15.1 1.6 %collective-permute-start.1 = (bf16[3,2,16,128]{3,2,1,0:T(8,128)(2,1)S(1)}, bf16[3,2,16,128]{3,2,1,0:T(8,128)(2,1)S(1)}, u32[]{:S(2)}, u32[]{:S(2)}) collective-permute-start(bf16[3,2,16,128]{3,2,1,0:T(8,128)(2,1)S(1)} %face.1), channel_id=1, source_target_pairs={{0,2},{2,0},{1,3},{3,1},{4,6},{6,4},{5,7},{7,5},{8,10},{10,8},{9,1... | collective-permute-start | bytes 73736 | tf_op jit(solution)/shard_map/ppermute | solution.py:474
  16.7 0.0 collective-permute-done.face_y
  16.7 2.4 %inner.1 = (bf16[1024,512]{1,0:T(8,128)(2,1)S(1)}, bf16[1024,128]{1,0:T(8,128)(2,1)S(1)}, f32[2,16,128]{2,1,0:T(8,128)S(1)}, f32[1,8,128]{2,1,0:T(8,128)S(1)}, f...) custom-call(f32[3,2,8,16,128]{4,3,2,1,0:T(8,128)S(1)} %get-tuple-element.18.tiles, ...), custom_call_target="tpu_custom_call" | custom-call | tf_op jit(solution)/shard_map/inner/pallas_call | solution.py:477
  19.1 0.0 collective-permute-done.1.face_x
  19.1 2.7 %outer.1 = (f32[8,8,32]{2,1,0:T(8,128)}, f32[8,8,32]{2,1,0:T(8,128)}) custom-call(f32[3,2,8,16,128]{4,3,2,1,0:T(8,128)S(1)} %get-tuple-element.18.tiles, f32[2,8,8,128]{3,2,1,0:T(8,128)S(1)} %get-tuple-element.19.ends, bf16[1024,512]{1,0:T(8,128)(2,1)S(1)} %get-tuple-element.26.pairs, bf16[1024,128]{1,0:T(8,128)(2,1)S(1)} %get-tuple-element.27.linear, ...), custom_call_target="tpu_custom_call" | custom-call | tf_op jit(solution)/shard_map/outer/pallas_call | solution.py:487
Async XLA Ops:
  14.9 1.8 %collective-permute-start = (bf16[3,2,16,128]{3,2,1,0:T(8,128)(2,1)S(1)}, bf16[3,2,16,128]{3,2,1,0:T(8,128)(2,1)S(1)}, u32[]{:S(2)}, u32[]{:S(2)}) collective-permute-start(bf16[3,2,16,128]{3,2,1,0:T(8,128)(2,1)S(1)} %get-tuple-element.25), channel_id=1, source_target_pairs={{0,1},{1,0},{2,3},{3,2},{4,5},{5,4},{6,7},{7,6},{8,9},{9,8},{10,11... | collective-permute-start | bytes 73736 | tf_op jit(solution)/shard_map/ppermute | solution.py:465
  15.1 4.0 %collective-permute-start.1 = (bf16[3,2,16,128]{3,2,1,0:T(8,128)(2,1)S(1)}, bf16[3,2,16,128]{3,2,1,0:T(8,128)(2,1)S(1)}, u32[]{:S(2)}, u32[]{:S(2)}) collective-permute-start(bf16[3,2,16,128]{3,2,1,0:T(8,128)(2,1)S(1)} %face.1), channel_id=1, source_target_pairs={{0,2},{2,0},{1,3},{3,1},{4,6},{6,4},{5,7},{7,5},{8,10},{10,8},{9,1... | collective-permute-start | bytes 73736 | tf_op jit(solution)/shard_map/ppermute | solution.py:474

commit v10 on v8

--- a/solution.py
+++ b/solution.py
@@ -190,20 +190,22 @@
     channels = field.shape[0] // height
     parts = []
     for m in range(channels):
-        parts.append([field[m * height + i * ROWS : m * height + (i + 1) * ROWS, :].astype(F32) for i in range(quarters)])
+        parts.append([field[m * height + i * ROWS : m * height + (i + 1) * ROWS, :] for i in range(quarters)])
         for at, g in enumerate(order):
             pieces = [piece[:, g * slab : (g + 1) * slab] for piece in parts[m]]
-            out[at, m * ROWS : (m + 1) * ROWS, :] = jnp.concatenate(pieces, axis=1).astype(BF16)
+            out[at, m * ROWS : (m + 1) * ROWS, :] = jnp.concatenate(pieces, axis=1)
     lane = lax.broadcasted_iota(jnp.int32, (ROWS, depth), 1)
+    place = lane % slab
+    inner = (place % 2 == 0) & (lane >= slab) | (place % 2 == 1) & (lane < depth - slab)
     ends = []
     for i in range(quarters):
         mixed = jnp.zeros((ROWS, depth), F32)
         for m in range(channels):
-            below = pltpu.roll(parts[m][i], 2 * m + 1, 1)
-            above = pltpu.roll(parts[m][i], (2 * m + 1 - slab) % depth, 1)
-            mixed = jnp.where((lane % slab == 2 * m) & (lane >= slab), below, mixed)
-            mixed = jnp.where((lane % slab == 2 * m + 1) & (lane < depth - slab), above, mixed)
-        ends.append(mixed)
+            plane = parts[m][i].astype(F32)
+            below = pltpu.roll(plane, 2 * m + 1, 1)
+            above = pltpu.roll(plane, (2 * m + 1 - slab) % depth, 1)
+            mixed = jnp.where(place == 2 * m, below, jnp.where(place == 2 * m + 1, above, mixed))
+        ends.append(jnp.where(inner, mixed, 0.0))
     cols = ROWS // 2
     for at, g in enumerate(order):
         short = slice(g * slab, g * slab + slab // 2)

time: 21.2 us -> 21.2 us (level)
  no operation moved by 1% of the time
where the time goes in v10:
time: 21.2 us; the launch traced here: 21 us
  blocking collectives  11.7 us (55%)
  Pallas kernels  6.91 us (33%)
  starting transfers between devices  1.66 us (8%)
  between operations  0.68 us (3%)
    all_to_all x1, blocking collectives, tiled_shards(): lax.all_to_all(packed, 'case', split_axis=0, concat_axis=0, axis_index_gr...  11.7 us
    pallas_call x1, Pallas kernels, tiled_shards(): pl.pallas_call(functools.partial(outer_kernel, slab), out_shape=(like((ro...  2.75 us
    pallas_call x1, Pallas kernels, tiled_shards(): pl.pallas_call(functools.partial(inner_kernel, main, slab), out_shape=(li...  2.39 us
    ppermute x1, starting transfers between devices, tiled_shards(): face_x = lax.ppermute(face_x, 'bx', [(0, 1), (1, 0)])  1.58 us
    pallas_call x1, Pallas kernels, tiled_shards(): pl.pallas_call(functools.partial(front_kernel, slab, order), out_shape=(p...  1.46 us
  transfers between devices with their start and end apart: 2, of which 0 were waited for; matrix products, arithmetic and copies ran while one was open for 0% of the time, Pallas kernels for 12%

profile of v10, /device:TPU:0, one launch (start us, length us, event | category | flops | bytes accessed | tf_op | source)
XLA Modules:
  0.0 21.0 jit_solution(14651902771538749408)
XLA Ops:
  0.6 1.5 %front.1 = (bf16[8,104,128]{2,1,0:T(8,128)(2,1)S(1)}, bf16[16,1024]{1,0:T(8,128)(2,1)S(1)}, bf16[16,256]{1,0:T(8,128)(2,1)S(1)}, s32[64,256]{1,0:T(8,128)S(1)}, f32[2,8]{1,0:T(2,128)S(1)}, /*index=5*/s32[2,8]{1,0:T(2,128)S(1)}) custom-call(bf16[384,256]{1,0:T(8,128)(2,1)} %bitcast.3, bf16[16,1024]{1,0:T(8,128)(2,1)} %bitcast.5, ...), custom_call_target="tpu_custom_call" | custom-call | tf_op jit(solution)/shard_map/front/pallas_call | solution.py:440
  2.1 11.7 %all_to_all.5.got = bf16[8,104,128]{2,1,0:T(8,128)(2,1)S(1)} all-to-all(bf16[8,104,128]{2,1,0:T(8,128)(2,1)S(1)} %get-tuple-element.17), channel_id=1, replica_groups={{20,24,16,4,28,12,8,0},{21,25,17,5,29,13,9,1},{22,26,18,6,30,14,10,2},{..., dimensions={0} | all-to-all | bytes 425984 | tf_op jit(solution)/shard_map/all_to_all | solution.py:452
  13.8 0.2 gather.1
  14.0 0.1 collective-permute-start
  14.1 0.1 face.1
  14.2 1.6 %collective-permute-start.1 = (bf16[3,2,16,128]{3,2,1,0:T(8,128)(2,1)S(1)}, bf16[3,2,16,128]{3,2,1,0:T(8,128)(2,1)S(1)}, u32[]{:S(2)}, u32[]{:S(2)}) collective-permute-start(bf16[3,2,16,128]{3,2,1,0:T(8,128)(2,1)S(1)} %face.1), channel_id=1, source_target_pairs={{0,2},{2,0},{1,3},{3,1},{4,6},{6,4},{5,7},{7,5},{8,10},{10,8},{9,1... | collective-permute-start | bytes 73736 | tf_op jit(solution)/shard_map/ppermute | solution.py:475
  15.8 0.0 collective-permute-done.face_y
  15.8 2.4 %inner.1 = (bf16[1024,512]{1,0:T(8,128)(2,1)S(1)}, bf16[1024,128]{1,0:T(8,128)(2,1)S(1)}, f32[2,16,128]{2,1,0:T(8,128)S(1)}, f32[1,8,128]{2,1,0:T(8,128)S(1)}, f...) custom-call(f32[3,2,8,16,128]{4,3,2,1,0:T(8,128)S(1)} %get-tuple-element.18.tiles, ...), custom_call_target="tpu_custom_call" | custom-call | tf_op jit(solution)/shard_map/inner/pallas_call | solution.py:478
  18.2 0.0 collective-permute-done.1.face_x
  18.2 2.7 %outer.1 = (f32[8,8,32]{2,1,0:T(8,128)}, f32[8,8,32]{2,1,0:T(8,128)}) custom-call(f32[3,2,8,16,128]{4,3,2,1,0:T(8,128)S(1)} %get-tuple-element.18.tiles, f32[2,8,8,128]{3,2,1,0:T(8,128)S(1)} %get-tuple-element.19.ends, bf16[1024,512]{1,0:T(8,128)(2,1)S(1)} %get-tuple-element.26.pairs, bf16[1024,128]{1,0:T(8,128)(2,1)S(1)} %get-tuple-element.27.linear, ...), custom_call_target="tpu_custom_call" | custom-call | tf_op jit(solution)/shard_map/outer/pallas_call | solution.py:488
Async XLA Ops:
  14.0 1.8 %collective-permute-start = (bf16[3,2,16,128]{3,2,1,0:T(8,128)(2,1)S(1)}, bf16[3,2,16,128]{3,2,1,0:T(8,128)(2,1)S(1)}, u32[]{:S(2)}, u32[]{:S(2)}) collective-permute-start(bf16[3,2,16,128]{3,2,1,0:T(8,128)(2,1)S(1)} %get-tuple-element.25), channel_id=1, source_target_pairs={{0,1},{1,0},{2,3},{3,2},{4,5},{5,4},{6,7},{7,6},{8,9},{9,8},{10,11... | collective-permute-start | bytes 73736 | tf_op jit(solution)/shard_map/ppermute | solution.py:466
  14.2 4.0 %collective-permute-start.1 = (bf16[3,2,16,128]{3,2,1,0:T(8,128)(2,1)S(1)}, bf16[3,2,16,128]{3,2,1,0:T(8,128)(2,1)S(1)}, u32[]{:S(2)}, u32[]{:S(2)}) collective-permute-start(bf16[3,2,16,128]{3,2,1,0:T(8,128)(2,1)S(1)} %face.1), channel_id=1, source_target_pairs={{0,2},{2,0},{1,3},{3,1},{4,6},{6,4},{5,7},{7,5},{8,10},{10,8},{9,1... | collective-permute-start | bytes 73736 | tf_op jit(solution)/shard_map/ppermute | solution.py:475

commit v11 on v10

--- a/solution.py
+++ b/solution.py
@@ -361,9 +361,15 @@
 
     def reduce(step, rhs, sums):
         _, columns, _, slot = step
-        mises2 = jnp.dot(pairs[...], rhs[...], preferred_element_type=F32)
         hydro = jnp.dot(linear[:, : 3 * cases], sums[...], preferred_element_type=F32)
-        tops = (jnp.max(mises2, axis=0, keepdims=True), jnp.max(hydro, axis=0, keepdims=True), jnp.min(hydro, axis=0, keepdims=True))
+        most, least = jnp.max(hydro, axis=0, keepdims=True), jnp.min(hydro, axis=0, keepdims=True)
+        half = pairs.shape[0] // 2
+        top = None
+        for at in (0, half):
+            mises2 = jnp.dot(pairs[at : at + half, :], rhs[...], preferred_element_type=F32)
+            found = jnp.max(mises2, axis=0, keepdims=True)
+            top = found if top is None else jnp.maximum(top, found)
+        tops = (top, most, least)
         for half, y in enumerate(columns):
             for into, row in zip((best, high, low), tops):
                 into[slot, y : y + 1, :] = row[:, half * TILE : (half + 1) * TILE]

time: 21.2 us -> 21.1 us (level)
  no operation moved by 1% of the time
where the time goes in v11:
time: 21.1 us; the launch traced here: 20.9 us
  blocking collectives  11.7 us (55%)
  Pallas kernels  6.86 us (33%)
  starting transfers between devices  1.66 us (8%)
  between operations  0.68 us (3%)
    all_to_all x1, blocking collectives, tiled_shards(): lax.all_to_all(packed, 'case', split_axis=0, concat_axis=0, axis_index_gr...  11.7 us
    pallas_call x1, Pallas kernels, tiled_shards(): pl.pallas_call(functools.partial(outer_kernel, slab), out_shape=(like((ro...  2.74 us
    pallas_call x1, Pallas kernels, tiled_shards(): pl.pallas_call(functools.partial(inner_kernel, main, slab), out_shape=(li...  2.35 us
    ppermute x1, starting transfers between devices, tiled_shards(): face_x = lax.ppermute(face_x, 'bx', [(0, 1), (1, 0)])  1.58 us
    pallas_call x1, Pallas kernels, tiled_shards(): pl.pallas_call(functools.partial(front_kernel, slab, order), out_shape=(p...  1.46 us
  transfers between devices with their start and end apart: 2, of which 0 were waited for; matrix products, arithmetic and copies ran while one was open for 0% of the time, Pallas kernels for 12%

profile of v11, /device:TPU:0, one launch (start us, length us, event | category | flops | bytes accessed | tf_op | source)
XLA Modules:
  0.0 20.9 jit_solution(4951396353699181119)
XLA Ops:
  0.6 1.5 %front.1 = (bf16[8,104,128]{2,1,0:T(8,128)(2,1)S(1)}, bf16[16,1024]{1,0:T(8,128)(2,1)S(1)}, bf16[16,256]{1,0:T(8,128)(2,1)S(1)}, s32[64,256]{1,0:T(8,128)S(1)}, f32[2,8]{1,0:T(2,128)S(1)}, /*index=5*/s32[2,8]{1,0:T(2,128)S(1)}) custom-call(bf16[384,256]{1,0:T(8,128)(2,1)} %bitcast.3, bf16[16,1024]{1,0:T(8,128)(2,1)} %bitcast.5, ...), custom_call_target="tpu_custom_call" | custom-call | tf_op jit(solution)/shard_map/front/pallas_call | solution.py:446
  2.1 11.7 %all_to_all.5.got = bf16[8,104,128]{2,1,0:T(8,128)(2,1)S(1)} all-to-all(bf16[8,104,128]{2,1,0:T(8,128)(2,1)S(1)} %get-tuple-element.17), channel_id=1, replica_groups={{20,24,16,4,28,12,8,0},{21,25,17,5,29,13,9,1},{22,26,18,6,30,14,10,2},{..., dimensions={0} | all-to-all | bytes 425984 | tf_op jit(solution)/shard_map/all_to_all | solution.py:458
  13.8 0.2 gather.1
  14.0 0.1 collective-permute-start
  14.1 0.1 face.1
  14.2 1.6 %collective-permute-start.1 = (bf16[3,2,16,128]{3,2,1,0:T(8,128)(2,1)S(1)}, bf16[3,2,16,128]{3,2,1,0:T(8,128)(2,1)S(1)}, u32[]{:S(2)}, u32[]{:S(2)}) collective-permute-start(bf16[3,2,16,128]{3,2,1,0:T(8,128)(2,1)S(1)} %face.1), channel_id=1, source_target_pairs={{0,2},{2,0},{1,3},{3,1},{4,6},{6,4},{5,7},{7,5},{8,10},{10,8},{9,1... | collective-permute-start | bytes 73736 | tf_op jit(solution)/shard_map/ppermute | solution.py:481
  15.8 0.0 collective-permute-done.face_y
  15.8 2.3 %inner.1 = (bf16[1024,512]{1,0:T(8,128)(2,1)S(1)}, bf16[1024,128]{1,0:T(8,128)(2,1)S(1)}, f32[2,16,128]{2,1,0:T(8,128)S(1)}, f32[1,8,128]{2,1,0:T(8,128)S(1)}, f...) custom-call(f32[3,2,8,16,128]{4,3,2,1,0:T(8,128)S(1)} %get-tuple-element.18.tiles, ...), custom_call_target="tpu_custom_call" | custom-call | tf_op jit(solution)/shard_map/inner/pallas_call | solution.py:484
  18.2 0.0 collective-permute-done.1.face_x
  18.2 2.7 %outer.1 = (f32[8,8,32]{2,1,0:T(8,128)}, f32[8,8,32]{2,1,0:T(8,128)}) custom-call(f32[3,2,8,16,128]{4,3,2,1,0:T(8,128)S(1)} %get-tuple-element.18.tiles, f32[2,8,8,128]{3,2,1,0:T(8,128)S(1)} %get-tuple-element.19.ends, bf16[1024,512]{1,0:T(8,128)(2,1)S(1)} %get-tuple-element.26.pairs, bf16[1024,128]{1,0:T(8,128)(2,1)S(1)} %get-tuple-element.27.linear, ...), custom_call_target="tpu_custom_call" | custom-call | tf_op jit(solution)/shard_map/outer/pallas_call | solution.py:494
Async XLA Ops:
  14.0 1.8 %collective-permute-start = (bf16[3,2,16,128]{3,2,1,0:T(8,128)(2,1)S(1)}, bf16[3,2,16,128]{3,2,1,0:T(8,128)(2,1)S(1)}, u32[]{:S(2)}, u32[]{:S(2)}) collective-permute-start(bf16[3,2,16,128]{3,2,1,0:T(8,128)(2,1)S(1)} %get-tuple-element.25), channel_id=1, source_target_pairs={{0,1},{1,0},{2,3},{3,2},{4,5},{5,4},{6,7},{7,6},{8,9},{9,8},{10,11... | collective-permute-start | bytes 73736 | tf_op jit(solution)/shard_map/ppermute | solution.py:472
  14.2 3.9 %collective-permute-start.1 = (bf16[3,2,16,128]{3,2,1,0:T(8,128)(2,1)S(1)}, bf16[3,2,16,128]{3,2,1,0:T(8,128)(2,1)S(1)}, u32[]{:S(2)}, u32[]{:S(2)}) collective-permute-start(bf16[3,2,16,128]{3,2,1,0:T(8,128)(2,1)S(1)} %face.1), channel_id=1, source_target_pairs={{0,2},{2,0},{1,3},{3,1},{4,6},{6,4},{5,7},{7,5},{8,10},{10,8},{9,1... | collective-permute-start | bytes 73736 | tf_op jit(solution)/shard_map/ppermute | solution.py:481
